TPU v7x, 32 devices: a whole 2x2x4 slice. The times are simulated.
32 devices in a mesh: blk: 2 (over x), wide: 16 (over z, y, core).
Axes of the slice: x: 2, y: 2, z: 4, core: 2. Of those that a mesh axis runs over, the one named last changes fastest.
Arguments:
- tokens: bfloat16 [16, 2048, 768], P('wide', 'blk'), may hold values from -6 to 6
- segments: int32 [16, 2048], P('wide'), may hold values from 0 to 7, as said below
- routes: int32 [16, 2048, 1], P('wide', 'blk'), may hold values from 0 to 15; in each aligned block of 1024 rows (0 to 1023, 1024 to 2047, ..., all dimensions but the last counted through in order) at most 128 rows name the same one
- project_in: bfloat16 [768, 2304], replicated, may hold values from -0.21875 to 0.21875
- project_out: bfloat16 [768, 768], replicated, may hold values from -0.625 to 0.625
- first_gain: float32 [768], replicated, may hold values from 0.5 to 1.5
- first_shift: float32 [768], replicated, may hold values from -1 to 1
- second_gain: float32 [768], replicated, may hold values from 0.5 to 1.5
- second_shift: float32 [768], replicated, may hold values from -1 to 1
- centroids: float32 [16, 768], replicated, may hold values from -0.15625 to 0.15625
- expert_up: bfloat16 [16, 768, 3072], P('wide'), may hold values from -0.21875 to 0.21875
- expert_down: bfloat16 [16, 3072, 768], P('wide'), may hold values from -0.21875 to 0.21875
- cotangent: bfloat16 [16, 2048, 768], P('wide', 'blk'), may hold values from -6 to 6
Outputs:
- result: bfloat16 [16, 2048, 768], P('wide', 'blk')
- input_grad: float32 [16, 2048, 768], P('wide', 'blk')
- project_in_grad: float32 [768, 2304], replicated
- project_out_grad: float32 [768, 768], replicated
- first_gain_grad: float32 [768], replicated
- first_shift_grad: float32 [768], replicated
- second_gain_grad: float32 [768], replicated
- second_shift_grad: float32 [768], replicated
- expert_up_grad: float32 [16, 768, 3072], P('wide', None, 'blk')
- expert_down_grad: float32 [16, 3072, 768], P('wide', 'blk')
Inputs may be any that keep to these rules, and one draw needn't show every extreme that they name: `segments`: within a row the numbers never fall. Half of the rows hold eight documents of 256 tokens each, numbered 0 to 7; in each other row one document begins among the row's first 1024 tokens and ends among its last 1024. `routes`: among the 1024 tokens of one row's block on one device (aligned blocks along a row) each expert is named at most 128 times, a bound that some block reaches.
All inputs are finite; a program needn't handle non-finite values.
Results may differ from a plain program's by a relative error of at most 0.024.
Values may be sent and summed in bfloat16 or wider, within the bound.
No kernel may reach another device: no remote copies, remote signals or barrier semaphores. Data moves between devices by JAX's collectives and lax.ppermute only.
A program may use at most 320 MiB of HBM per device.

v0:
```python
import jax
import jax.numpy as jnp
from jax import lax
from jax.sharding import PartitionSpec as P

HEAD_DIM = 64


def layer_norm(inputs, scaling, offsets):
    center = inputs - jnp.mean(inputs, -1, keepdims=True)
    variance = jnp.mean(center * center, -1, keepdims=True)
    return center * lax.rsqrt(variance + 1e-05) * scaling + offsets


def gelu_exact(inputs):
    return jax.nn.gelu(inputs, approximate=False)


def build_mask(query_places, query_segments, key_places, key_segments):
    causal = key_places[None, :] <= query_places[:, None]
    same = key_segments[:, None, :] == query_segments[:, :, None]
    return causal[None] & same


def block_scores(query_heads, key_heads, allowed, score_scale):
    raw_scores = (
        jnp.einsum("rqhd,rkhd->rhqk", query_heads, key_heads, preferred_element_type=jnp.float32)
        * score_scale
    )
    return jnp.where(allowed[:, None], raw_scores, -1e30)


def block_probs(masked, allowed, peaks, totals):
    return jnp.where(allowed[:, None], jnp.exp(masked - peaks[..., None]) / totals[..., None], 0.0)


def keep_state(state):
    return state


def body(
    tokens,
    segments,
    routes,
    project_in,
    project_out,
    first_gain,
    first_shift,
    second_gain,
    second_shift,
    centroids,
    expert_up,
    expert_down,
    cotangent,
):
    f32 = jnp.float32
    bf16 = jnp.bfloat16
    row_count, block_len, model_width = tokens.shape
    head_count = model_width // HEAD_DIM
    blocks = lax.axis_size("blk")
    length = block_len * blocks
    score_scale = HEAD_DIM ** (-0.5)
    flat_tokens = row_count * block_len
    head_shape = (row_count, block_len, head_count, HEAD_DIM)
    offset = lax.axis_index("blk") * block_len
    local_places = lax.iota(jnp.int32, block_len)
    own_places = offset + local_places
    own_segments = lax.dynamic_slice_in_dim(segments, offset, block_len, 1)
    stream = tokens.reshape(flat_tokens, model_width).astype(f32)
    normed_one, norm_one_back = jax.vjp(layer_norm, stream, first_gain, first_shift)
    normed_one_low = normed_one.astype(bf16)
    joint_proj = jnp.dot(normed_one_low, project_in, preferred_element_type=f32).astype(bf16)
    query_flat = joint_proj[:, :model_width].reshape(row_count, block_len, model_width)
    queries = query_flat.reshape(head_shape)
    keyvals = joint_proj[:, model_width:].reshape(row_count, block_len, 2 * model_width)
    gathered = lax.all_gather(keyvals, "blk", axis=1, tiled=True)

    def key_block(index):
        start = index * block_len
        rows = lax.dynamic_slice_in_dim(gathered, start, block_len, 1)
        key_heads = rows[:, :, :model_width].reshape(head_shape)
        value_heads = rows[:, :, model_width:].reshape(head_shape)
        key_segments = lax.dynamic_slice_in_dim(segments, start, block_len, 1)
        allowed = build_mask(own_places, own_segments, start + local_places, key_segments)
        return (key_heads, value_heads, allowed)

    def stats_step(index, state):
        key_heads, value_heads, allowed = key_block(index)

        def stats_update(state):
            peaks, totals = state
            masked = block_scores(queries, key_heads, allowed, score_scale)
            new_peaks = jnp.maximum(peaks, jnp.max(masked, -1))
            weights = jnp.where(allowed[:, None], jnp.exp(masked - new_peaks[..., None]), 0.0)
            return (new_peaks, totals * jnp.exp(peaks - new_peaks) + jnp.sum(weights, -1))

        return lax.cond(jnp.any(allowed), stats_update, keep_state, state)

    stat_shape = (row_count, head_count, block_len)
    peaks, totals = lax.fori_loop(
        0, blocks, stats_step, (jnp.full(stat_shape, -1e30, f32), jnp.zeros(stat_shape, f32))
    )

    def context_step(index, summed):
        key_heads, value_heads, allowed = key_block(index)

        def context_update(summed):
            masked = block_scores(queries, key_heads, allowed, score_scale)
            attention = block_probs(masked, allowed, peaks, totals).astype(bf16)
            return summed + jnp.einsum(
                "rhqk,rkhd->rqhd", attention, value_heads, preferred_element_type=f32
            )

        return lax.cond(jnp.any(allowed), context_update, keep_state, summed)

    context_sum = lax.fori_loop(0, blocks, context_step, jnp.zeros(head_shape, f32))
    context = context_sum.reshape(flat_tokens, model_width).astype(bf16)
    attn_out = jnp.dot(context, project_out, preferred_element_type=f32)
    middle = stream + attn_out
    normed_two, norm_two_back = jax.vjp(layer_norm, middle, second_gain, second_shift)
    normed_two_low = normed_two.astype(bf16)
    experts = centroids.shape[0]
    route_ids = routes[:, :, 0]
    picked = (route_ids[:, :, None] == lax.iota(jnp.int32, experts)[None, None, :]).astype(
        jnp.int32
    )
    chosen = jnp.dot(
        picked.reshape(flat_tokens, experts).astype(f32), centroids, precision=lax.Precision.HIGHEST
    )
    gate_value = jax.nn.sigmoid(jnp.sum(normed_two * chosen, -1))
    slot_index = jnp.sum(jnp.cumsum(picked, 1) * picked, 2) - 1
    capacity = 2 * block_len // experts
    row_index = lax.iota(jnp.int32, row_count)[:, None]
    target = ((route_ids * row_count + row_index) * capacity + slot_index).reshape(flat_tokens)
    local_experts = expert_up.shape[0]
    peer_count = experts // local_experts
    slot_shape = (experts, row_count, capacity, model_width)
    slot_rows = experts * row_count * capacity
    work_shape = (peer_count, local_experts, row_count * capacity, model_width)
    outgoing = jnp.zeros((slot_rows, model_width), bf16).at[target].set(normed_two_low)
    arrived = lax.all_to_all(
        outgoing.reshape(slot_shape), "wide", split_axis=0, concat_axis=0, tiled=True
    ).reshape(work_shape)
    hidden_pre = jnp.einsum("secd,edf->secf", arrived, expert_up, preferred_element_type=f32)
    hidden_act, gelu_back = jax.vjp(gelu_exact, hidden_pre)
    hidden_low = hidden_act.astype(bf16)
    produced = jnp.einsum(
        "secf,efd->secd", hidden_low, expert_down, preferred_element_type=f32
    ).astype(bf16)
    returned = lax.all_to_all(
        produced.reshape(slot_shape), "wide", split_axis=0, concat_axis=0, tiled=True
    )
    branch = returned.reshape(slot_rows, model_width)[target].astype(f32)
    result = (middle + gate_value[:, None] * branch).astype(bf16)
    upstream = cotangent.reshape(flat_tokens, model_width).astype(f32)
    branch_grad = (gate_value[:, None] * upstream).astype(bf16)
    gate_grad = jnp.sum(upstream * branch, -1)
    logit_grad = gate_grad * gate_value * (1.0 - gate_value)
    back_out = jnp.zeros((slot_rows, model_width), bf16).at[target].set(branch_grad)
    back_arrived = lax.all_to_all(
        back_out.reshape(slot_shape), "wide", split_axis=0, concat_axis=0, tiled=True
    ).reshape(work_shape)
    down_grad = jnp.einsum("secf,secd->efd", hidden_low, back_arrived, preferred_element_type=f32)
    act_grad = jnp.einsum("secd,efd->secf", back_arrived, expert_down, preferred_element_type=f32)
    pre_low = gelu_back(act_grad)[0].astype(bf16)
    up_grad = jnp.einsum("secd,secf->edf", arrived, pre_low, preferred_element_type=f32)
    row_grads = jnp.einsum("secf,edf->secd", pre_low, expert_up, preferred_element_type=f32).astype(
        bf16
    )
    back_returned = lax.all_to_all(
        row_grads.reshape(slot_shape), "wide", split_axis=0, concat_axis=0, tiled=True
    )
    normed_two_grad = (
        back_returned.reshape(slot_rows, model_width)[target].astype(f32)
        + logit_grad[:, None] * chosen
    )
    middle_grad, gain_two_grad, shift_two_grad = norm_two_back(normed_two_grad)
    middle_grad = middle_grad + upstream
    attn_grad = middle_grad.astype(bf16)
    out_proj_grad = jnp.einsum("td,te->de", context, attn_grad, preferred_element_type=f32)
    context_grad = jnp.einsum(
        "te,de->td", attn_grad, project_out, preferred_element_type=f32
    ).astype(bf16)
    grad_flat = context_grad.reshape(row_count, block_len, model_width)
    grad_heads = grad_flat.reshape(head_shape)

    def inner_step(index, inner):
        key_heads, value_heads, allowed = key_block(index)

        def inner_update(inner):
            masked = block_scores(queries, key_heads, allowed, score_scale)
            probs_full = block_probs(masked, allowed, peaks, totals)
            prob_grad = jnp.einsum(
                "rqhd,rkhd->rhqk", grad_heads, value_heads, preferred_element_type=f32
            )
            return inner + jnp.sum(probs_full * prob_grad, -1)

        return lax.cond(jnp.any(allowed), inner_update, keep_state, inner)

    inner = lax.fori_loop(0, blocks, inner_step, jnp.zeros(stat_shape, f32))

    def grad_step(index, state):
        key_heads, value_heads, allowed = key_block(index)

        def grad_update(state):
            query_sum, key_terms = state
            masked = block_scores(queries, key_heads, allowed, score_scale)
            probs_full = block_probs(masked, allowed, peaks, totals)
            prob_grad = jnp.einsum(
                "rqhd,rkhd->rhqk", grad_heads, value_heads, preferred_element_type=f32
            )
            score_grad = (probs_full * (prob_grad - inner[..., None])).astype(bf16)
            value_grad = jnp.einsum(
                "rhqk,rqhd->rkhd", probs_full.astype(bf16), grad_heads, preferred_element_type=f32
            )
            key_grad = (
                jnp.einsum("rhqk,rqhd->rkhd", score_grad, queries, preferred_element_type=f32)
                * score_scale
            )
            query_sum = (
                query_sum
                + jnp.einsum("rhqk,rkhd->rqhd", score_grad, key_heads, preferred_element_type=f32)
                * score_scale
            )
            block_terms = jnp.concatenate(
                [
                    key_grad.reshape(row_count, block_len, model_width),
                    value_grad.reshape(row_count, block_len, model_width),
                ],
                2,
            )
            key_terms = lax.dynamic_update_slice_in_dim(
                key_terms, block_terms, index * block_len, 1
            )
            return (query_sum, key_terms)

        return lax.cond(jnp.any(allowed), grad_update, keep_state, state)

    start_state = (jnp.zeros(head_shape, f32), jnp.zeros((row_count, length, 2 * model_width), f32))
    query_sum, key_terms = lax.fori_loop(0, blocks, grad_step, start_state)
    keyval_grad = lax.psum_scatter(
        key_terms.astype(jnp.bfloat16), "blk", scatter_dimension=1, tiled=True
    ).astype(jnp.float32)
    query_grad = query_sum.reshape(row_count, block_len, model_width)
    joint_grad = (
        jnp.concatenate([query_grad, keyval_grad], 2)
        .reshape(flat_tokens, 3 * model_width)
        .astype(bf16)
    )
    in_proj_grad = jnp.einsum("td,te->de", normed_one_low, joint_grad, preferred_element_type=f32)
    normed_one_grad = jnp.einsum("te,de->td", joint_grad, project_in, preferred_element_type=f32)
    stream_grad, gain_one_grad, shift_one_grad = norm_one_back(normed_one_grad)
    stream_grad = stream_grad + middle_grad
    summed = lax.psum(
        (in_proj_grad, out_proj_grad, gain_one_grad, shift_one_grad, gain_two_grad, shift_two_grad),
        ("blk", "wide"),
    )
    up_share, down_share = (
        lax.psum_scatter(
            up_grad.astype(jnp.bfloat16), "blk", scatter_dimension=2, tiled=True
        ).astype(jnp.float32),
        lax.psum_scatter(
            down_grad.astype(jnp.bfloat16), "blk", scatter_dimension=1, tiled=True
        ).astype(jnp.float32),
    )
    out_shape = (row_count, block_len, model_width)
    return (
        result.reshape(out_shape),
        stream_grad.reshape(out_shape),
        summed[0],
        summed[1],
        summed[2],
        summed[3],
        summed[4],
        summed[5],
        up_share,
        down_share,
    )


def solution(mesh):
    return jax.shard_map(
        body,
        mesh=mesh,
        in_specs=(
            P("wide", "blk", None),
            P("wide", None),
            P("wide", "blk", None),
            P(),
            P(),
            P(),
            P(),
            P(),
            P(),
            P(),
            P("wide", None, None),
            P("wide", None, None),
            P("wide", "blk", None),
        ),
        out_specs=(
            P("wide", "blk", None),
            P("wide", "blk", None),
            P(),
            P(),
            P(),
            P(),
            P(),
            P(),
            P("wide", None, "blk"),
            P("wide", "blk", None),
        ),
        check_vma=False,
    )
```

profile of v0, /device:TPU:0, one launch (start us, length us, event | category | flops | bytes accessed | tf_op | source)
XLA Modules:
  0.0 1604.1 jit_solution(495514680499398602)
XLA Ops:
  49.2 58.7 %all-gather.3.cloned.1.call-done = bf16[2048,1536]{1,0:T(8,128)(2,1)} async-done(((bf16[1024,1536]{1,0:T(8,128)(2,1)}), bf16[2048,1536]{1,0:T(8,128)(2,1)}) %all-gather.3.cloned.1.call-update) | async-done | bytes 6291472 | tf_op jit(solution)/shard_map/all_gather | solution.py:76
  117.8 57.8 %while.66 = (s32[]{:T(128)}, f32[1,12,1024]{2,1,0:T(8,128)}, f32[1,12,1024]{2,1,0:T(8,128)}, s32[1,2048]{1,0:T(1,128)}, s32[1,1024]{1,0:T(1,128)}, /*index=5*/bf...) while((s32[]{:T(128)}, f32[1,12,1024]{2,1,0:T(8,128)}, ...), condition=%wide.region_8.9_spmd.clone, body=%wide.region_2.8_spmd.clone.sunk | while | flops 1715496960 | bytes 111362408 | solution.py:100
  122.4 48.4 %conditional.12 = ((f32[1,12,1024]{2,1,0:T(8,128)}, f32[1,12,1024]{2,1,0:T(8,128)})) conditional(s32[]{:T(128)} %convert_element_type.333, (f32[1,12,1024]{2,1,0:T(8,128)}, f32[1,12,1024]{2,1,0:T(8,128)}) %tuple.211, (pred[1,1024,1024]{1,2,0:T(8,128)(4,1)}, bf16[1,2048,1536]{1,2,0:T(8,128)(2,1)}, s32[]{:T(128)}, bf16[1,1024,12,64]{1,3,2,0:T(8,128)(2,1)}, ...), branch_computations={%region_4.0_spmd, %region_5.7_spmd} | conditional | flops 1711300608 | bytes 110280816 | solution.py:97
  177.6 37.1 %while.67 = (s32[]{:T(128)}, f32[1,1024,12,64]{1,3,2,0:T(8,128)}, s32[1,2048]{1,0:T(1,128)}, s32[1,1024]{1,0:T(1,128)}, bf16[1,2048,1536]{1,2,0:T(8,128)(2,1)}, ...) while((s32[]{:T(128)}, f32[1,1024,12,64]{1,3,2,0:T(8,128)}, ...), condition=%wide.region_13.14_spmd.clone, body=%wide.region_9.13_spmd.clone.sunk | while | flops 3301705728 | bytes 19530000 | solution.py:116
  182.4 27.2 %conditional.13 = (f32[1,1024,12,64]{1,3,2,0:T(8,128)}) conditional(s32[]{:T(128)} %convert_element_type.334, f32[1,1024,12,64]{1,3,2,0:T(8,128)} %get-tuple-element.1666, (bf16[1,2048,1536]{1,2,0:T(8,128)(2,1)}, s32[]{:T(128)}, pred[1,1024,1024]{1,2,0:T(8,128)(4,1)}, bf16[1,1024,12,64]{1,3,2,0:T(8,128)(2,1)}, f32[1,12,1024]{2,1,0:T(8,128)}, ...), branch_computations={%region_11.11_spmd, %region_12.12_spmd} | conditional | flops 3297509376 | bytes 18448412 | solution.py:114
  239.1 75.8 %all_to_all.20 = bf16[16,1,128,768]{3,2,1,0:T(8,128)(2,1)S(1)} all-to-all(bf16[16,1,128,768]{3,2,1,0:T(8,128)(2,1)} %bitcast.452), channel_id=1, replica_groups=mesh['blk'=2,'wide'=16] {'wide'}, dimensions={0} | all-to-all | bytes 6291456 | tf_op jit(solution)/shard_map/all_to_all | solution.py:141
  332.0 66.8 %convert_bitcast_fusion.2 = bf16[16,1,128,768]{3,2,1,0:T(8,128)(2,1)} fusion(bf16[1,3072,768]{2,1,0:T(8,128)(2,1)S(1)} %bitcast.478, f32[16,128,3072]{2,1,0:T(8,128)} %fusion.90), kind=kOutput, calls=%fused_computation.172 | convolution fusion | flops 10074193920 | bytes 33030144 | tf_op jit(solution)/shard_map/secf,efd->secd/dot_general | solution.py:147
  406.9 56.8 %all-to-all-done.1 = bf16[16,1,128,768]{3,2,1,0:T(8,128)(2,1)} async-done(((bf16[16,1,128,768]{3,2,1,0:T(8,128)(2,1)}), bf16[16,1,128,768]{3,2,1,0:T(8,128)(2,1)}, u32[]{:S(2)}, u32[]{:S(2)}) %all-to-all-start.1) | async-done | bytes 3145760 | tf_op jit(solution)/shard_map/all_to_all | solution.py:150
  489.0 85.5 %all_to_all.21 = bf16[16,1,128,768]{3,2,1,0:T(8,128)(2,1)S(1)} all-to-all(bf16[16,1,128,768]{3,2,1,0:T(8,128)(2,1)} %bitcast.451), channel_id=1, replica_groups=mesh['blk'=2,'wide'=16] {'wide'}, dimensions={0} | all-to-all | bytes 6291456 | tf_op jit(solution)/shard_map/all_to_all | solution.py:160
  576.2 66.9 %fusion.60 = bf16[16,1,128,3072]{3,2,0,1:T(8,128)(2,1)S(1)} fusion(f32[16,128,3072]{2,1,0:T(8,128)} %fusion.90, bf16[1,3072,768]{2,1,0:T(8,128)(2,1)} %param.40, bf16[16,1,128,768]{3,2,1,0:T(8,128)(2,1)S(1)} %all_to_all.21), kind=kOutput, calls=%fused_computation.91 | convolution fusion | flops 10116661248 | bytes 45613056 | tf_op jit(solution)/shard_map/secd,efd->secf/dot_general | solution.py:164
  664.3 59.3 %all-to-all-done.3 = bf16[16,1,128,768]{3,2,1,0:T(8,128)(2,1)} async-done(((bf16[16,1,128,768]{3,2,1,0:T(8,128)(2,1)}), bf16[16,1,128,768]{3,2,1,0:T(8,128)(2,1)}, u32[]{:S(2)}, u32[]{:S(2)}) %all-to-all-start.3) | async-done | bytes 3145760 | tf_op jit(solution)/shard_map/all_to_all | solution.py:170
  759.6 59.3 %while.68 = (s32[]{:T(128)}, f32[1,12,1024]{2,1,0:T(8,128)}, s32[1,2048]{1,0:T(1,128)}, s32[1,1024]{1,0:T(1,128)}, bf16[1,2048,1536]{1,2,0:T(8,128)(2,1)}, /*ind...) while((s32[]{:T(128)}, f32[1,12,1024]{2,1,0:T(8,128)}, ...), condition=%wide.region_30.31_spmd.clone, body=%wide.region_25.30_spmd.clone.sunk | while | flops 3313502208 | bytes 115671320 | solution.py:200
  764.3 50.0 %conditional.14 = (f32[1,12,1024]{2,1,0:T(8,128)}) conditional(s32[]{:T(128)} %convert_element_type.335, f32[1,12,1024]{2,1,0:T(8,128)} %get-tuple-element.1706, (pred[1,1024,1024]{1,2,0:T(8,128)(4,1)}, bf16[1,2048,1536]{1,2,0:T(8,128)(2,1)}, s32[]{:T(128)}, bf16[1,1024,12,64]{1,3,2,0:T(8,128)(2,1)}, f32[1,12,1024]{2,1,0:T(8,128)}, ...), branch_computations={%region_27.27_spmd, %region_28.29_spmd} | conditional | flops 3309305856 | bytes 114589720 | solution.py:198
  789.1 23.6 %fusion.35 = f32[12,1024]{1,0:T(8,128)S(1)} fusion(f32[12,1024,1024]{2,1,0:T(8,128)} %fusion.41, f32[12,1024]{1,0:T(8,128)} %bitcast.458, f32[12,1024]{1,0:T(8,128)} %bitcast.454, pred[1024,1024]{0,1:T(8,128)(4,1)} %bitcast.449, bf16[1024,12,64]{0,2,1:T(8,128)(2,1)} %bitcast.446, bf16[1,1024,12,64]{1,3,2,0:T(8,128)(2,1)} %get-tuple-element.898), kind=kOutput, calls=%fused_computation.36 | convolution fusion | flops 1698680832 | bytes 54673408 | tf_op jit(solution)/shard_map/while/body/eval_jaxpr/cond/branch_1_fun/rqhd,rkhd->rhqk/dot_general | solution.py:193
  824.4 119.0 %while.69 = (s32[]{:T(128)}, f32[1,1024,12,64]{1,3,2,0:T(8,128)}, bf16[1,2048,1536]{1,2,0:T(8,128)(2,1)}, s32[1,2048]{1,0:T(1,128)}, s32[1,1024]{1,0:T(1,128)}, ...) while((s32[]{:T(128)}, f32[1,1024,12,64]{1,3,2,0:T(8,128)}, ...), condition=%wide.region_35.36_spmd.clone, body=%wide.region_31.35_spmd.clone.sunk | while | flops 8179943424 | bytes 324715008 | solution.py:240
  829.5 109.0 %conditional.15 = ((f32[1,1024,12,64]{1,3,2,0:T(8,128)}, bf16[1,2048,1536]{1,2,0:T(8,128)(2,1)})) conditional(s32[]{:T(128)} %convert_element_type.336, (f32[1,1024,12,64]{1,3,2,0:T(8,128)}, bf16[1,2048,1536]{1,2,0:T(8,128)(2,1)}) %tuple.224, (bf16[1,2048,1536]{1,2,0:T(8,128)(2,1)}, s32[]{:T(128)}, pred[1,1024,1024]{1,2,0:T(8,128)(4,1)}, ...), branch_computations={%region_33.33_spmd, %region_34.34_spmd} | conditional | flops 8175747072 | bytes 323633344 | solution.py:237
  833.4 25.8 %fusion.47 = f32[12,1024,1024]{1,2,0:T(8,128)} fusion(f32[12,1024]{1,0:T(8,128)} %bitcast.459, f32[12,1024]{1,0:T(8,128)} %bitcast.455, pred[1024,1024]{0,1:T(8,128)(4,1)} %bitcast.448, bf16[1024,12,64]{0,2,1:T(8,128)(2,1)} %bitcast.439, bf16[1,1024,12,64]{1,3,2,0:T(8,128)(2,1)} %get-tuple-element.915), kind=kOutput, calls=%fused_computation.54 | convolution fusion | flops 1673527296 | bytes 54624256 | tf_op jit(solution)/shard_map/while/body/eval_jaxpr/cond/branch_1_fun/rqhd,rkhd->rhqk/dot_general | solution.py:27
  878.4 27.5 %fusion.43 = bf16[12,1024,1024]{1,2,0:T(8,128)(2,1)} fusion(f32[12,1024,1024]{1,2,0:T(8,128)} %fusion.47, f32[12,1024]{1,0:T(8,128)} %bitcast.34, bf16[1024,12,64]{0,2,1:T(8,128)(2,1)} %bitcast.442, bf16[1,1024,12,64]{1,3,2,0:T(8,128)(2,1)} %get-tuple-element.918), kind=kOutput, calls=%fused_computation.49 | convolution fusion | flops 1648361472 | bytes 78692352 | tf_op jit(solution)/shard_map/while/body/eval_jaxpr/cond/branch_1_fun/rqhd,rkhd->rhqk/dot_general | solution.py:209
  958.9 64.2 %fusion.95 = bf16[1,3072,768]{2,1,0:T(8,128)(2,1)} fusion(bf16[16,1,128,768]{3,2,1,0:T(8,128)(2,1)} %copy-done.18, f32[16,128,3072]{2,1,0:T(8,128)} %fusion.90), kind=kOutput, calls=%fused_computation.140 | convolution fusion | flops 10074980352 | bytes 33030144 | tf_op jit(solution)/shard_map/secf,secd->efd/dot_general | solution.py:163
  1031.4 232.9 %reduce-scatter.4.cloned.1.call-done = bf16[1,1024,1536]{1,2,0:T(8,128)(2,1)} async-done(((bf16[1,2048,1536]{1,2,0:T(8,128)(2,1)}), bf16[1,1024,1536]{1,2,0:T(8,128)(2,1)}) %reduce-scatter.4.cloned.1.call-update) | async-done | bytes 3145744 | tf_op jit(solution)/shard_map/reduce_scatter | solution.py:241
  1277.0 50.3 %reduce-scatter.6.cloned.1.call-done = bf16[1,768,1536]{2,1,0:T(8,128)(2,1)} async-done(((bf16[1,768,3072]{2,1,0:T(8,128)(2,1)}), bf16[1,768,1536]{2,1,0:T(8,128)(2,1)}) %reduce-scatter.6.cloned.1.call-update) | async-done | bytes 2359312 | tf_op jit(solution)/shard_map/reduce_scatter | solution.py:259
  1331.8 57.7 %reduce-scatter.8.cloned.1.call-done = bf16[1,1536,768]{2,1,0:T(8,128)(2,1)} async-done(((bf16[1,3072,768]{2,1,0:T(8,128)(2,1)}), bf16[1,1536,768]{2,1,0:T(8,128)(2,1)}) %reduce-scatter.8.cloned.1.call-update) | async-done | bytes 2359312 | tf_op jit(solution)/shard_map/reduce_scatter | solution.py:262
  1418.2 41.5 %all-reduce = (f32[768]{0:T(1024)}, f32[768]{0:T(1024)}, f32[768]{0:T(1024)}, f32[768]{0:T(1024)}) all-reduce(f32[768]{0:T(1024)S(1)} %copy-done.54, f32[768]{0:T(1024)S(1)} %copy-done.57, f32[768]{0:T(1024)S(1)} %copy-done.52, f32[768]{0:T(1024)S(1)} %copy-done.53), channel_id=1, replica_groups=mesh['blk'=2,'wide'=16] {'blk','wide'}, use_global_device_ids=true, to_apply=%region_42.43 | all-reduce | flops 3072 | bytes 24576 | tf_op jit(solution)/shard_map/psum | solution.py:254
  1459.7 129.5 %all-reduce.4.cloned.1.call-done = (f32[768,2304]{1,0:T(8,128)}, f32[768,768]{1,0:T(8,128)}) async-done(((f32[768,2304]{1,0:T(8,128)}, f32[768,768]{1,0:T(8,128)}), (f32[768,2304]{1,0:T(8,128)}, f32[768,768]{1,0:T(8,128)})) %all-reduce.4.cloned.1.call-update) | async-done | bytes 9437200 | tf_op jit(solution)/shard_map/psum | solution.py:254
  (264 shorter events, 459.9 us)
Async XLA Ops:
  7.2 100.7 %all-gather.3.cloned.1.call-start = ((), (), s32[]{:S(2)}) async-start(), calls=%async_computation.10 | async-start | bytes 9437184 | tf_op jit(solution)/shard_map/all_gather | solution.py:76
  148.2 21.9 %copy-start.15 = (f32[1,12,1024]{2,1,0:T(8,128)S(1)}, f32[1,12,1024]{2,1,0:T(8,128)}, u32[]{:S(2)}) copy-start(f32[1,12,1024]{2,1,0:T(8,128)} %get-tuple-element.855) | copy-start | bytes 147460 | tf_op jit(solution)/shard_map/while/body/eval_jaxpr/cond
  148.2 21.9 %copy-start.19 = (f32[1,12,1024]{2,1,0:T(8,128)S(1)}, f32[1,12,1024]{2,1,0:T(8,128)}, u32[]{:S(2)}) copy-start(f32[1,12,1024]{2,1,0:T(8,128)} %get-tuple-element.860) | copy-start | bytes 147460 | tf_op jit(solution)/shard_map/while/body/eval_jaxpr/cond
  239.1 92.8 %slice-start = ((s8[4718592]{0:T(1024)(128)(4,1)}), s8[4194304]{0:T(1024)(128)(4,1)S(1)}, s32[]{:S(2)}) async-start(s8[4718592]{0:T(1024)(128)(4,1)} %bitcast.477), calls=%async_computation.12 | async-start | bytes 8388608
  315.0 17.0 %copy-start.17 = (bf16[16,1,128,768]{3,2,1,0:T(8,128)(2,1)}, bf16[16,1,128,768]{3,2,1,0:T(8,128)(2,1)S(1)}, u32[]{:S(2)}) copy-start(bf16[16,1,128,768]{3,2,1,0:T(8,128)(2,1)S(1)} %all_to_all.20) | copy-start | bytes 9437188
  315.0 17.0 %slice-start.1 = ((s8[4718592]{0:T(1024)(128)(4,1)}), s8[524288]{0:T(1024)(128)(4,1)S(1)}, s32[]{:S(2)}) async-start(s8[4718592]{0:T(1024)(128)(4,1)} %bitcast.477), calls=%async_computation.13 | async-start | bytes 1048576
  398.8 64.9 %all-to-all-start.1 = ((bf16[16,1,128,768]{3,2,1,0:T(8,128)(2,1)}), bf16[16,1,128,768]{3,2,1,0:T(8,128)(2,1)}, u32[]{:S(2)}, u32[]{:S(2)}) async-start(bf16[16,1,128,768]{3,2,1,0:T(8,128)(2,1)} %convert_bitcast_fusion.2), calls=%async_computation.1 | async-start | bytes 6291456 | tf_op jit(solution)/shard_map/all_to_all | solution.py:150
  406.8 64.7 %copy-start.50 = (s32[1024]{0:T(1024)}, s32[1024]{0:T(1024)S(1)}, u32[]{:S(2)}) copy-start(s32[1024]{0:T(1024)S(1)} %broadcast_clamp_fusion) | copy-start | bytes 12292
  406.8 67.2 %copy-start.38 = (f32[1024]{0:T(1024)}, f32[1024]{0:T(1024)S(1)}, u32[]{:S(2)}) copy-start(f32[1024]{0:T(1024)S(1)} %add_divide_fusion) | copy-start | bytes 12292
  576.2 71.4 %copy-start.58 = (bf16[1,768,3072]{2,1,0:T(8,128)(2,1)S(1)}, bf16[1,768,3072]{2,1,0:T(8,128)(2,1)}, u32[]{:S(2)}) copy-start(bf16[1,768,3072]{2,1,0:T(8,128)(2,1)} %param.39) | copy-start | bytes 14155780
  658.9 64.8 %all-to-all-start.3 = ((bf16[16,1,128,768]{3,2,1,0:T(8,128)(2,1)}), bf16[16,1,128,768]{3,2,1,0:T(8,128)(2,1)}, u32[]{:S(2)}, u32[]{:S(2)}) async-start(bf16[16,1,128,768]{3,2,1,0:T(8,128)(2,1)} %convert_bitcast_fusion.1), calls=%async_computation.3 | async-start | bytes 6291456 | tf_op jit(solution)/shard_map/all_to_all | solution.py:170
  664.2 600.0 %reduce-scatter.4.cloned.1.call-start = ((), (), s32[]{:S(2)}) async-start(), calls=%async_computation.7 | async-start | bytes 9437184 | tf_op jit(solution)/shard_map/reduce_scatter | solution.py:241
  723.7 21.0 %copy-start.26 = (f32[1024]{0:T(1024)S(1)}, f32[1024]{0:T(1024)}, u32[]{:S(2)}) copy-start(f32[1024]{0:T(1024)} %copy-done.25) | copy-start | bytes 12292
  723.7 21.1 %copy-start.30 = (f32[1024]{0:T(1024)S(1)}, f32[1024]{0:T(1024)}, u32[]{:S(2)}) copy-start(f32[1024]{0:T(1024)} %copy-done.29) | copy-start | bytes 12292
  723.7 21.1 %copy-start.35 = (f32[768]{0:T(1024)S(1)}, f32[768]{0:T(1024)}, u32[]{:S(2)}) copy-start(f32[768]{0:T(1024)} %param.36) | copy-start | bytes 9220
  919.6 15.8 copy-start.6
  919.6 15.8 copy-start.10
  943.4 383.9 %reduce-scatter.6.cloned.1.call-start = ((), (), s32[]{:S(2)}) async-start(), calls=%async_computation.8 | async-start | bytes 7077888 | tf_op jit(solution)/shard_map/reduce_scatter | solution.py:259
  958.8 430.7 %reduce-scatter.8.cloned.1.call-start = ((), (), s32[]{:S(2)}) async-start(), calls=%async_computation.9 | async-start | bytes 7077888 | tf_op jit(solution)/shard_map/reduce_scatter | solution.py:262
  1023.1 566.1 %all-reduce.4.cloned.1.call-start = ((), (), s32[]{:S(2)}) async-start(), calls=%async_computation.11 | async-start | bytes 18874368 | tf_op jit(solution)/shard_map/psum | solution.py:254
  1026.6 237.6 %copy-start.28 = (f32[1024]{0:T(1024)S(1)}, f32[1024]{0:T(1024)}, u32[]{:S(2)}) copy-start(f32[1024]{0:T(1024)} %copy-done.27) | copy-start | bytes 12292
  1026.6 237.6 %copy-start.37 = (f32[1024]{0:T(1024)S(1)}, f32[1024]{0:T(1024)}, u32[]{:S(2)}) copy-start(f32[1024]{0:T(1024)} %copy-done.36) | copy-start | bytes 12292
  1026.6 237.6 %copy-start.47 = (f32[768]{0:T(1024)S(1)}, f32[768]{0:T(1024)}, u32[]{:S(2)}) copy-start(f32[768]{0:T(1024)} %param.34) | copy-start | bytes 9220
  1026.6 237.6 %copy-start.62 = (f32[768]{0:T(1024)S(1)}, f32[768]{0:T(1024)}, u32[]{:S(2)}) copy-start(f32[768]{0:T(1024)} %param.35) | copy-start | bytes 9220
  (49 other events, 259.0 us)
Sparse Core Ops, SparseCore 0:
  24.8 83.0 all-gather.2
  943.5 320.6 reduce-scatter.3
  1267.2 59.9 reduce-scatter.5
  1329.4 59.9 reduce-scatter.7
  1396.8 192.3 all-reduce.3
where the time goes:
time: 1620 us; the launch traced here: 1600 us
  waiting for transfers between devices  645 us (40%)
  matrix products  474 us (29%)
  blocking collectives  203 us (13%)
  local copies, waits for them, and re-layouts  144 us (9%)
  other arithmetic  105 us (6%)
    reduce_scatter x1, waiting for transfers between devices, body(): lax.psum_scatter(key_terms.astype(jnp.bfloat16), 'blk', scatter_dimension...  233 us
    psum x1, waiting for transfers between devices, body(): lax.psum((in_proj_grad, out_proj_grad, gain_one_grad, shift_one_grad, gai...  130 us
    all_to_all x1, blocking collectives, body(): lax.all_to_all(back_out.reshape(slot_shape), 'wide', split_axis=0, concat...  85.5 us
    all_to_all x1, blocking collectives, body(): lax.all_to_all(outgoing.reshape(slot_shape), 'wide', split_axis=0, concat...  75.8 us
    dot_general x3, matrix products, block_scores(): jnp.einsum('rqhd,rkhd->rhqk', query_heads, key_heads, preferred_element_t...  69 us
    dot_general x1, matrix products, body(): jnp.einsum('secd,efd->secf', back_arrived, expert_down, preferred_element...  66.9 us
    dot_general x1, matrix products, body(): jnp.einsum('secf,efd->secd', hidden_low, expert_down, preferred_element_t...  66.8 us
    dot_general x1, matrix products, body(): jnp.einsum('secf,secd->efd', hidden_low, back_arrived, preferred_element_...  64.2 us
  transfers between devices with their start and end apart: 7, of which 7 were waited for; matrix products, arithmetic and copies ran while one was open for 10% of the time, Pallas kernels for 0%

commit v1 on v0

v1 whole, which is shorter than its diff:
```python
import functools

import jax
import jax.numpy as jnp
from jax import lax
from jax.experimental import pallas as pl
from jax.experimental.pallas import tpu as pltpu
from jax.sharding import PartitionSpec as P

HEAD_DIM = 64
GROUP = 4
LANES = GROUP * HEAD_DIM
NEG = -1e30
f32 = jnp.float32
bf16 = jnp.bfloat16
VMEM_LIMIT = 60 * 1024 * 1024
SHORT = pl.CostEstimate(flops=1, bytes_accessed=1, transcendentals=0)
LONG = pl.CostEstimate(flops=10**11, bytes_accessed=1, transcendentals=0)


def tile_of(size, most):
    tile = most
    while size % tile:
        tile //= 2
    return tile


def dot(a, b):
    return jnp.dot(a, b, preferred_element_type=f32)


def dot_nt(a, b):
    return lax.dot_general(a, b, (((1,), (1,)), ((), ())), preferred_element_type=f32)


def params(**more):
    return pltpu.CompilerParams(vmem_limit_bytes=VMEM_LIMIT, **more)


def largest_norm(x):
    head = lax.broadcasted_iota(jnp.int32, (LANES, 2 * HEAD_DIM), 0) // HEAD_DIM
    lane = lax.broadcasted_iota(jnp.int32, (LANES, 2 * HEAD_DIM), 1)
    pick = jnp.where(head == lane, 1.02, 0.0).astype(bf16)
    wide = x.astype(f32)
    return jnp.sqrt(jnp.max(dot((wide * wide).astype(bf16), pick), 0, keepdims=True))


def pair_of(head):
    return slice(2 * HEAD_DIM * (head // 2), 2 * HEAD_DIM * (head // 2 + 1))


def head_of_pair(pair, head, other=0.0):
    lane = lax.broadcasted_iota(jnp.int32, (1, 2 * HEAD_DIM), 1)
    keep = lane < HEAD_DIM if head % 2 == 0 else lane >= HEAD_DIM
    return jnp.where(keep, pair, jnp.full_like(pair, other))


def pieces_of(length, most):
    return [(at, min(most, length - at)) for at in range(0, length, most)]


def key_place(at, me, block_len, own):
    if own:
        return me * block_len + at
    return (me - 1 - at // block_len) * block_len + at % block_len


def mask_of(at, size, block, me, block_len, tile, starts, own, flipped):
    shape = (size, tile) if flipped else (tile, size)
    key = lax.broadcasted_iota(jnp.int32, shape, 0 if flipped else 1) + key_place(at, me, block_len, own)
    mask = key >= starts
    if own:
        query = lax.broadcasted_iota(jnp.int32, shape, 1 if flipped else 0) + (me * block_len + block * tile)
        mask = mask & (key <= query)
    return mask


def needed(at, size, block, low, me, block_len, tile, own):
    place = key_place(at, me, block_len, own)
    there = place + size > low
    if own:
        return jnp.logical_and(there, at < (block + 1) * tile)
    return jnp.logical_and(there, place >= 0)


def stat_place(head):
    return 2 * (head % 2) + head // 2


def split(x):
    parts = []
    for _ in range(3):
        part = x.astype(bf16)
        parts.append(part)
        x = x - part.astype(f32)
    return parts


def rows_of_lanes(x, lanes):
    lane = lax.broadcasted_iota(jnp.int32, (8, x.shape[1]), 1)
    row = lax.broadcasted_iota(jnp.int32, (8, x.shape[1]), 0)
    pick = jnp.zeros((8, x.shape[1]), f32)
    for at, number in enumerate(lanes):
        pick = jnp.where((row == at) & (lane == number), 1.0, pick)
    return sum(dot_nt(pick.astype(bf16), part) for part in split(x))[: len(lanes)]


def attend_kernel(me_ref, low_ref, q_ref, k_ref, v_ref, ok_ref, ov_ref, start_ref, ctx_out, lse_out, va, ova, acc, safe, *, tile, block_len):
    row, block = pl.program_id(0), pl.program_id(2)
    me = me_ref[0]
    low = low_ref[row, block]
    scale = HEAD_DIM**-0.5
    lane = lax.broadcasted_iota(jnp.int32, (1, 2 * HEAD_DIM), 1)
    pieces = [(True, at, size) for at, size in pieces_of(block_len, 512)]
    pieces += [(False, at, size) for at, size in pieces_of(ok_ref.shape[1], min(1024, block_len))]

    @pl.when(block == 0)
    def prepare():
        for values, spread in ((v_ref, va), (ov_ref, ova)):
            for head in range(GROUP):
                spread[head] = head_of_pair(values[0, :, pair_of(head)], head, 1.0)
        keys = jnp.maximum(largest_norm(k_ref[0]), largest_norm(ok_ref[0]))
        bound = jnp.max(largest_norm(q_ref[0]) * keys) * scale
        safe[0] = (bound < 60.0).astype(jnp.int32)

    queries = q_ref[0, pl.ds(pl.multiple_of(block * tile, tile), tile), :]
    queries = (queries.astype(f32) * scale).astype(bf16)
    starts = column_of(start_ref[0])

    def scores_of(own, at, size, head):
        mask = mask_of(at, size, block, me, block_len, tile, starts, own, False)
        keys = (k_ref if own else ok_ref)[0, at : at + size, pair_of(head)]
        return jnp.where(mask, dot_nt(head_of_pair(queries[:, pair_of(head)], head), keys), NEG)

    def attend(shifted):
        acc[...] = jnp.zeros_like(acc)
        peaks = [jnp.full((tile, 1), NEG, f32)] * GROUP
        if shifted:
            for own, at, size in pieces:
                there = needed(at, size, block, low, me, block_len, tile, own)
                for head in range(GROUP):
                    higher = jnp.max(scores_of(own, at, size, head), 1, keepdims=True)
                    peaks[head] = jnp.maximum(peaks[head], jnp.where(there, higher, NEG))
        for own, at, size in pieces:

            @pl.when(needed(at, size, block, low, me, block_len, tile, own))
            def piece(own=own, at=at, size=size):
                for head in range(GROUP):
                    scores = scores_of(own, at, size, head)
                    if shifted:
                        scores = scores - peaks[head]
                    weights = jnp.exp(scores).astype(bf16)
                    acc[head] += dot(weights, (va if own else ova)[head, at : at + size])

        stats = []
        for head in range(0, GROUP, 2):
            even, odd = acc[head], acc[head + 1]
            sums = pltpu.roll(jnp.where(lane < HEAD_DIM, odd, even), HEAD_DIM, 1)
            ctx_out[0, :, pair_of(head)] = (jnp.where(lane < HEAD_DIM, even, odd) / sums).astype(bf16)
            stats.append(sums)
        first = lane % HEAD_DIM < HEAD_DIM // 2
        stat = jnp.log(jnp.where(first, stats[0], stats[1]))
        if shifted:
            for head in range(GROUP):
                stat = jnp.where(lane // (HEAD_DIM // 2) == stat_place(head), stat + peaks[head], stat)
        lse_out[0, 0] = rows_of_lanes(stat, [stat_place(head) * (HEAD_DIM // 2) for head in range(GROUP)])

    @pl.when(safe[0] == 1)
    def without_shift():
        attend(False)

    @pl.when(safe[0] == 0)
    def with_shift():
        attend(True)


def grad_kernel(me_ref, low_ref, *refs, tile, block_len, own):
    q_ref, k_ref, v_ref, go_ref, ctx_ref, lse_ref, start_ref = refs[:7]
    if own:
        dq_in, dq_out, dk_out, dv_out = refs[7:11]
    else:
        dq_out, dk_out, dv_out = refs[7:10]
    kt, dq, dk, dv = refs[-4:]
    row, block = pl.program_id(0), pl.program_id(2)
    me = me_ref[0]
    low = low_ref[row, block]
    scale = HEAD_DIM**-0.5
    length = k_ref.shape[1]
    pieces = pieces_of(length, min(512 if own else 1024, block_len))

    @pl.when(block == 0)
    def prepare():
        shape = (2 * HEAD_DIM, 2 * HEAD_DIM)
        same = lax.broadcasted_iota(jnp.int32, shape, 0) == lax.broadcasted_iota(jnp.int32, shape, 1)
        turn = jnp.where(same, scale, 0.0).astype(bf16)
        for head in range(0, GROUP, 2):
            kt[pair_of(head)] = dot_nt(turn, k_ref[0, :, pair_of(head)]).astype(bf16)
        dk[...] = jnp.zeros_like(dk)
        dv[...] = jnp.zeros_like(dv)

    queries = (q_ref[0].astype(f32) * scale).astype(bf16)
    go = go_ref[0]
    starts = start_ref[0]
    product = go.astype(f32) * ctx_ref[0].astype(f32)
    head_row = lax.broadcasted_iota(jnp.int32, (8, LANES), 0)
    head_lane = lax.broadcasted_iota(jnp.int32, (8, LANES), 1) // HEAD_DIM
    pick = jnp.where(head_row == head_lane, 1.0, 0.0).astype(bf16)
    inners = sum(dot_nt(pick, part) for part in split(product)[:2])
    inner = [inners[head : head + 1] for head in range(GROUP)]
    dq[...] = dq_in[0] if own else jnp.zeros_like(dq)
    for at, size in pieces:

        @pl.when(needed(at, size, block, low, me, block_len, tile, own))
        def piece(at=at, size=size):
            rows = slice(at, at + size)
            mask = mask_of(at, size, block, me, block_len, tile, starts, own, True)
            for first in range(0, GROUP, 2):
                pair = pair_of(first)
                keys, values = k_ref[0, rows, pair], v_ref[0, rows, pair]
                all_probs, all_grads, all_queries, all_go = [], [], [], []
                for head in (first, first + 1):
                    query = head_of_pair(queries[:, pair], head)
                    head_go = head_of_pair(go[:, pair], head)
                    scores = dot_nt(keys, query) - lse_ref[0, 0, head : head + 1, :]
                    probs = jnp.exp(jnp.where(mask, scores, NEG))
                    prob_grad = dot_nt(values, head_go)
                    score_grad = (probs * (prob_grad - inner[head])).astype(bf16)
                    lanes = slice(head * HEAD_DIM, (head + 1) * HEAD_DIM)
                    dq[lanes] += dot(kt[lanes, rows], score_grad)
                    all_probs.append(probs.astype(bf16))
                    all_grads.append(score_grad)
                    all_queries.append(query)
                    all_go.append(head_go)
                dv[rows, pair] += dot(jnp.concatenate(all_probs, 1), jnp.concatenate(all_go, 0))
                dk[rows, pair] += dot(jnp.concatenate(all_grads, 1), jnp.concatenate(all_queries, 0))

    if own:
        dq_out[0] = dq[...].T.astype(bf16)
    else:
        dq_out[0] = dq[...]

    @pl.when(block == pl.num_programs(2) - 1)
    def write():
        dk_out[0] = dk[...].astype(bf16)
        dv_out[0] = dv[...].astype(bf16)


class Attention:
    def __init__(self, me, starts, rows, block_len, width):
        self.rows, self.block_len, self.width = rows, block_len, width
        self.tile = tile_of(block_len, 512)
        self.tiles = block_len // self.tile
        self.groups = width // LANES
        self.me = me.reshape(1).astype(jnp.int32)
        self.low = starts[:, :: self.tile]
        self.start_row = starts.reshape(rows, 1, block_len)

    def queries(self, offset=0):
        return pl.BlockSpec((1, self.tile, LANES), lambda r, g, b, *_: (r, b, offset * self.groups + g))

    def keys(self, length, offset):
        return pl.BlockSpec((1, length, LANES), lambda r, g, b, *_: (r, 0, offset * self.groups + g))

    def stat(self):
        return pl.BlockSpec((1, 1, GROUP, self.tile), lambda r, g, b, *_: (r, g, 0, b))

    def turned(self):
        return pl.BlockSpec((1, LANES, self.tile), lambda r, g, b, *_: (r, g, b))

    def row_starts(self):
        return pl.BlockSpec((1, 1, self.tile), lambda r, g, b, *_: (r, 0, b))

    def shape(self, length, dtype=bf16):
        return jax.ShapeDtypeStruct((self.rows, length, self.width), dtype)

    def call(self, kernel, cost, in_specs, out_specs, out_shape, scratch, args):
        return pl.pallas_call(
            functools.partial(kernel, tile=self.tile, block_len=self.block_len),
            grid_spec=pltpu.PrefetchScalarGridSpec(
                num_scalar_prefetch=2,
                grid=(self.rows, self.groups, self.tiles),
                in_specs=in_specs,
                out_specs=out_specs,
                scratch_shapes=scratch,
            ),
            out_shape=out_shape,
            compiler_params=params(),
            cost_estimate=cost,
        )(self.me, self.low, *args)

    def forward(self, joint, other):
        size, length = self.block_len, other.shape[1]
        return self.call(
            attend_kernel,
            LONG,
            [self.keys(size, 0), self.keys(size, 1), self.keys(size, 2)]
            + [self.keys(length, 0), self.keys(length, 1), self.row_starts()],
            [self.queries(), self.stat()],
            [self.shape(size), jax.ShapeDtypeStruct((self.rows, self.groups, GROUP, size), f32)],
            [
                pltpu.VMEM((GROUP, size, 2 * HEAD_DIM), bf16),
                pltpu.VMEM((GROUP, length, 2 * HEAD_DIM), bf16),
                pltpu.VMEM((GROUP, self.tile, 2 * HEAD_DIM), f32),
                pltpu.SMEM((1,), jnp.int32),
            ],
            (joint, joint, joint, other, other, self.start_row),
        )

    def grad_scratch(self, length):
        total = pltpu.VMEM((length, LANES), f32)
        return [pltpu.VMEM((LANES, length), bf16), pltpu.VMEM((LANES, self.tile), f32), total, total]

    def backward_other(self, joint, other, grad, context, lse):
        size, length = self.block_len, other.shape[1]
        return self.call(
            functools.partial(grad_kernel, own=False),
            SHORT,
            [self.queries(), self.keys(length, 0), self.keys(length, 1)]
            + [self.queries(), self.queries(), self.stat(), self.row_starts()],
            [self.turned(), self.keys(length, 0), self.keys(length, 0)],
            [
                jax.ShapeDtypeStruct((self.rows, self.width, size), f32),
                self.shape(length),
                self.shape(length),
            ],
            self.grad_scratch(length),
            (joint, other, other, grad, context, lse, self.start_row),
        )

    def backward_own(self, joint, grad, context, lse, dq_state):
        size = self.block_len
        return self.call(
            functools.partial(grad_kernel, own=True),
            LONG,
            [self.queries(), self.keys(size, 1), self.keys(size, 2)]
            + [self.queries(), self.queries(), self.stat(), self.row_starts(), self.turned()],
            [self.queries(), self.keys(size, 0), self.keys(size, 0)],
            [self.shape(size)] * 3,
            self.grad_scratch(size),
            (joint, joint, joint, grad, context, lse, self.start_row, dq_state),
        )


def place_kernel(target_ref, x_ref, out_ref):
    tile = out_ref.shape[0]
    slots = lax.broadcasted_iota(jnp.int32, (tile, target_ref.shape[1]), 0) + pl.program_id(0) * tile
    picked = jnp.where(slots == target_ref[...], 1.0, 0.0).astype(bf16)
    out_ref[...] = dot(picked, x_ref[...]).astype(bf16)


def place(target_row, x, slots):
    flat, width = x.shape
    tile = tile_of(slots, 256)
    return pl.pallas_call(
        place_kernel,
        grid=(slots // tile,),
        in_specs=[pl.BlockSpec((1, flat), lambda i: (0, 0)), pl.BlockSpec((flat, width), lambda i: (0, 0))],
        out_specs=pl.BlockSpec((tile, width), lambda i: (i, 0)),
        out_shape=jax.ShapeDtypeStruct((slots, width), bf16),
        compiler_params=params(),
        cost_estimate=SHORT,
    )(target_row, x)


def column_of(row):
    return jnp.broadcast_to(row.astype(f32), (8, row.shape[1])).T[:, :1].astype(jnp.int32)


def fetched(target, sources):
    total, before = 0.0, 0
    for source in sources:
        slots = lax.broadcasted_iota(jnp.int32, (target.shape[0], source.shape[0]), 1) + before
        total += dot(jnp.where(slots == target, 1.0, 0.0).astype(bf16), source[...])
        before += source.shape[0]
    return total


def result_kernel(target_ref, middle_ref, gate_ref, *refs):
    branch = fetched(column_of(target_ref[...]), refs[:-1])
    refs[-1][...] = (middle_ref[...] + gate_ref[...] * branch).astype(bf16)


def unit_of(x):
    center = x - jnp.mean(x, -1, keepdims=True)
    rate = lax.rsqrt(jnp.mean(center * center, -1, keepdims=True) + 1e-05)
    return center * rate, rate


def norm_back(grad, gain, unit, rate):
    scaled = grad * gain
    mean_one = jnp.mean(scaled, -1, keepdims=True)
    mean_two = jnp.mean(scaled * unit, -1, keepdims=True)
    return rate * (scaled - mean_one - unit * mean_two)


def add_sums(sums_ref, grad, unit):
    @pl.when(pl.program_id(0) == 0)
    def clear():
        sums_ref[...] = jnp.zeros_like(sums_ref)

    sums_ref[0:1] += jnp.sum(grad * unit, 0, keepdims=True)
    sums_ref[1:2] += jnp.sum(grad, 0, keepdims=True)


def second_norm_grad_kernel(target_ref, middle_ref, upstream_ref, gain_ref, weight_ref, *refs):
    sources = refs[:-4]
    grad_ref, low_ref, context_ref, sums_ref = refs[-4:]
    grad = fetched(column_of(target_ref[...]), sources)
    unit, rate = unit_of(middle_ref[...])
    add_sums(sums_ref, grad, unit)
    total = upstream_ref[...].astype(f32) + norm_back(grad, gain_ref[...], unit, rate)
    grad_ref[...] = total
    low = total.astype(bf16)
    low_ref[...] = low
    context_ref[...] = dot_nt(low, weight_ref[...]).astype(bf16)


def input_grad_kernel(tokens_ref, *refs):
    grad_ref, sums_ref = refs[-2:]
    count = (len(refs) - 2) // 2
    grad = 0.0
    for part, weight in zip(refs[:count], refs[count : 2 * count]):
        grad += dot_nt(part[...], weight[...])
    unit, _ = unit_of(tokens_ref[...].astype(f32))
    add_sums(sums_ref, grad, unit)
    grad_ref[...] = grad.astype(grad_ref.dtype)


def joint_kernel(tokens_ref, gain_ref, shift_ref, *refs):
    weights, (normed_ref, joint_ref) = refs[:-2], refs[-2:]
    normed = unit_of(tokens_ref[...].astype(f32))[0] * gain_ref[...] + shift_ref[...]
    normed = normed.astype(bf16)
    normed_ref[...] = normed
    width = normed.shape[1]
    for at, weight in enumerate(weights):
        joint_ref[:, at * width : (at + 1) * width] = dot(normed, weight[...]).astype(bf16)


def middle_kernel(context_ref, tokens_ref, route_ref, weight_ref, gain_ref, shift_ref, centroid_ref, middle_ref, normed_ref, gate_ref):
    middle = tokens_ref[...].astype(f32) + dot(context_ref[...], weight_ref[...])
    middle_ref[...] = middle
    normed = unit_of(middle)[0] * gain_ref[...] + shift_ref[...]
    normed_ref[...] = normed.astype(bf16)
    experts = centroid_ref.shape[0]
    route = column_of(route_ref[...])
    picked = route == lax.broadcasted_iota(jnp.int32, (route.shape[0], experts), 1)
    chosen = jnp.dot(
        picked.astype(f32), centroid_ref[...], precision=lax.Precision.HIGHEST, preferred_element_type=f32
    )
    gate_ref[...] = jax.nn.sigmoid(jnp.sum(normed * chosen, -1, keepdims=True))


def turned(x):
    size = tile_of(x.shape[1], 256)
    same = lax.broadcasted_iota(jnp.int32, (size, size), 0) == lax.broadcasted_iota(jnp.int32, (size, size), 1)
    unit = jnp.where(same, 1.0, 0.0).astype(bf16)
    return jnp.concatenate(
        [dot_nt(unit, x[:, at : at + size]).astype(bf16) for at in range(0, x.shape[1], size)], 0
    )


def weight_grad_kernel(*refs, count, into):
    lefts, rights = refs[:count], refs[count : 2 * count]
    out_ref = refs[2 * count + (1 if into else 0)]
    turns = refs[-count:]

    @pl.when(pl.program_id(0) == 0)
    def turn():
        for left, turn_ref in zip(lefts, turns):
            turn_ref[...] = turned(left[...])

    out_ref[...] = sum(dot(turn_ref[...], right[...]) for turn_ref, right in zip(turns, rights)).astype(bf16)


def weight_grad(pairs, columns, offset, into):
    width, wide = pairs[0][0].shape[1], pairs[0][1].shape[1]
    tile = tile_of(wide, 256)
    lefts, rights = [a for a, _ in pairs], [b for _, b in pairs]
    specs = [pl.BlockSpec(a.shape, lambda i: (0, 0), pipeline_mode=pl.Buffered(1)) for a in lefts]
    specs += [pl.BlockSpec((b.shape[0], tile), lambda i: (0, i)) for b in rights]
    arrays, aliases = lefts + rights, {}
    if into is not None:
        aliases = {len(arrays): 0}
        specs.append(pl.BlockSpec(memory_space=pl.ANY))
        arrays.append(into)
    return pl.pallas_call(
        functools.partial(weight_grad_kernel, count=len(pairs), into=into is not None),
        grid=(wide // tile,),
        in_specs=specs,
        out_specs=pl.BlockSpec((width, tile), lambda i: (0, offset // tile + i)),
        out_shape=jax.ShapeDtypeStruct((width, columns), bf16),
        scratch_shapes=[pltpu.VMEM((width, a.shape[0]), bf16) for a in lefts],
        input_output_aliases=aliases,
        compiler_params=params(),
        cost_estimate=SHORT,
    )(*arrays)


def sums_kernel(first_ref, other_ref, second_ref, into_ref, out_ref):
    rows = jnp.concatenate([first_ref[...] + other_ref[...], second_ref[...]], 0)
    rows = jnp.concatenate([rows, jnp.zeros((124, rows.shape[1]), f32)], 0)
    out_ref[...] = rows.T.astype(bf16)


def put_sums(first, other, second, into):
    width, columns = into.shape
    spec = pl.BlockSpec((2, width), lambda i: (0, 0))
    return pl.pallas_call(
        sums_kernel,
        grid=(1,),
        in_specs=[spec, spec, spec, pl.BlockSpec(memory_space=pl.ANY)],
        out_specs=pl.BlockSpec((width, 128), lambda i: (0, columns // 128 - 1)),
        out_shape=jax.ShapeDtypeStruct(into.shape, bf16),
        input_output_aliases={3: 0},
        compiler_params=params(),
        cost_estimate=SHORT,
    )(first, other, second, into)


def by_tokens(kernel, flat, tiled, whole, out_shape):
    tile = tile_of(flat, 256)

    def cut(array):
        if array.shape == (1, flat):
            return pl.BlockSpec((1, tile), lambda i: (0, i))
        if array.shape[0] == flat:
            return pl.BlockSpec((tile, array.shape[1]), lambda i: (i, 0))
        return pl.BlockSpec(array.shape, lambda i: (0, 0))

    specs = [cut(array) for array in tiled]
    for array, column in whole:
        if column is None:
            specs.append(pl.BlockSpec(array.shape, lambda i: (0, 0), pipeline_mode=pl.Buffered(1)))
        else:
            shape = (array.shape[0], array.shape[0])
            specs.append(pl.BlockSpec(shape, lambda i, c=column: (0, c), pipeline_mode=pl.Buffered(1)))
    arrays = list(tiled) + [array for array, _ in whole]
    return pl.pallas_call(
        kernel,
        grid=(flat // tile,),
        in_specs=specs,
        out_specs=[cut(shape) for shape in out_shape],
        out_shape=out_shape,
        compiler_params=params(),
        cost_estimate=SHORT,
    )(*arrays)


def expert_kernel(*refs):
    x_ref, g_ref, up_ref, down_ref, cent_ref = refs[:5]
    out_ref, dx_ref, act_ref, pre_ref, pg_ref = refs[-5:]
    x = x_ref[...]
    g = g_ref[...].reshape(x.shape).astype(f32)
    centroid = cent_ref[...]
    gate = jax.nn.sigmoid(jnp.sum(x.astype(f32) * centroid, -1, keepdims=True))
    produced_grad = (gate * g).astype(bf16)
    pg_ref[...] = produced_grad
    pre = dot(x, up_ref[...])
    cumulative = 0.5 + 0.5 * lax.erf(pre * (0.5**0.5))
    act = (pre * cumulative).astype(bf16)
    slope = cumulative + pre * (jnp.exp(-0.5 * pre * pre) * 0.3989422804014327)
    act_ref[...] = act
    pre_grad = (dot_nt(produced_grad, down_ref[...]) * slope).astype(bf16)
    pre_ref[...] = pre_grad
    produced = dot(act, down_ref[...]).astype(bf16)
    out_ref[...] = produced.reshape(out_ref.shape)
    gate_grad = jnp.sum(g * produced.astype(f32), -1, keepdims=True)
    logit_grad = gate_grad * gate * (1.0 - gate)
    dx_ref[...] = (dot_nt(pre_grad, up_ref[...]) + logit_grad * centroid).astype(bf16)


def run_expert(x, g, half, up, down, centroid, outputs):
    rows, width = x.shape
    peers, halves, depth, _ = g.shape
    hidden = up.shape[1]
    tile = depth * tile_of(peers, max(1, 256 // depth))
    by_row = pl.BlockSpec((tile, width), lambda i: (i, 0))
    by_hidden = pl.BlockSpec((tile, hidden), lambda i: (i, 0))
    by_peer = pl.BlockSpec((tile // depth, 1, depth, width), lambda i: (i, half, 0, 0))

    def whole(shape):
        return pl.BlockSpec(shape, lambda i: (0, 0), pipeline_mode=pl.Buffered(1))

    in_specs = [by_row, by_peer, whole((width, hidden)), whole((hidden, width)), whole((1, width))]
    arrays = [x, g, up, down, centroid]
    aliases = {}
    if outputs is not None:
        in_specs.append(pl.BlockSpec(memory_space=pl.ANY))
        arrays.append(outputs)
        aliases = {5: 0}
    row_shape = jax.ShapeDtypeStruct((rows, width), bf16)
    hidden_shape = jax.ShapeDtypeStruct((rows, hidden), bf16)
    return pl.pallas_call(
        expert_kernel,
        grid=(rows // tile,),
        in_specs=in_specs,
        out_specs=[by_peer, by_row, by_hidden, by_hidden, by_row],
        out_shape=[jax.ShapeDtypeStruct(g.shape, bf16), row_shape, hidden_shape, hidden_shape, row_shape],
        input_output_aliases=aliases,
        compiler_params=params(),
        cost_estimate=SHORT,
    )(*arrays)


def stages_of(wide, blocks):
    def bits(low, high):
        found = []
        while low < high:
            found.append(low)
            low *= 2
        return found

    stages = (bits(1, min(2, wide)), bits(2, min(4, wide)) + bits(wide, wide * blocks), bits(4, wide))
    return [stage for stage in stages if stage]


def spread(code, bits):
    return sum(bit for i, bit in enumerate(bits) if code >> i & 1)


def swap(array, mask):
    total = lax.axis_size("blk") * lax.axis_size("wide")
    return lax.ppermute(array, ("blk", "wide"), [(i, i ^ mask) for i in range(total)])


def places_of(stages):
    me = lax.axis_index("blk") * lax.axis_size("wide") + lax.axis_index("wide")
    return [sum((me // bit % 2) << i for i, bit in enumerate(bits)) for bits in stages]


def reduce_step(parts, bits, code):
    count = 1 << len(bits)
    summed = []
    for x in parts:
        rows = x.shape[0] // count

        def piece(index):
            return lax.dynamic_slice_in_dim(x, index * rows, rows, 0)

        got = [swap(piece(code ^ other).astype(bf16), spread(other, bits)) for other in range(1, count)]
        total = piece(code).astype(f32)
        for part in got:
            total = total + part.astype(f32)
        summed.append(total)
    return summed


def gather_parts(parts):
    stages = stages_of(lax.axis_size("wide"), lax.axis_size("blk"))
    for bits, code in reversed(list(zip(stages, places_of(stages)))):
        gathered = []
        for x in parts:
            rows = x.shape[0]
            whole = jnp.zeros((rows << len(bits), x.shape[1]), bf16)
            whole = lax.dynamic_update_slice_in_dim(whole, x, code * rows, 0)
            for other in range(1, 1 << len(bits)):
                part = swap(x, spread(other, bits))
                whole = lax.dynamic_update_slice_in_dim(whole, part, (code ^ other) * rows, 0)
            gathered.append(whole)
        parts = gathered
    return parts


def body(
    tokens,
    segments,
    routes,
    project_in,
    project_out,
    first_gain,
    first_shift,
    second_gain,
    second_shift,
    centroids,
    expert_up,
    expert_down,
    cotangent,
):
    rows, block_len, width = tokens.shape
    blocks = lax.axis_size("blk")
    me = lax.axis_index("blk")
    flat = rows * block_len
    experts = centroids.shape[0]
    local_experts = expert_up.shape[0]
    peers = experts // local_experts
    capacity = 2 * block_len // experts
    halves = 2 if capacity % 16 == 0 else 1
    depth = capacity // halves
    half_slots = experts * rows * depth

    shifts = range(1, blocks)

    def ahead(array, shift):
        return lax.ppermute(array, "blk", [(i, i + shift) for i in range(blocks - shift)])

    def behind(array, shift):
        return lax.ppermute(array, "blk", [(i + shift, i) for i in range(blocks - shift)])

    other_tokens = jnp.concatenate([ahead(tokens, shift) for shift in shifts], 1)
    other_flat = other_tokens.reshape(-1, width)

    route_ids = routes[:, :, 0]
    picked = route_ids[:, :, None] == lax.iota(jnp.int32, experts)[None, None, :]
    places = lax.iota(jnp.int32, block_len)
    before = (places[None, :] <= places[:, None]).astype(bf16)
    ranks = jnp.einsum("qk,rke->rqe", before, picked.astype(bf16), preferred_element_type=f32)
    slot_index = jnp.sum(jnp.where(picked, ranks, 0.0), 2).astype(jnp.int32) - 1
    row_index = lax.iota(jnp.int32, rows)[:, None]
    half = slot_index // depth
    place_in_half = row_index * depth + slot_index - half * depth
    target_halves = half * half_slots + route_ids * (rows * depth) + place_in_half
    target_whole = (route_ids * halves + half) * (rows * depth) + place_in_half

    def exchange(array):
        return lax.all_to_all(
            array.reshape(experts, -1, width), "wide", split_axis=0, concat_axis=0, tiled=True
        )

    upstream = cotangent.reshape(flat, width)

    own_segments = lax.dynamic_slice_in_dim(segments, me * block_len, block_len, 1)
    smaller = segments[:, None, :] < own_segments[:, :, None]
    starts = jnp.sum(smaller.astype(jnp.int32), 2)
    attention = Attention(me, starts, rows, block_len, width)

    tokens_flat = tokens.reshape(flat, width)

    first_gain_row, first_shift_row = first_gain.reshape(1, width), first_shift.reshape(1, width)

    def joined(x, columns):
        count = len(columns)
        return by_tokens(
            joint_kernel,
            x.shape[0],
            (x,),
            [(first_gain_row, None), (first_shift_row, None)] + [(project_in, column) for column in columns],
            [
                jax.ShapeDtypeStruct(x.shape, bf16),
                jax.ShapeDtypeStruct((x.shape[0], count * width), bf16),
            ],
        )

    normed_one, joint = joined(tokens_flat, (0, 1, 2))
    route_row = routes.reshape(1, flat)
    target_halves_row, target_whole_row = target_halves.reshape(1, flat), target_whole.reshape(1, flat)
    second_gain_row, second_shift_row = second_gain.reshape(1, width), second_shift.reshape(1, width)
    small = (attention.low, attention.start_row, route_row, target_halves_row, target_whole_row)
    small += (first_gain_row, first_shift_row, second_gain_row, second_shift_row)
    joint, small, to_place = lax.optimization_barrier((joint, small, upstream))
    attention.low, attention.start_row, route_row, target_halves_row, target_whole_row = small[:5]
    first_gain_row, first_shift_row, second_gain_row, second_shift_row = small[5:]
    grads_arrived = exchange(place(target_whole_row, to_place, halves * half_slots))
    grads_arrived = grads_arrived.reshape(peers, local_experts, halves, rows * depth, width)
    joint = joint.reshape(rows, block_len, 3 * width)
    normed_other, other = joined(other_flat, (1, 2))
    other = other.reshape(rows, (blocks - 1) * block_len, 2 * width)
    context, lse = attention.forward(joint, other)
    context_flat = context.reshape(flat, width)

    wide_shape = jax.ShapeDtypeStruct((flat, width), f32)
    low_shape = jax.ShapeDtypeStruct((flat, width), bf16)
    sums_shape = jax.ShapeDtypeStruct((2, width), f32)
    middle, normed_two, gate = by_tokens(
        middle_kernel,
        flat,
        (context_flat, tokens_flat, route_row),
        [(project_out, None), (second_gain_row, None), (second_shift_row, None), (centroids, None)],
        [wide_shape, low_shape, jax.ShapeDtypeStruct((flat, 1), f32)],
    )
    normed_two, grads_arrived = lax.optimization_barrier((normed_two, grads_arrived))
    placed = place(target_halves_row, normed_two, halves * half_slots)
    placed = placed.reshape(halves, half_slots, width)
    arrived = [exchange(placed[h]).reshape(peers, local_experts, rows * depth, width) for h in range(halves)]

    own_experts = lax.axis_index("wide") * local_experts
    outputs, row_grads = [None] * local_experts, []
    down_pairs, up_pairs = [[] for _ in range(local_experts)], [[] for _ in range(local_experts)]
    for h in range(halves):
        half_dx = []
        for local in range(local_experts):
            x = arrived[h][:, local].reshape(-1, width)
            centroid = lax.dynamic_slice_in_dim(centroids, own_experts + local, 1, 0)
            outputs[local], dx, act, pre_grad, out_grad = run_expert(
                x, grads_arrived[:, local], h, expert_up[local], expert_down[local], centroid, outputs[local]
            )
            half_dx.append(dx.reshape(peers, 1, rows * depth, width))
            down_pairs[local].append((act, out_grad))
            up_pairs[local].append((x, pre_grad))
        row_grads.append(half_dx[0] if local_experts == 1 else jnp.concatenate(half_dx, 1))
    share = expert_up.shape[2] // blocks

    def share_of(array, block):
        return lax.dynamic_slice_in_dim(array, block * share, share, 1)

    def down_product(pairs, block):
        return sum(
            jnp.einsum("cf,cd->fd", share_of(act, block), out_grad, preferred_element_type=f32)
            for act, out_grad in pairs
        )

    def up_product(pairs, block):
        return sum(
            jnp.einsum("cd,cf->df", x, share_of(pre_grad, block), preferred_element_type=f32)
            for x, pre_grad in pairs
        )

    def product_shares(pairs, product):
        sent = [[product(pair, lax.rem(me + shift, blocks)).astype(bf16) for shift in shifts] for pair in pairs]
        return sent, [product(pair, me) for pair in pairs]

    def send_shares(sent):
        return [
            [
                lax.ppermute(part, "blk", [(i, (i + shift) % blocks) for i in range(blocks)])
                for shift, part in zip(shifts, parts)
            ]
            for parts in sent
        ]

    def summed_shares(own, got):
        totals = []
        for total, parts in zip(own, got):
            for part in parts:
                total = total + part.astype(f32)
            totals.append(total)
        return jnp.stack(totals, 0)

    back_arrived = [exchange(part).reshape(half_slots, width) for part in row_grads]
    back_arrived[0], down_pairs, up_pairs = lax.optimization_barrier((back_arrived[0], down_pairs, up_pairs))
    down_sent, down_own = product_shares(down_pairs, down_product)
    up_sent, up_own = product_shares(up_pairs, up_product)
    down_got, up_got = send_shares(down_sent), send_shares(up_sent)
    output = outputs[0][:, None] if local_experts == 1 else jnp.stack(outputs, 1)
    back_arrived, down_own, up_own, _, _ = lax.optimization_barrier(
        (back_arrived, down_own, up_own, down_sent, up_sent)
    )

    middle_grad, attn_grad, context_grad, second_sums = by_tokens(
        second_norm_grad_kernel,
        flat,
        (target_halves_row, middle, upstream),
        [(second_gain_row, None), (project_out, None)] + [(part, None) for part in back_arrived],
        [wide_shape, low_shape, low_shape, sums_shape],
    )
    context_grad, output = lax.optimization_barrier((context_grad, output))
    produced = exchange(output).reshape(halves * half_slots, width)
    context_grad = context_grad.reshape(rows, block_len, width)
    dq_state, dk_other, dv_other = attention.backward_other(joint, other, context_grad, context, lse)
    dk_other, dv_other = dk_other.reshape(-1, width), dv_other.reshape(-1, width)
    other_len = other_flat.shape[0]
    other_grad, other_sums = by_tokens(
        input_grad_kernel,
        other_len,
        (other_flat, dk_other, dv_other),
        [(project_in, 1), (project_in, 2)],
        [jax.ShapeDtypeStruct((other_len, width), bf16), sums_shape],
    )
    other_grad = other_grad.reshape(rows, blocks - 1, block_len, width)
    context_grad, returned, down_got = lax.optimization_barrier((context_grad, other_grad, down_got))
    returned = [behind(returned[:, shift - 1], shift) for shift in shifts]
    dq, dk, dv = attention.backward_own(joint, context_grad, context, lse, dq_state)
    dq, dk, dv = [part.reshape(flat, width) for part in (dq, dk, dv)]
    dq, dk, dv, produced, down_got, up_got = lax.optimization_barrier((dq, dk, dv, produced, down_got, up_got))

    kv_grad = weight_grad([(normed_one, dk), (normed_other, dk_other)], 2 * width, 0, None)
    kv_grad = weight_grad([(normed_one, dv), (normed_other, dv_other)], 2 * width, width, kv_grad)
    columns = 2 * width + 128
    rest_grad = weight_grad([(context_flat, attn_grad)], columns, width, None)
    rest_grad = weight_grad([(normed_one, dq)], columns, 0, rest_grad)
    own_grad, own_sums = by_tokens(
        input_grad_kernel,
        flat,
        (tokens_flat, dq, dk, dv),
        [(project_in, 0), (project_in, 1), (project_in, 2)],
        [wide_shape, sums_shape],
    )

    rest_grad = put_sums(own_sums, other_sums, second_sums, rest_grad)
    rest_grad, returned = lax.optimization_barrier((rest_grad, returned))
    shares = [kv_grad, rest_grad]
    stages = stages_of(lax.axis_size("wide"), blocks)
    for number, (bits, code) in enumerate(zip(stages, places_of(stages))):
        shares = reduce_step(shares, bits, code)
        if number == 0:
            late = (down_own, up_own, down_got, up_got, middle, produced, own_grad, returned)
            late, shares = lax.optimization_barrier((late, shares))
            down_own, up_own, down_got, up_got, middle, produced, own_grad, returned = late
    shares = [x.astype(bf16) for x in shares]

    down_share = summed_shares(down_own, down_got)
    up_share = summed_shares(up_own, up_got)
    total_grad = own_grad
    for part in returned:
        total_grad = total_grad + part.reshape(flat, width).astype(f32)
    unit_one, rate_one = unit_of(tokens_flat.astype(f32))
    stream_grad = middle_grad + norm_back(total_grad, first_gain, unit_one, rate_one)
    (result,) = by_tokens(
        result_kernel,
        flat,
        (target_whole_row, middle, gate),
        [(produced, None)],
        [low_shape],
    )
    down_share, up_share, stream_grad, result, shares = lax.optimization_barrier(
        (down_share, up_share, stream_grad, result, shares)
    )
    kv_sum, q_sum = [part.astype(f32) for part in gather_parts(shares)]

    out_shape = (rows, block_len, width)
    return (
        result.reshape(out_shape),
        stream_grad.reshape(out_shape),
        jnp.concatenate([q_sum[:, :width], kv_sum], 1),
        q_sum[:, width : 2 * width],
        q_sum[:, 2 * width],
        q_sum[:, 2 * width + 1],
        q_sum[:, 2 * width + 2],
        q_sum[:, 2 * width + 3],
        up_share,
        down_share,
    )


def solution(mesh):
    return jax.shard_map(
        body,
        mesh=mesh,
        in_specs=(
            P("wide", "blk", None),
            P("wide", None),
            P("wide", "blk", None),
            P(),
            P(),
            P(),
            P(),
            P(),
            P(),
            P(),
            P("wide", None, None),
            P("wide", None, None),
            P("wide", "blk", None),
        ),
        out_specs=(
            P("wide", "blk", None),
            P("wide", "blk", None),
            P(),
            P(),
            P(),
            P(),
            P(),
            P(),
            P("wide", None, "blk"),
            P("wide", "blk", None),
        ),
        check_vma=False,
    )
```

time: 1620 us -> 553 us (0.34)
  waiting for transfers between devices: 645 us -> 54.9 us
  matrix products: 474 us -> 34.9 us
  Pallas kernels: 0 us -> 243 us
  blocking collectives: 203 us -> 51.4 us
  local copies, waits for them, and re-layouts: 144 us -> 22.9 us
  starting transfers between devices: 11.2 us -> 107 us
  other arithmetic: 105 us -> 31 us
    dot_general x22 -> x9, matrix products: 474 us -> 34.9 us  [the longest x4 18.3 us: down_product(): jnp.einsum('cf,cd->fd', share_of(act, block), out_grad, preferred_element...]
    reduce_scatter x3 -> x0, waiting for transfers between devices: 341 us -> none  [the longest x1 233 us: body(): lax.psum_scatter(key_terms.astype(jnp.bfloat16), 'blk', scatter_dimension...]
    pallas_call x0 -> x19, Pallas kernels: none -> 243 us  [the longest x3 82.7 us: call(): pl.pallas_call(functools.partial(kernel, tile=self.tile, block_len=self.b...]
    psum x1 -> x0, waiting for transfers between devices: 130 us -> none  [body(): lax.psum((in_proj_grad, out_proj_grad, gain_one_grad, shift_one_grad, gai...]
    all_to_all x2 -> x1, blocking collectives: 161 us -> 51.4 us  [exchange(): lax.all_to_all(array.reshape(experts, -1, width), 'wide', split_axis=0, c...]
    all_to_all x2 -> x5, waiting for transfers between devices: 116 us -> 17 us  [exchange(): lax.all_to_all(array.reshape(experts, -1, width), 'wide', split_axis=0, c...]
    ppermute x0 -> x32, starting transfers between devices: none -> 71.7 us  [the longest x28 62.5 us: swap(): lax.ppermute(array, ('blk', 'wide'), [(i, i ^ mask) for i in range(total)])]
    all_gather x1 -> x0, waiting for transfers between devices: 58.7 us -> none  [body(): gathered = lax.all_gather(keyvals, 'blk', axis=1, tiled=True)]
  transfers between devices with their start and end apart: 7 -> 37, of which waited for: 7 -> 17; matrix products, arithmetic and copies ran while one was open for 10% -> 14% of each run, Pallas kernels for 0% -> 43%
where the time goes in v1:
time: 553 us; the launch traced here: 547 us
  Pallas kernels  243 us (44%)
  starting transfers between devices  107 us (19%)
  waiting for transfers between devices  54.9 us (10%)
  blocking collectives  51.4 us (9%)
  matrix products  34.9 us (6%)
  other arithmetic  31 us (6%)
  local copies, waits for them, and re-layouts  22.9 us (4%)
    pallas_call x3, Pallas kernels, call(): pl.pallas_call(functools.partial(kernel, tile=self.tile, block_len=self.b...  82.7 us
    ppermute x28, starting transfers between devices, swap(): lax.ppermute(array, ('blk', 'wide'), [(i, i ^ mask) for i in range(total)])  62.5 us
    pallas_call x7, Pallas kernels, by_tokens(): pl.pallas_call(kernel, grid=(flat // tile,), in_specs=specs, out_specs=[c...  61.6 us
    pallas_call x2, Pallas kernels, run_expert(): pl.pallas_call(expert_kernel, grid=(rows // tile,), in_specs=in_specs, ou...  54.7 us
    all_to_all x1, blocking collectives, exchange(): lax.all_to_all(array.reshape(experts, -1, width), 'wide', split_axis=0, c...  51.4 us
    all_to_all x5, starting transfers between devices, exchange(): lax.all_to_all(array.reshape(experts, -1, width), 'wide', split_axis=0, c...  35.7 us
    ppermute x28, waiting for transfers between devices, swap(): lax.ppermute(array, ('blk', 'wide'), [(i, i ^ mask) for i in range(total)])  34.2 us
    pallas_call x4, Pallas kernels, weight_grad(): pl.pallas_call(functools.partial(weight_grad_kernel, count=len(pairs), in...  26.4 us
  transfers between devices with their start and end apart: 37, of which 17 were waited for; matrix products, arithmetic and copies ran while one was open for 14% of the time, Pallas kernels for 43%

profile of v1, /device:TPU:0, one launch (start us, length us, event | category | flops | bytes accessed | tf_op | source)
XLA Modules:
  0.0 546.8 jit_solution(8223278986265504659)
XLA Ops:
  0.6 6.0 %collective-permute-start = (bf16[1,1024,768]{2,1,0:T(8,128)(2,1)}, bf16[1,1024,768]{2,1,0:T(8,128)(2,1)}, u32[]{:S(2)}, u32[]{:S(2)}) collective-permute-start(bf16[1,1024,768]{2,1,0:T(8,128)(2,1)} %param.13), channel_id=1, source_target_pairs={{0,16},{1,17},{2,18},{3,19},{4,20},{5,21},{6,22},{7,23},{8,24},{9,... | collective-permute-start | bytes 4718600 | tf_op jit(solution)/shard_map/ppermute | solution.py:694
  9.2 8.5 %shard_map.204 = (bf16[1024,768]{1,0:T(8,128)(2,1)}, bf16[1024,2304]{1,0:T(8,128)(2,1)}) custom-call(bf16[1024,768]{1,0:T(8,128)(2,1)} %bitcast.75, f32[1,768]{1,0:T(1,128)} %reshape.385.gain_ref, f32[1,768]{1,0:T(1,128)} %reshape.386.shift_ref, bf16[768,2304]{1,0:T(8,128)(2,1)} %refs_5_.1, bf16[768,2304]{1,0:T(8,128)(2,1)} %refs_5_.1, bf16[768,2304]{1,0:T(8,128)(2,1)} %refs_5_.1), custom_call_target="tpu_custom_call" | custom-call | flops 1 | bytes 1 | tf_op jit(solution)/shard_map/pallas_call | solution.py:538
  22.5 7.3 %shard_map.208 = bf16[2048,768]{1,0:T(8,128)(2,1)} custom-call(s32[1,1024]{1,0:T(1,128)} %get-tuple-element.111.target_ref, bf16[1024,768]{1,0:T(8,128)(2,1)} %bitcast.95), custom_call_target="tpu_custom_call" | custom-call | flops 1 | bytes 1 | tf_op jit(solution)/shard_map/pallas_call | solution.py:354
  39.4 7.1 %shard_map.205 = (bf16[1024,768]{1,0:T(8,128)(2,1)}, bf16[1024,1536]{1,0:T(8,128)(2,1)}) custom-call(bf16[1024,768]{1,0:T(8,128)(2,1)} %bitcast.13.tokens_ref, f32[1,768]{1,0:T(1,128)} %reshape.385.gain_ref, f32[1,768]{1,0:T(1,128)} %reshape.386.shift_ref, bf16[768,2304]{1,0:T(8,128)(2,1)} %refs_5_.1, bf16[768,2304]{1,0:T(8,128)(2,1)} %refs_5_.1), custom_call_target="tpu_custom_call" | custom-call | flops 1 | bytes 1 | tf_op jit(solution)/shard_map/pallas_call | solution.py:538
  46.6 33.0 %shard_map.206 = (bf16[1,1024,768]{2,1,0:T(8,128)(2,1)}, f32[1,3,4,1024]{3,2,1,0:T(4,128)}) custom-call(s32[1]{0:T(128)} %bitcast.11.me_ref, s32[1,2]{1,0:T(1,128)} %slice.29.low_ref, bf16[1,1024,2304]{2,1,0:T(8,128)(2,1)} %bitcast.113, bf16[1,1024,2304]{2,1,0:T(8,128)(2,1)} %bitcast.114, bf16[1,1024,2304]{2,1,0:T(8,128)(2,1)} %bitcast.115, ...), custom_call_target="tpu_custom_call" | custom-call | flops 99999997952 | bytes 1 | tf_op jit(solution)/shard_map/pallas_call | solution.py:277
  79.6 7.5 %shard_map.207 = (f32[1024,768]{1,0:T(8,128)}, bf16[1024,768]{1,0:T(8,128)(2,1)}, f32[1024,1]{1,0:T(8,128)}) custom-call(bf16[1024,768]{1,0:T(8,128)(2,1)} %bitcast.84, bf16[1024,768]{1,0:T(8,128)(2,1)} %bitcast.76, s32[1,1024]{1,0:T(1,128)} %bitcast.132, bf16[768,768]{1,0:T(8,128)(2,1)} %weight_ref.3, f32[1,768]{1,0:T(1,128)} %reshape.389.gain_ref, ...), custom_call_target="tpu_custom_call" | custom-call | flops 1 | bytes 1 | tf_op jit(solution)/shard_map/pallas_call | solution.py:538
  87.1 8.0 %all-to-all-done = bf16[16,128,768]{2,1,0:T(8,128)(2,1)S(1)} async-done(((bf16[16,128,768]{2,1,0:T(8,128)(2,1)}), bf16[16,128,768]{2,1,0:T(8,128)(2,1)S(1)}, u32[]{:S(2)}, u32[]{:S(2)}) %all-to-all-start) | async-done | bytes 3145760 | tf_op jit(solution)/shard_map/all_to_all | solution.py:715
  95.2 8.4 %shard_map.209 = bf16[2048,768]{1,0:T(8,128)(2,1)} custom-call(s32[1,1024]{1,0:T(1,128)} %add_add_fusion.target_ref, bf16[1024,768]{1,0:T(8,128)(2,1)} %get-tuple-element.113.x_ref), custom_call_target="tpu_custom_call" | custom-call | flops 1 | bytes 1 | tf_op jit(solution)/shard_map/pallas_call | solution.py:354
  106.8 51.4 %all_to_all.30 = bf16[16,64,768]{2,1,0:T(8,128)(2,1)} all-to-all(bf16[16,64,768]{2,1,0:T(8,128)(2,1)S(1)} %bitcast.99), channel_id=1, replica_groups=mesh['blk'=2,'wide'=16] {'wide'}, dimensions={0} | all-to-all | bytes 3145728 | tf_op jit(solution)/shard_map/all_to_all | solution.py:715
  164.6 27.3 %shard_map.210 = (bf16[16,2,64,768]{3,2,1,0:T(8,128)(2,1)}, bf16[1024,768]{1,0:T(8,128)(2,1)}, bf16[1024,3072]{1,0:T(8,128)(2,1)}, bf16[1024,3072]{1,0:T(8,128)(2,1)}, bf16[1024,768]{1,0:T(8,128)(2,1)}) custom-call(bf16[1024,768]{1,0:T(8,128)(2,1)} %bitcast.106, bf16[16,2,64,768]{3,2,1,0:T(8,128)(2,1)} %bitcast.78, bf16[768,3072]{1,0:T(8,128)(2,1)} %bitcast.80, ...), custom_call_target="tpu_custom_call" | custom-call | flops 1 | bytes 1 | tf_op jit(solution)/shard_map/pallas_call | solution.py:593
  195.2 9.1 %all-to-all-start.2 = ((bf16[16,64,768]{2,1,0:T(8,128)(2,1)}), bf16[16,64,768]{2,1,0:T(8,128)(2,1)S(1)}, u32[]{:S(2)}, u32[]{:S(2)}) async-start(bf16[16,64,768]{2,1,0:T(8,128)(2,1)} %bitcast.125), calls=%async_computation.2 | async-start | bytes 3145728 | tf_op jit(solution)/shard_map/all_to_all | solution.py:715
  204.4 27.4 %shard_map.211 = (bf16[16,2,64,768]{3,2,1,0:T(8,128)(2,1)}, bf16[1024,768]{1,0:T(8,128)(2,1)}, bf16[1024,3072]{1,0:T(8,128)(2,1)}, bf16[1024,3072]{1,0:T(8,128)(2,1)}, bf16[1024,768]{1,0:T(8,128)(2,1)}) custom-call(bf16[1024,768]{1,0:T(8,128)(2,1)} %bitcast.86, bf16[16,2,64,768]{3,2,1,0:T(8,128)(2,1)} %bitcast.79, ...), custom_call_target="tpu_custom_call", output_to_operand_aliasing={{0}: (5, {})} | custom-call | flops 1 | bytes 1 | tf_op jit(solution)/shard_map/pallas_call | solution.py:593
  236.3 9.5 %all-to-all-start.4 = ((bf16[16,64,768]{2,1,0:T(8,128)(2,1)}), bf16[16,64,768]{2,1,0:T(8,128)(2,1)S(1)}, u32[]{:S(2)}, u32[]{:S(2)}) async-start(bf16[16,64,768]{2,1,0:T(8,128)(2,1)} %bitcast.126), calls=%async_computation.4 | async-start | bytes 3145728 | tf_op jit(solution)/shard_map/all_to_all | solution.py:715
  283.3 13.6 %shard_map.212 = (f32[1024,768]{1,0:T(8,128)}, bf16[1024,768]{1,0:T(8,128)(2,1)}, bf16[1024,768]{1,0:T(8,128)(2,1)}, f32[2,768]{1,0:T(2,128)}) custom-call(s32[1,1024]{1,0:T(1,128)} %add_add_fusion.target_ref, f32[1024,768]{1,0:T(8,128)} %get-tuple-element.175.middle_ref, bf16[1024,768]{1,0:T(8,128)(2,1)} %bitcast.96, f32[1,768]{1,0:T(1,128)} %reshape.389.gain_ref, ...), custom_call_target="tpu_custom_call" | custom-call | flops 1 | bytes 1 | tf_op jit(solution)/shard_map/pallas_call | solution.py:538
  296.9 6.1 %all-to-all-start.5 = ((bf16[16,128,768]{2,1,0:T(8,128)(2,1)}), bf16[16,128,768]{2,1,0:T(8,128)(2,1)S(1)}, u32[]{:S(2)}, u32[]{:S(2)}) async-start(bf16[16,128,768]{2,1,0:T(8,128)(2,1)} %bitcast.37), calls=%async_computation.5 | async-start | bytes 6291456 | tf_op jit(solution)/shard_map/all_to_all | solution.py:715
  303.1 10.6 %shard_map.213 = (f32[1,768,1024]{2,1,0:T(8,128)}, bf16[1,1024,768]{2,1,0:T(8,128)(2,1)}, bf16[1,1024,768]{2,1,0:T(8,128)(2,1)}) custom-call(s32[1]{0:T(128)} %bitcast.11.me_ref, s32[1,2]{1,0:T(1,128)} %slice.29.low_ref, bf16[1,1024,2304]{2,1,0:T(8,128)(2,1)} %bitcast.116, bf16[1,1024,1536]{2,1,0:T(8,128)(2,1)} %bitcast.91, bf16[1,1024,1536]{2,1,0:T(8,128)(2,1)} %bitcast.92, ...), custom_call_target="tpu_custom_call" | custom-call | flops 1 | bytes 1 | tf_op jit(solution)/shard_map/pallas_call | solution.py:277
  313.7 7.4 %shard_map.214 = (bf16[1024,768]{1,0:T(8,128)(2,1)}, f32[2,768]{1,0:T(2,128)}) custom-call(bf16[1024,768]{1,0:T(8,128)(2,1)} %bitcast.13.tokens_ref, bf16[1024,768]{1,0:T(8,128)(2,1)} %bitcast.111, bf16[1024,768]{1,0:T(8,128)(2,1)} %bitcast.109, bf16[768,2304]{1,0:T(8,128)(2,1)} %refs_5_.1, bf16[768,2304]{1,0:T(8,128)(2,1)} %refs_5_.1), custom_call_target="tpu_custom_call" | custom-call | flops 1 | bytes 1 | tf_op jit(solution)/shard_map/pallas_call | solution.py:538
  322.3 39.0 %shard_map.215 = (bf16[1,1024,768]{2,1,0:T(8,128)(2,1)}, bf16[1,1024,768]{2,1,0:T(8,128)(2,1)}, bf16[1,1024,768]{2,1,0:T(8,128)(2,1)}) custom-call(s32[1]{0:T(128)} %bitcast.11.me_ref, s32[1,2]{1,0:T(1,128)} %slice.29.low_ref, bf16[1,1024,2304]{2,1,0:T(8,128)(2,1)} %bitcast.117, bf16[1,1024,2304]{2,1,0:T(8,128)(2,1)} %bitcast.118, ...), custom_call_target="tpu_custom_call" | custom-call | flops 99999997952 | bytes 1 | tf_op jit(solution)/shard_map/pallas_call | solution.py:277
  362.4 8.4 %shard_map.220.refs_4_ = bf16[768,1536]{1,0:T(8,128)(2,1)} custom-call(bf16[1024,768]{1,0:T(8,128)(2,1)} %get-tuple-element.162.refs_0_, bf16[1024,768]{1,0:T(8,128)(2,1)} %get-tuple-element.166.refs_1_, bf16[1024,768]{1,0:T(8,128)(2,1)} %bitcast.102, bf16[1024,768]{1,0:T(8,128)(2,1)} %bitcast.112), custom_call_target="tpu_custom_call" | custom-call | flops 1 | bytes 1 | tf_op jit(solution)/shard_map/pallas_call | solution.py:486
  370.9 7.4 %shard_map.221 = bf16[768,1536]{1,0:T(8,128)(2,1)} custom-call(bf16[1024,768]{1,0:T(8,128)(2,1)} %get-tuple-element.162.refs_0_, bf16[1024,768]{1,0:T(8,128)(2,1)} %get-tuple-element.166.refs_1_, bf16[1024,768]{1,0:T(8,128)(2,1)} %bitcast.104, bf16[1024,768]{1,0:T(8,128)(2,1)} %bitcast.110, ...), custom_call_target="tpu_custom_call", output_to_operand_aliasing={{}: (4, {})} | custom-call | flops 1 | bytes 1 | tf_op jit(solution)/shard_map/pallas_call | solution.py:486
  386.7 9.3 %shard_map.216 = (f32[1024,768]{1,0:T(8,128)}, f32[2,768]{1,0:T(2,128)}) custom-call(bf16[1024,768]{1,0:T(8,128)(2,1)} %bitcast.77, bf16[1024,768]{1,0:T(8,128)(2,1)} %bitcast.100, bf16[1024,768]{1,0:T(8,128)(2,1)} %bitcast.103, bf16[1024,768]{1,0:T(8,128)(2,1)} %bitcast.105, bf16[768,2304]{1,0:T(8,128)(2,1)} %refs_5_.1, bf16[768,2304]{1,0:T(8,128)(2,1)} %refs_5_.1, ...), custom_call_target="tpu_custom_call" | custom-call | flops 1 | bytes 1 | tf_op jit(solution)/shard_map/pallas_call | solution.py:538
  415.9 28.9 %collective-permute-start.13 = (bf16[96,1664]{1,0:T(8,128)(2,1)S(1)}, bf16[96,1664]{1,0:T(8,128)(2,1)S(1)}, u32[]{:S(2)}, u32[]{:S(2)}) collective-permute-start(bf16[96,1664]{1,0:T(8,128)(2,1)S(1)} %get-tuple-element.200), channel_id=1, source_target_pairs={{0,16},{1,17},{2,18},{3,19},{4,20},{5,21},{6,22},{7,23},{8,24},{9,... | collective-permute-start | bytes 958472 | tf_op jit(solution)/shard_map/ppermute | solution.py:623
  452.1 6.0 %add_bitcast_fusion = f32[1,768,1536]{2,1,0:T(8,128)} fusion(f32[768,1536]{1,0:T(8,128)} %convolution_add_fusion, bf16[768,1536]{1,0:T(8,128)(2,1)} %collective-permute-done.2), kind=kLoop, calls=%fused_computation.2 | loop fusion | flops 2359296 | bytes 11796480 | tf_op jit(solution)/shard_map/stack | solution.py:826
  462.7 8.2 %shard_map.222 = bf16[1024,768]{1,0:T(8,128)(2,1)} custom-call(s32[1,1024]{1,0:T(1,128)} %get-tuple-element.111.target_ref, f32[1024,768]{1,0:T(8,128)} %get-tuple-element.175.middle_ref, f32[1024,1]{1,0:T(8,128)} %get-tuple-element.176.gate_ref, bf16[2048,768]{1,0:T(8,128)(2,1)} %bitcast.93), custom_call_target="tpu_custom_call" | custom-call | flops 1 | bytes 1 | tf_op jit(solution)/shard_map/pallas_call | solution.py:538
  (211 shorter events, 189.5 us)
Async XLA Ops:
  0.6 38.8 %collective-permute-start = (bf16[1,1024,768]{2,1,0:T(8,128)(2,1)}, bf16[1,1024,768]{2,1,0:T(8,128)(2,1)}, u32[]{:S(2)}, u32[]{:S(2)}) collective-permute-start(bf16[1,1024,768]{2,1,0:T(8,128)(2,1)} %param.13), channel_id=1, source_target_pairs={{0,16},{1,17},{2,18},{3,19},{4,20},{5,21},{6,22},{7,23},{8,24},{9,... | collective-permute-start | bytes 4718600 | tf_op jit(solution)/shard_map/ppermute | solution.py:694
  29.8 65.3 %all-to-all-start = ((bf16[16,128,768]{2,1,0:T(8,128)(2,1)}), bf16[16,128,768]{2,1,0:T(8,128)(2,1)S(1)}, u32[]{:S(2)}, u32[]{:S(2)}) async-start(bf16[16,128,768]{2,1,0:T(8,128)(2,1)} %bitcast.94), calls=%async_computation | async-start | bytes 6291456 | tf_op jit(solution)/shard_map/all_to_all | solution.py:715
  158.2 37.0 %all-to-all-start.3 = ((bf16[16,64,768]{2,1,0:T(8,128)(2,1)}), bf16[16,64,768]{2,1,0:T(8,128)(2,1)S(1)}, u32[]{:S(2)}, u32[]{:S(2)}) async-start(bf16[16,64,768]{2,1,0:T(8,128)(2,1)} %bitcast.25), calls=%async_computation.3 | async-start | bytes 3145728 | tf_op jit(solution)/shard_map/all_to_all | solution.py:715
  195.2 41.1 %all-to-all-start.2 = ((bf16[16,64,768]{2,1,0:T(8,128)(2,1)}), bf16[16,64,768]{2,1,0:T(8,128)(2,1)S(1)}, u32[]{:S(2)}, u32[]{:S(2)}) async-start(bf16[16,64,768]{2,1,0:T(8,128)(2,1)} %bitcast.125), calls=%async_computation.2 | async-start | bytes 3145728 | tf_op jit(solution)/shard_map/all_to_all | solution.py:715
  236.3 45.8 %all-to-all-start.4 = ((bf16[16,64,768]{2,1,0:T(8,128)(2,1)}), bf16[16,64,768]{2,1,0:T(8,128)(2,1)S(1)}, u32[]{:S(2)}, u32[]{:S(2)}) async-start(bf16[16,64,768]{2,1,0:T(8,128)(2,1)} %bitcast.126), calls=%async_computation.4 | async-start | bytes 3145728 | tf_op jit(solution)/shard_map/all_to_all | solution.py:715
  255.4 65.6 %collective-permute-start.1 = (bf16[1536,768]{1,0:T(8,128)(2,1)}, bf16[1536,768]{1,0:T(8,128)(2,1)}, u32[]{:S(2)}, u32[]{:S(2)}) collective-permute-start(bf16[1536,768]{1,0:T(8,128)(2,1)} %add_convert_fusion.1), channel_id=1, source_target_pairs={{0,16},{16,0},{1,17},{17,1},{2,18},{18,2},{3,19},{19,3},{4,20},{20... | collective-permute-start | bytes 7077896 | tf_op jit(solution)/shard_map/ppermute | solution.py:814
  262.4 99.0 %collective-permute-start.2 = (bf16[768,1536]{1,0:T(8,128)(2,1)}, bf16[768,1536]{1,0:T(8,128)(2,1)}, u32[]{:S(2)}, u32[]{:S(2)}) collective-permute-start(bf16[768,1536]{1,0:T(8,128)(2,1)} %add_convert_fusion), channel_id=1, source_target_pairs={{0,16},{16,0},{1,17},{17,1},{2,18},{18,2},{3,19},{19,3},{4,20},{20... | collective-permute-start | bytes 7077896 | tf_op jit(solution)/shard_map/ppermute | solution.py:814
  296.9 65.5 %all-to-all-start.5 = ((bf16[16,128,768]{2,1,0:T(8,128)(2,1)}), bf16[16,128,768]{2,1,0:T(8,128)(2,1)S(1)}, u32[]{:S(2)}, u32[]{:S(2)}) async-start(bf16[16,128,768]{2,1,0:T(8,128)(2,1)} %bitcast.37), calls=%async_computation.5 | async-start | bytes 6291456 | tf_op jit(solution)/shard_map/all_to_all | solution.py:715
  321.1 81.8 %collective-permute-start.3 = (bf16[1,1024,768]{2,1,0:T(8,128)(2,1)}, bf16[1,1024,768]{2,1,0:T(8,128)(2,1)}, u32[]{:S(2)}, u32[]{:S(2)}) collective-permute-start(bf16[1,1024,768]{2,1,0:T(8,128)(2,1)} %bitcast.144), channel_id=1, source_target_pairs={{16,0},{17,1},{18,2},{19,3},{20,4},{21,5},{22,6},{23,7},{24,8},{25... | collective-permute-start | bytes 4718600 | tf_op jit(solution)/shard_map/ppermute | solution.py:697
  380.6 25.9 %collective-permute-start.4 = (bf16[384,1536]{1,0:T(8,128)(2,1)}, bf16[384,1536]{1,0:T(8,128)(2,1)}, u32[]{:S(2)}, u32[]{:S(2)}) collective-permute-start(bf16[384,1536]{1,0:T(8,128)(2,1)} %constant_dynamic-slice_fusion.1), channel_id=1, source_target_pairs={{0,1},{1,0},{2,3},{3,2},{4,5},{5,4},{6,7},{7,6},{8,9},{9,8},{10,11... | collective-permute-start | bytes 3538952 | tf_op jit(solution)/shard_map/ppermute | solution.py:623
  411.1 70.7 %collective-permute-start.12 = (bf16[96,1664]{1,0:T(8,128)(2,1)S(1)}, bf16[96,1664]{1,0:T(8,128)(2,1)S(1)}, u32[]{:S(2)}, u32[]{:S(2)}) collective-permute-start(bf16[96,1664]{1,0:T(8,128)(2,1)S(1)} %get-tuple-element.198), channel_id=1, source_target_pairs={{0,2},{1,3},{2,0},{3,1},{4,6},{5,7},{6,4},{7,5},{8,10},{9,11},{10,... | collective-permute-start | bytes 958472 | tf_op jit(solution)/shard_map/ppermute | solution.py:623
  415.9 65.8 %collective-permute-start.13 = (bf16[96,1664]{1,0:T(8,128)(2,1)S(1)}, bf16[96,1664]{1,0:T(8,128)(2,1)S(1)}, u32[]{:S(2)}, u32[]{:S(2)}) collective-permute-start(bf16[96,1664]{1,0:T(8,128)(2,1)S(1)} %get-tuple-element.200), channel_id=1, source_target_pairs={{0,16},{1,17},{2,18},{3,19},{4,20},{5,21},{6,22},{7,23},{8,24},{9,... | collective-permute-start | bytes 958472 | tf_op jit(solution)/shard_map/ppermute | solution.py:623
  445.8 30.3 %collective-permute-start.6 = (bf16[96,1536]{1,0:T(8,128)(2,1)}, bf16[96,1536]{1,0:T(8,128)(2,1)S(1)}, u32[]{:S(2)}, u32[]{:S(2)}) collective-permute-start(bf16[96,1536]{1,0:T(8,128)(2,1)} %get-tuple-element.201), channel_id=1, source_target_pairs={{0,2},{1,3},{2,0},{3,1},{4,6},{5,7},{6,4},{7,5},{8,10},{9,11},{10,... | collective-permute-start | bytes 884744 | tf_op jit(solution)/shard_map/ppermute | solution.py:623
  446.3 29.9 %collective-permute-start.7 = (bf16[96,1536]{1,0:T(8,128)(2,1)}, bf16[96,1536]{1,0:T(8,128)(2,1)S(1)}, u32[]{:S(2)}, u32[]{:S(2)}) collective-permute-start(bf16[96,1536]{1,0:T(8,128)(2,1)} %get-tuple-element.203), channel_id=1, source_target_pairs={{0,16},{1,17},{2,18},{3,19},{4,20},{5,21},{6,22},{7,23},{8,24},{9,... | collective-permute-start | bytes 884744 | tf_op jit(solution)/shard_map/ppermute | solution.py:623
  446.3 29.9 %collective-permute-start.8 = (bf16[96,1536]{1,0:T(8,128)(2,1)}, bf16[96,1536]{1,0:T(8,128)(2,1)}, u32[]{:S(2)}, u32[]{:S(2)}) collective-permute-start(bf16[96,1536]{1,0:T(8,128)(2,1)} %get-tuple-element.202), channel_id=1, source_target_pairs={{0,18},{1,19},{2,16},{3,17},{4,22},{5,23},{6,20},{7,21},{8,26},{9,... | collective-permute-start | bytes 884744 | tf_op jit(solution)/shard_map/ppermute | solution.py:623
  477.5 11.9 %collective-permute-start.10 = (bf16[24,1536]{1,0:T(8,128)(2,1)S(1)}, bf16[24,1536]{1,0:T(8,128)(2,1)S(1)}, u32[]{:S(2)}, u32[]{:S(2)}) collective-permute-start(bf16[24,1536]{1,0:T(8,128)(2,1)S(1)} %get-tuple-element.209), channel_id=1, source_target_pairs={{0,8},{1,9},{2,10},{3,11},{4,12},{5,13},{6,14},{7,15},{8,0},{9,1},... | collective-permute-start | bytes 221192 | tf_op jit(solution)/shard_map/ppermute | solution.py:623
  480.3 11.0 %collective-permute-start.11 = (bf16[24,1536]{1,0:T(8,128)(2,1)S(1)}, bf16[24,1536]{1,0:T(8,128)(2,1)S(1)}, u32[]{:S(2)}, u32[]{:S(2)}) collective-permute-start(bf16[24,1536]{1,0:T(8,128)(2,1)S(1)} %get-tuple-element.208), channel_id=1, source_target_pairs={{0,12},{1,13},{2,14},{3,15},{4,8},{5,9},{6,10},{7,11},{8,4},{9,5},... | collective-permute-start | bytes 221192 | tf_op jit(solution)/shard_map/ppermute | solution.py:623
  495.8 17.9 %collective-permute-start.18 = (bf16[24,1664]{1,0:T(8,128)(2,1)S(1)}, bf16[24,1664]{1,0:T(8,128)(2,1)S(1)}, u32[]{:S(2)}, u32[]{:S(2)}) collective-permute-start(bf16[24,1664]{1,0:T(8,128)(2,1)S(1)} %add_convert_fusion.2), channel_id=1, source_target_pairs={{0,4},{1,5},{2,6},{3,7},{4,0},{5,1},{6,2},{7,3},{8,12},{9,13},{10,... | collective-permute-start | bytes 239624 | tf_op jit(solution)/shard_map/ppermute | solution.py:623
  496.7 19.5 %collective-permute-start.19 = (bf16[24,1664]{1,0:T(8,128)(2,1)S(1)}, bf16[24,1664]{1,0:T(8,128)(2,1)S(1)}, u32[]{:S(2)}, u32[]{:S(2)}) collective-permute-start(bf16[24,1664]{1,0:T(8,128)(2,1)S(1)} %add_convert_fusion.2), channel_id=1, source_target_pairs={{0,8},{1,9},{2,10},{3,11},{4,12},{5,13},{6,14},{7,15},{8,0},{9,1},... | collective-permute-start | bytes 239624 | tf_op jit(solution)/shard_map/ppermute | solution.py:623
  498.3 17.9 %collective-permute-start.20 = (bf16[24,1664]{1,0:T(8,128)(2,1)S(1)}, bf16[24,1664]{1,0:T(8,128)(2,1)S(1)}, u32[]{:S(2)}, u32[]{:S(2)}) collective-permute-start(bf16[24,1664]{1,0:T(8,128)(2,1)S(1)} %add_convert_fusion.2), channel_id=1, source_target_pairs={{0,12},{1,13},{2,14},{3,15},{4,8},{5,9},{6,10},{7,11},{8,4},{9,5},... | collective-permute-start | bytes 239624 | tf_op jit(solution)/shard_map/ppermute | solution.py:623
  513.7 16.0 %collective-permute-start.30 = (bf16[96,1536]{1,0:T(8,128)(2,1)S(1)}, bf16[96,1536]{1,0:T(8,128)(2,1)S(1)}, u32[]{:S(2)}, u32[]{:S(2)}) collective-permute-start(bf16[96,1536]{1,0:T(8,128)(2,1)S(1)} %constant_dynamic-update-slice_fusion.6), channel_id=1, source_target_pairs={{0,18},{1,19},{2,16},{3,17},{4,22},{5,23},{6,20},{7,21},{8,26},{9,... | collective-permute-start | bytes 884744 | tf_op jit(solution)/shard_map/ppermute | solution.py:623
  516.3 15.3 %collective-permute-start.21 = (bf16[96,1664]{1,0:T(8,128)(2,1)S(1)}, bf16[96,1664]{1,0:T(8,128)(2,1)S(1)}, u32[]{:S(2)}, u32[]{:S(2)}) collective-permute-start(bf16[96,1664]{1,0:T(8,128)(2,1)S(1)} %constant_dynamic-update-slice_fusion.16), channel_id=1, source_target_pairs={{0,2},{1,3},{2,0},{3,1},{4,6},{5,7},{6,4},{7,5},{8,10},{9,11},{10,... | collective-permute-start | bytes 958472 | tf_op jit(solution)/shard_map/ppermute | solution.py:623
  516.9 15.6 %collective-permute-start.22 = (bf16[96,1664]{1,0:T(8,128)(2,1)S(1)}, bf16[96,1664]{1,0:T(8,128)(2,1)S(1)}, u32[]{:S(2)}, u32[]{:S(2)}) collective-permute-start(bf16[96,1664]{1,0:T(8,128)(2,1)S(1)} %constant_dynamic-update-slice_fusion.16), channel_id=1, source_target_pairs={{0,16},{1,17},{2,18},{3,19},{4,20},{5,21},{6,22},{7,23},{8,24},{9,... | collective-permute-start | bytes 958472 | tf_op jit(solution)/shard_map/ppermute | solution.py:623
  521.6 14.9 %collective-permute-start.23 = (bf16[96,1664]{1,0:T(8,128)(2,1)S(1)}, bf16[96,1664]{1,0:T(8,128)(2,1)S(1)}, u32[]{:S(2)}, u32[]{:S(2)}) collective-permute-start(bf16[96,1664]{1,0:T(8,128)(2,1)S(1)} %constant_dynamic-update-slice_fusion.16), channel_id=1, source_target_pairs={{0,18},{1,19},{2,16},{3,17},{4,22},{5,23},{6,20},{7,21},{8,26},{9,... | collective-permute-start | bytes 958472 | tf_op jit(solution)/shard_map/ppermute | solution.py:623
  (45 other events, 414.3 us)

commit v2 on v1

--- a/solution.py
+++ b/solution.py
@@ -459,62 +459,77 @@
     )
 
 
-def weight_grad_kernel(*refs, count, into):
-    lefts, rights = refs[:count], refs[count : 2 * count]
-    out_ref = refs[2 * count + (1 if into else 0)]
-    turns = refs[-count:]
-
-    @pl.when(pl.program_id(0) == 0)
-    def turn():
-        for left, turn_ref in zip(lefts, turns):
-            turn_ref[...] = turned(left[...])
-
-    out_ref[...] = sum(dot(turn_ref[...], right[...]) for turn_ref, right in zip(turns, rights)).astype(bf16)
-
-
-def weight_grad(pairs, columns, offset, into):
-    width, wide = pairs[0][0].shape[1], pairs[0][1].shape[1]
-    tile = tile_of(wide, 256)
-    lefts, rights = [a for a, _ in pairs], [b for _, b in pairs]
-    specs = [pl.BlockSpec(a.shape, lambda i: (0, 0), pipeline_mode=pl.Buffered(1)) for a in lefts]
-    specs += [pl.BlockSpec((b.shape[0], tile), lambda i: (0, i)) for b in rights]
-    arrays, aliases = lefts + rights, {}
-    if into is not None:
-        aliases = {len(arrays): 0}
-        specs.append(pl.BlockSpec(memory_space=pl.ANY))
-        arrays.append(into)
+def weight_grads_kernel(*refs):
+    early_ref, late_ref = refs[-2:]
+    width = early_ref.shape[1] // 2
+    own, other, context = [turned(ref[...]) for ref in refs[:3]]
+    dq, dk, dv, dk_other, dv_other, attn_grad = [ref[...] for ref in refs[3:9]]
+    early_ref[:, :width] = (dot(own, dk) + dot(other, dk_other)).astype(bf16)
+    early_ref[:, width:] = (dot(own, dv) + dot(other, dv_other)).astype(bf16)
+    late_ref[:, :width] = dot(own, dq).astype(bf16)
+    late_ref[:, width:] = dot(context, attn_grad).astype(bf16)
+
+
+def weight_grads(own, other, context, dq, dk, dv, dk_other, dv_other, attn_grad):
+    width = own.shape[1]
+    tile = tile_of(width, 256)
+    lefts, rights = [own, other, context], [dq, dk, dv, dk_other, dv_other, attn_grad]
+    specs = [pl.BlockSpec((left.shape[0], tile), lambda i: (0, i)) for left in lefts]
+    specs += [pl.BlockSpec(right.shape, lambda i: (0, 0), pipeline_mode=pl.Buffered(1)) for right in rights]
+    shape = jax.ShapeDtypeStruct((width, 2 * width), bf16)
+    spec = pl.BlockSpec((tile, 2 * width), lambda i: (i, 0))
     return pl.pallas_call(
-        functools.partial(weight_grad_kernel, count=len(pairs), into=into is not None),
-        grid=(wide // tile,),
+        weight_grads_kernel,
+        grid=(width // tile,),
         in_specs=specs,
-        out_specs=pl.BlockSpec((width, tile), lambda i: (0, offset // tile + i)),
-        out_shape=jax.ShapeDtypeStruct((width, columns), bf16),
-        scratch_shapes=[pltpu.VMEM((width, a.shape[0]), bf16) for a in lefts],
-        input_output_aliases=aliases,
+        out_specs=[spec, spec],
+        out_shape=[shape, shape],
         compiler_params=params(),
         cost_estimate=SHORT,
-    )(*arrays)
-
-
-def sums_kernel(first_ref, other_ref, second_ref, into_ref, out_ref):
-    rows = jnp.concatenate([first_ref[...] + other_ref[...], second_ref[...]], 0)
+    )(*lefts, *rights)
+
+
+def sums_kernel(*refs):
+    rows = jnp.concatenate([refs[0][...] + refs[1][...], refs[2][...]], 0)
     rows = jnp.concatenate([rows, jnp.zeros((124, rows.shape[1]), f32)], 0)
-    out_ref[...] = rows.T.astype(bf16)
-
-
-def put_sums(first, other, second, into):
-    width, columns = into.shape
-    spec = pl.BlockSpec((2, width), lambda i: (0, 0))
+    refs[-1][...] = rows.T.astype(bf16)
+
+
+def column_sums(own, other, second):
     return pl.pallas_call(
         sums_kernel,
-        grid=(1,),
-        in_specs=[spec, spec, spec, pl.BlockSpec(memory_space=pl.ANY)],
-        out_specs=pl.BlockSpec((width, 128), lambda i: (0, columns // 128 - 1)),
-        out_shape=jax.ShapeDtypeStruct(into.shape, bf16),
-        input_output_aliases={3: 0},
+        out_shape=jax.ShapeDtypeStruct((own.shape[1], 128), bf16),
         compiler_params=params(),
         cost_estimate=SHORT,
-    )(first, other, second, into)
+    )(own, other, second)
+
+
+def finish_kernel(early_ref, late_ref, in_ref, out_ref, vectors_ref):
+    width = out_ref.shape[1]
+    in_ref[:, :width] = late_ref[:, :width].astype(f32)
+    in_ref[:, width:] = early_ref[...].astype(f32)
+    out_ref[...] = late_ref[:, width : 2 * width].astype(f32)
+    vectors_ref[...] = late_ref[:, 2 * width :].astype(f32).T[:8]
+
+
+def finish(early, late):
+    width = early.shape[0]
+    tile = tile_of(width, 256)
+
+    def cut(array):
+        return pl.BlockSpec((tile, array.shape[1]), lambda i: (i, 0))
+
+    in_shape = jax.ShapeDtypeStruct((width, 3 * width), f32)
+    out_shape = jax.ShapeDtypeStruct((width, width), f32)
+    return pl.pallas_call(
+        finish_kernel,
+        grid=(width // tile,),
+        in_specs=[cut(early), cut(late)],
+        out_specs=[cut(in_shape), cut(out_shape), pl.BlockSpec((8, tile), lambda i: (0, i))],
+        out_shape=[in_shape, out_shape, jax.ShapeDtypeStruct((8, width), f32)],
+        compiler_params=params(),
+        cost_estimate=SHORT,
+    )(early, late)
 
 
 def by_tokens(kernel, flat, tiled, whole, out_shape):
@@ -645,20 +660,17 @@
     return summed
 
 
-def gather_parts(parts):
-    stages = stages_of(lax.axis_size("wide"), lax.axis_size("blk"))
-    for bits, code in reversed(list(zip(stages, places_of(stages)))):
-        gathered = []
-        for x in parts:
-            rows = x.shape[0]
-            whole = jnp.zeros((rows << len(bits), x.shape[1]), bf16)
-            whole = lax.dynamic_update_slice_in_dim(whole, x, code * rows, 0)
-            for other in range(1, 1 << len(bits)):
-                part = swap(x, spread(other, bits))
-                whole = lax.dynamic_update_slice_in_dim(whole, part, (code ^ other) * rows, 0)
-            gathered.append(whole)
-        parts = gathered
-    return parts
+def gather_step(parts, bits, code):
+    gathered = []
+    for x in parts:
+        rows = x.shape[0]
+        whole = jnp.zeros((rows << len(bits), x.shape[1]), bf16)
+        whole = lax.dynamic_update_slice_in_dim(whole, x, code * rows, 0)
+        for other in range(1, 1 << len(bits)):
+            part = swap(x, spread(other, bits))
+            whole = lax.dynamic_update_slice_in_dim(whole, part, (code ^ other) * rows, 0)
+        gathered.append(whole)
+    return gathered
 
 
 def body(
@@ -746,7 +758,7 @@
     second_gain_row, second_shift_row = second_gain.reshape(1, width), second_shift.reshape(1, width)
     small = (attention.low, attention.start_row, route_row, target_halves_row, target_whole_row)
     small += (first_gain_row, first_shift_row, second_gain_row, second_shift_row)
-    joint, small, to_place = lax.optimization_barrier((joint, small, upstream))
+    small, to_place = lax.optimization_barrier((small, upstream))
     attention.low, attention.start_row, route_row, target_halves_row, target_whole_row = small[:5]
     first_gain_row, first_shift_row, second_gain_row, second_shift_row = small[5:]
     grads_arrived = exchange(place(target_whole_row, to_place, halves * half_slots))
@@ -768,9 +780,8 @@
         [wide_shape, low_shape, jax.ShapeDtypeStruct((flat, 1), f32)],
     )
     normed_two, grads_arrived = lax.optimization_barrier((normed_two, grads_arrived))
-    placed = place(target_halves_row, normed_two, halves * half_slots)
-    placed = placed.reshape(halves, half_slots, width)
-    arrived = [exchange(placed[h]).reshape(peers, local_experts, rows * depth, width) for h in range(halves)]
+    placed = [place(target_halves_row - h * half_slots, normed_two, half_slots) for h in range(halves)]
+    arrived = [exchange(part).reshape(peers, local_experts, rows * depth, width) for part in placed]
 
     own_experts = lax.axis_index("wide") * local_experts
     outputs, row_grads = [None] * local_experts, []
@@ -860,13 +871,12 @@
     returned = [behind(returned[:, shift - 1], shift) for shift in shifts]
     dq, dk, dv = attention.backward_own(joint, context_grad, context, lse, dq_state)
     dq, dk, dv = [part.reshape(flat, width) for part in (dq, dk, dv)]
-    dq, dk, dv, produced, down_got, up_got = lax.optimization_barrier((dq, dk, dv, produced, down_got, up_got))
-
-    kv_grad = weight_grad([(normed_one, dk), (normed_other, dk_other)], 2 * width, 0, None)
-    kv_grad = weight_grad([(normed_one, dv), (normed_other, dv_other)], 2 * width, width, kv_grad)
-    columns = 2 * width + 128
-    rest_grad = weight_grad([(context_flat, attn_grad)], columns, width, None)
-    rest_grad = weight_grad([(normed_one, dq)], columns, 0, rest_grad)
+    tied = (dq, dk, dv, produced, down_got, up_got, returned)
+    dq, dk, dv, produced, down_got, up_got, returned = lax.optimization_barrier(tied)
+
+    early, late = weight_grads(
+        normed_one, normed_other, context_flat, dq, dk, dv, dk_other, dv_other, attn_grad
+    )
     own_grad, own_sums = by_tokens(
         input_grad_kernel,
         flat,
@@ -874,21 +884,27 @@
         [(project_in, 0), (project_in, 1), (project_in, 2)],
         [wide_shape, sums_shape],
     )
-
-    rest_grad = put_sums(own_sums, other_sums, second_sums, rest_grad)
-    rest_grad, returned = lax.optimization_barrier((rest_grad, returned))
-    shares = [kv_grad, rest_grad]
+    vectors = column_sums(own_sums, other_sums, second_sums)
+
     stages = stages_of(lax.axis_size("wide"), blocks)
-    for number, (bits, code) in enumerate(zip(stages, places_of(stages))):
-        shares = reduce_step(shares, bits, code)
-        if number == 0:
-            late = (down_own, up_own, down_got, up_got, middle, produced, own_grad, returned)
-            late, shares = lax.optimization_barrier((late, shares))
-            down_own, up_own, down_got, up_got, middle, produced, own_grad, returned = late
-    shares = [x.astype(bf16) for x in shares]
-
+    steps = list(zip(stages, places_of(stages)))
+    early, late, vectors = reduce_step([early, late, vectors], *steps[0])
+    rest = (down_own, up_own, down_got, up_got)
+    rest, early = lax.optimization_barrier((rest, early))
+    down_own, up_own, down_got, up_got = rest
     down_share = summed_shares(down_own, down_got)
     up_share = summed_shares(up_own, up_got)
+    shares = [early, jnp.concatenate([late, vectors], 1)]
+    for step in steps[1:-1]:
+        shares = reduce_step(shares, *step)
+    down_share, up_share, shares = lax.optimization_barrier((down_share, up_share, shares))
+    shares = reduce_step(shares, *steps[-1])
+    shares = [x.astype(bf16) for x in shares]
+
+    shares = gather_step(shares, *steps[-1])
+    rest = (middle, produced, own_grad, returned)
+    rest, shares = lax.optimization_barrier((rest, shares))
+    middle, produced, own_grad, returned = rest
     total_grad = own_grad
     for part in returned:
         total_grad = total_grad + part.reshape(flat, width).astype(f32)
@@ -901,21 +917,21 @@
         [(produced, None)],
         [low_shape],
     )
-    down_share, up_share, stream_grad, result, shares = lax.optimization_barrier(
-        (down_share, up_share, stream_grad, result, shares)
-    )
-    kv_sum, q_sum = [part.astype(f32) for part in gather_parts(shares)]
+    for step in reversed(steps[1:-1]):
+        shares = gather_step(shares, *step)
+    stream_grad, result, shares = lax.optimization_barrier((stream_grad, result, shares))
+    in_sum, out_sum, vectors = finish(*gather_step(shares, *steps[0]))
 
     out_shape = (rows, block_len, width)
     return (
         result.reshape(out_shape),
         stream_grad.reshape(out_shape),
-        jnp.concatenate([q_sum[:, :width], kv_sum], 1),
-        q_sum[:, width : 2 * width],
-        q_sum[:, 2 * width],
-        q_sum[:, 2 * width + 1],
-        q_sum[:, 2 * width + 2],
-        q_sum[:, 2 * width + 3],
+        in_sum,
+        out_sum,
+        vectors[0],
+        vectors[1],
+        vectors[2],
+        vectors[3],
         up_share,
         down_share,
     )

time: 553 us -> 533 us (0.964)
  blocking collectives: 51.4 us -> 0 us
  waiting for transfers between devices: 54.9 us -> 104 us
  Pallas kernels: 243 us -> 230 us
    all_to_all x1 -> x0, blocking collectives: 51.4 us -> none  [exchange(): lax.all_to_all(array.reshape(experts, -1, width), 'wide', split_axis=0, c...]
    ppermute x1, waiting for transfers between devices: 0.01 us -> 32.2 us  [behind(): lax.ppermute(array, 'blk', [(i + shift, i) for i in range(blocks - shift)])]
    all_to_all x5 -> x6, waiting for transfers between devices: 17 us -> 45.8 us  [exchange(): lax.all_to_all(array.reshape(experts, -1, width), 'wide', split_axis=0, c...]
    ppermute x28 -> x29, starting transfers between devices: 62.5 us -> 38.5 us  [swap(): lax.ppermute(array, ('blk', 'wide'), [(i, i ^ mask) for i in range(total)])]
    all_to_all x5 -> x6, starting transfers between devices: 35.7 us -> 55.6 us  [exchange(): lax.all_to_all(array.reshape(experts, -1, width), 'wide', split_axis=0, c...]
    pallas_call x3, Pallas kernels: 82.7 us -> 74.1 us  [call(): pl.pallas_call(functools.partial(kernel, tile=self.tile, block_len=self.b...]
    ppermute x28 -> x29, waiting for transfers between devices: 34.2 us -> 25.6 us  [swap(): lax.ppermute(array, ('blk', 'wide'), [(i, i ^ mask) for i in range(total)])]
    pallas_call x5 -> x3, Pallas kernels: 27.9 us -> 22.1 us  [the longest x1 14.5 us: weight_grads(): pl.pallas_call(weight_grads_kernel, grid=(width // tile,), in_specs=specs...]
  transfers between devices with their start and end apart: 37 -> 39, of which waited for: 17 -> 13; matrix products, arithmetic and copies ran while one was open for 14% -> 15% of each run, Pallas kernels for 43% -> 39%
where the time goes in v2:
time: 533 us; the launch traced here: 527 us
  Pallas kernels  230 us (43%)
  waiting for transfers between devices  104 us (20%)
  starting transfers between devices  103 us (19%)
  matrix products  34.8 us (7%)
  local copies, waits for them, and re-layouts  27 us (5%)
  other arithmetic  26.7 us (5%)
    pallas_call x3, Pallas kernels, call(): pl.pallas_call(functools.partial(kernel, tile=self.tile, block_len=self.b...  74.1 us
    pallas_call x7, Pallas kernels, by_tokens(): pl.pallas_call(kernel, grid=(flat // tile,), in_specs=specs, out_specs=[c...  61.5 us
    all_to_all x6, starting transfers between devices, exchange(): lax.all_to_all(array.reshape(experts, -1, width), 'wide', split_axis=0, c...  55.6 us
    pallas_call x2, Pallas kernels, run_expert(): pl.pallas_call(expert_kernel, grid=(rows // tile,), in_specs=in_specs, ou...  54.6 us
    all_to_all x6, waiting for transfers between devices, exchange(): lax.all_to_all(array.reshape(experts, -1, width), 'wide', split_axis=0, c...  45.8 us
    ppermute x29, starting transfers between devices, swap(): lax.ppermute(array, ('blk', 'wide'), [(i, i ^ mask) for i in range(total)])  38.5 us
    ppermute x1, waiting for transfers between devices, behind(): lax.ppermute(array, 'blk', [(i + shift, i) for i in range(blocks - shift)])  32.2 us
    ppermute x29, waiting for transfers between devices, swap(): lax.ppermute(array, ('blk', 'wide'), [(i, i ^ mask) for i in range(total)])  25.6 us
  transfers between devices with their start and end apart: 39, of which 13 were waited for; matrix products, arithmetic and copies ran while one was open for 15% of the time, Pallas kernels for 39%

profile of v2, /device:TPU:0, one launch (start us, length us, event | category | flops | bytes accessed | tf_op | source)
XLA Modules:
  0.0 527.0 jit_solution(14332537257645179241)
XLA Ops:
  0.6 6.0 %collective-permute-start = (bf16[1,1024,768]{2,1,0:T(8,128)(2,1)}, bf16[1,1024,768]{2,1,0:T(8,128)(2,1)}, u32[]{:S(2)}, u32[]{:S(2)}) collective-permute-start(bf16[1,1024,768]{2,1,0:T(8,128)(2,1)} %param.13), channel_id=1, source_target_pairs={{0,16},{1,17},{2,18},{3,19},{4,20},{5,21},{6,22},{7,23},{8,24},{9,... | collective-permute-start | bytes 4718600 | tf_op jit(solution)/shard_map/ppermute | solution.py:706
  18.9 7.3 %shard_map.208 = bf16[2048,768]{1,0:T(8,128)(2,1)} custom-call(s32[1,1024]{1,0:T(1,128)} %get-tuple-element.117.target_ref, bf16[1024,768]{1,0:T(8,128)(2,1)} %bitcast.101), custom_call_target="tpu_custom_call" | custom-call | flops 1 | bytes 1 | tf_op jit(solution)/shard_map/pallas_call | solution.py:354
  32.1 8.5 %shard_map.204 = (bf16[1024,768]{1,0:T(8,128)(2,1)}, bf16[1024,2304]{1,0:T(8,128)(2,1)}) custom-call(bf16[1024,768]{1,0:T(8,128)(2,1)} %bitcast.75, f32[1,768]{1,0:T(1,128)} %reshape.387.gain_ref, f32[1,768]{1,0:T(1,128)} %reshape.388.shift_ref, bf16[768,2304]{1,0:T(8,128)(2,1)} %refs_5_.1, bf16[768,2304]{1,0:T(8,128)(2,1)} %refs_5_.1, bf16[768,2304]{1,0:T(8,128)(2,1)} %refs_5_.1), custom_call_target="tpu_custom_call" | custom-call | flops 1 | bytes 1 | tf_op jit(solution)/shard_map/pallas_call | solution.py:553
  40.6 7.1 %shard_map.205 = (bf16[1024,768]{1,0:T(8,128)(2,1)}, bf16[1024,1536]{1,0:T(8,128)(2,1)}) custom-call(bf16[1024,768]{1,0:T(8,128)(2,1)} %bitcast.13.tokens_ref, f32[1,768]{1,0:T(1,128)} %reshape.387.gain_ref, f32[1,768]{1,0:T(1,128)} %reshape.388.shift_ref, bf16[768,2304]{1,0:T(8,128)(2,1)} %refs_5_.1, bf16[768,2304]{1,0:T(8,128)(2,1)} %refs_5_.1), custom_call_target="tpu_custom_call" | custom-call | flops 1 | bytes 1 | tf_op jit(solution)/shard_map/pallas_call | solution.py:553
  47.7 24.4 %shard_map.206 = (bf16[1,1024,768]{2,1,0:T(8,128)(2,1)}, f32[1,3,4,1024]{3,2,1,0:T(4,128)}) custom-call(s32[1]{0:T(128)} %bitcast.10.me_ref, s32[1,2]{1,0:T(1,128)} %slice.15.low_ref, bf16[1,1024,2304]{2,1,0:T(8,128)(2,1)} %bitcast.110, bf16[1,1024,2304]{2,1,0:T(8,128)(2,1)} %bitcast.111, bf16[1,1024,2304]{2,1,0:T(8,128)(2,1)} %bitcast.112, ...), custom_call_target="tpu_custom_call" | custom-call | flops 99999997952 | bytes 1 | tf_op jit(solution)/shard_map/pallas_call | solution.py:277
  72.1 7.5 %shard_map.207 = (f32[1024,768]{1,0:T(8,128)}, bf16[1024,768]{1,0:T(8,128)(2,1)}, f32[1024,1]{1,0:T(8,128)}) custom-call(bf16[1024,768]{1,0:T(8,128)(2,1)} %bitcast.84, bf16[1024,768]{1,0:T(8,128)(2,1)} %bitcast.76, s32[1,1024]{1,0:T(1,128)} %bitcast.132, bf16[768,768]{1,0:T(8,128)(2,1)} %weight_ref.3, f32[1,768]{1,0:T(1,128)} %reshape.389.gain_ref, ...), custom_call_target="tpu_custom_call" | custom-call | flops 1 | bytes 1 | tf_op jit(solution)/shard_map/pallas_call | solution.py:553
  79.6 11.9 %all-to-all-done = bf16[16,128,768]{2,1,0:T(8,128)(2,1)S(1)} async-done(((bf16[16,128,768]{2,1,0:T(8,128)(2,1)}), bf16[16,128,768]{2,1,0:T(8,128)(2,1)S(1)}, u32[]{:S(2)}, u32[]{:S(2)}) %all-to-all-start) | async-done | bytes 3145760 | tf_op jit(solution)/shard_map/all_to_all | solution.py:727
  97.3 15.6 %all-to-all-start.1 = ((bf16[16,64,768]{2,1,0:T(8,128)(2,1)}), bf16[16,64,768]{2,1,0:T(8,128)(2,1)}, u32[]{:S(2)}, u32[]{:S(2)}) async-start(bf16[16,64,768]{2,1,0:T(8,128)(2,1)} %bitcast.105), calls=%async_computation.1 | async-start | bytes 3145728 | tf_op jit(solution)/shard_map/all_to_all | solution.py:727
  118.2 26.7 %all-to-all-done.1 = bf16[16,64,768]{2,1,0:T(8,128)(2,1)} async-done(((bf16[16,64,768]{2,1,0:T(8,128)(2,1)}), bf16[16,64,768]{2,1,0:T(8,128)(2,1)}, u32[]{:S(2)}, u32[]{:S(2)}) %all-to-all-start.1) | async-done | bytes 1572896 | tf_op jit(solution)/shard_map/all_to_all | solution.py:727
  145.0 9.1 %all-to-all-start.3 = ((bf16[16,64,768]{2,1,0:T(8,128)(2,1)}), bf16[16,64,768]{2,1,0:T(8,128)(2,1)S(1)}, u32[]{:S(2)}, u32[]{:S(2)}) async-start(bf16[16,64,768]{2,1,0:T(8,128)(2,1)} %bitcast.104), calls=%async_computation.3 | async-start | bytes 3145728 | tf_op jit(solution)/shard_map/all_to_all | solution.py:727
  155.4 27.2 %shard_map.210 = (bf16[16,2,64,768]{3,2,1,0:T(8,128)(2,1)}, bf16[1024,768]{1,0:T(8,128)(2,1)}, bf16[1024,3072]{1,0:T(8,128)(2,1)}, bf16[1024,3072]{1,0:T(8,128)(2,1)}, bf16[1024,768]{1,0:T(8,128)(2,1)}) custom-call(bf16[1024,768]{1,0:T(8,128)(2,1)} %bitcast.19.refs_0_, bf16[16,2,64,768]{3,2,1,0:T(8,128)(2,1)} %bitcast.78, bf16[768,3072]{1,0:T(8,128)(2,1)} %bitcast.80, ...), custom_call_target="tpu_custom_call" | custom-call | flops 1 | bytes 1 | tf_op jit(solution)/shard_map/pallas_call | solution.py:608
  186.0 9.2 %all-to-all-start.2 = ((bf16[16,64,768]{2,1,0:T(8,128)(2,1)}), bf16[16,64,768]{2,1,0:T(8,128)(2,1)}, u32[]{:S(2)}, u32[]{:S(2)}) async-start(bf16[16,64,768]{2,1,0:T(8,128)(2,1)} %bitcast.124), calls=%async_computation.2 | async-start | bytes 3145728 | tf_op jit(solution)/shard_map/all_to_all | solution.py:727
  196.1 27.3 %shard_map.212 = (bf16[16,2,64,768]{3,2,1,0:T(8,128)(2,1)}, bf16[1024,768]{1,0:T(8,128)(2,1)}, bf16[1024,3072]{1,0:T(8,128)(2,1)}, bf16[1024,3072]{1,0:T(8,128)(2,1)}, bf16[1024,768]{1,0:T(8,128)(2,1)}) custom-call(bf16[1024,768]{1,0:T(8,128)(2,1)} %bitcast.86, bf16[16,2,64,768]{3,2,1,0:T(8,128)(2,1)} %bitcast.79, ...), custom_call_target="tpu_custom_call", output_to_operand_aliasing={{0}: (5, {})} | custom-call | flops 1 | bytes 1 | tf_op jit(solution)/shard_map/pallas_call | solution.py:608
  227.2 9.3 %all-to-all-start.4 = ((bf16[16,64,768]{2,1,0:T(8,128)(2,1)}), bf16[16,64,768]{2,1,0:T(8,128)(2,1)S(1)}, u32[]{:S(2)}, u32[]{:S(2)}) async-start(bf16[16,64,768]{2,1,0:T(8,128)(2,1)} %bitcast.125), calls=%async_computation.4 | async-start | bytes 3145728 | tf_op jit(solution)/shard_map/all_to_all | solution.py:727
  273.2 13.7 %shard_map.213 = (f32[1024,768]{1,0:T(8,128)}, bf16[1024,768]{1,0:T(8,128)(2,1)}, bf16[1024,768]{1,0:T(8,128)(2,1)}, f32[2,768]{1,0:T(2,128)}) custom-call(s32[1,1024]{1,0:T(1,128)} %add_add_fusion.target_ref, f32[1024,768]{1,0:T(8,128)} %get-tuple-element.184.middle_ref, bf16[1024,768]{1,0:T(8,128)(2,1)} %bitcast.102, f32[1,768]{1,0:T(1,128)} %reshape.389.gain_ref, ...), custom_call_target="tpu_custom_call" | custom-call | flops 1 | bytes 1 | tf_op jit(solution)/shard_map/pallas_call | solution.py:553
  286.8 6.5 %all-to-all-start.5 = ((bf16[16,128,768]{2,1,0:T(8,128)(2,1)}), bf16[16,128,768]{2,1,0:T(8,128)(2,1)S(1)}, u32[]{:S(2)}, u32[]{:S(2)}) async-start(bf16[16,128,768]{2,1,0:T(8,128)(2,1)} %bitcast.37), calls=%async_computation.5 | async-start | bytes 6291456 | tf_op jit(solution)/shard_map/all_to_all | solution.py:727
  293.4 10.6 %shard_map.214 = (f32[1,768,1024]{2,1,0:T(8,128)}, bf16[1,1024,768]{2,1,0:T(8,128)(2,1)}, bf16[1,1024,768]{2,1,0:T(8,128)(2,1)}) custom-call(s32[1]{0:T(128)} %bitcast.10.me_ref, s32[1,2]{1,0:T(1,128)} %slice.15.low_ref, bf16[1,1024,2304]{2,1,0:T(8,128)(2,1)} %bitcast.113, bf16[1,1024,1536]{2,1,0:T(8,128)(2,1)} %bitcast.91, bf16[1,1024,1536]{2,1,0:T(8,128)(2,1)} %bitcast.92, ...), custom_call_target="tpu_custom_call" | custom-call | flops 1 | bytes 1 | tf_op jit(solution)/shard_map/pallas_call | solution.py:277
  304.0 7.3 %shard_map.215 = (bf16[1024,768]{1,0:T(8,128)(2,1)}, f32[2,768]{1,0:T(2,128)}) custom-call(bf16[1024,768]{1,0:T(8,128)(2,1)} %bitcast.13.tokens_ref, bf16[1024,768]{1,0:T(8,128)(2,1)} %bitcast.106, bf16[1024,768]{1,0:T(8,128)(2,1)} %bitcast.108, bf16[768,2304]{1,0:T(8,128)(2,1)} %refs_5_.1, bf16[768,2304]{1,0:T(8,128)(2,1)} %refs_5_.1), custom_call_target="tpu_custom_call" | custom-call | flops 1 | bytes 1 | tf_op jit(solution)/shard_map/pallas_call | solution.py:553
  312.6 39.1 %shard_map.216 = (bf16[1,1024,768]{2,1,0:T(8,128)(2,1)}, bf16[1,1024,768]{2,1,0:T(8,128)(2,1)}, bf16[1,1024,768]{2,1,0:T(8,128)(2,1)}) custom-call(s32[1]{0:T(128)} %bitcast.10.me_ref, s32[1,2]{1,0:T(1,128)} %slice.15.low_ref, bf16[1,1024,2304]{2,1,0:T(8,128)(2,1)} %bitcast.114, bf16[1,1024,2304]{2,1,0:T(8,128)(2,1)} %bitcast.115, ...), custom_call_target="tpu_custom_call" | custom-call | flops 99999997952 | bytes 1 | tf_op jit(solution)/shard_map/pallas_call | solution.py:277
  351.7 32.2 %collective-permute-done.3 = bf16[1,1024,768]{2,1,0:T(8,128)(2,1)} collective-permute-done((bf16[1,1024,768]{2,1,0:T(8,128)(2,1)}, bf16[1,1024,768]{2,1,0:T(8,128)(2,1)}, u32[]{:S(2)}, u32[]{:S(2)}) %collective-permute-start.3) | collective-permute-done | bytes 1572896 | tf_op jit(solution)/shard_map/ppermute | solution.py:709
  385.6 14.5 %shard_map.218 = (bf16[768,1536]{1,0:T(8,128)(2,1)}, bf16[768,1536]{1,0:T(8,128)(2,1)}) custom-call(bf16[1024,768]{1,0:T(8,128)(2,1)} %get-tuple-element.167.refs_0_, bf16[1024,768]{1,0:T(8,128)(2,1)} %get-tuple-element.168.refs_1_, bf16[1024,768]{1,0:T(8,128)(2,1)} %bitcast.85, bf16[1024,768]{1,0:T(8,128)(2,1)} %bitcast.95, bf16[1024,768]{1,0:T(8,128)(2,1)} %bitcast.97, ...), custom_call_target="tpu_custom_call" | custom-call | flops 1 | bytes 1 | tf_op jit(solution)/shard_map/pallas_call | solution.py:481
  403.2 9.2 %shard_map.217 = (f32[1024,768]{1,0:T(8,128)}, f32[2,768]{1,0:T(2,128)}) custom-call(bf16[1024,768]{1,0:T(8,128)(2,1)} %bitcast.77, bf16[1024,768]{1,0:T(8,128)(2,1)} %bitcast.96, bf16[1024,768]{1,0:T(8,128)(2,1)} %bitcast.98, bf16[1024,768]{1,0:T(8,128)(2,1)} %bitcast.100, bf16[768,2304]{1,0:T(8,128)(2,1)} %refs_5_.1, bf16[768,2304]{1,0:T(8,128)(2,1)} %refs_5_.1, ...), custom_call_target="tpu_custom_call" | custom-call | flops 1 | bytes 1 | tf_op jit(solution)/shard_map/pallas_call | solution.py:553
  462.2 6.3 %collective-permute-start.16 = (bf16[24,1536]{1,0:T(8,128)(2,1)S(1)}, bf16[24,1536]{1,0:T(8,128)(2,1)S(1)}, u32[]{:S(2)}, u32[]{:S(2)}) collective-permute-start(bf16[24,1536]{1,0:T(8,128)(2,1)S(1)} %get-tuple-element.207), channel_id=1, source_target_pairs={{0,4},{1,5},{2,6},{3,7},{4,0},{5,1},{6,2},{7,3},{8,12},{9,13},{10,... | collective-permute-start | bytes 221192 | tf_op jit(solution)/shard_map/ppermute | solution.py:638
  495.4 8.2 %shard_map.220 = bf16[1024,768]{1,0:T(8,128)(2,1)} custom-call(s32[1,1024]{1,0:T(1,128)} %get-tuple-element.117.target_ref, f32[1024,768]{1,0:T(8,128)} %get-tuple-element.184.middle_ref, f32[1024,1]{1,0:T(8,128)} %get-tuple-element.185.gate_ref, bf16[2048,768]{1,0:T(8,128)(2,1)} %bitcast.93), custom_call_target="tpu_custom_call" | custom-call | flops 1 | bytes 1 | tf_op jit(solution)/shard_map/pallas_call | solution.py:553
  (206 shorter events, 180.7 us)
Async XLA Ops:
  0.6 40.0 %collective-permute-start = (bf16[1,1024,768]{2,1,0:T(8,128)(2,1)}, bf16[1,1024,768]{2,1,0:T(8,128)(2,1)}, u32[]{:S(2)}, u32[]{:S(2)}) collective-permute-start(bf16[1,1024,768]{2,1,0:T(8,128)(2,1)} %param.13), channel_id=1, source_target_pairs={{0,16},{1,17},{2,18},{3,19},{4,20},{5,21},{6,22},{7,23},{8,24},{9,... | collective-permute-start | bytes 4718600 | tf_op jit(solution)/shard_map/ppermute | solution.py:706
  26.2 65.3 %all-to-all-start = ((bf16[16,128,768]{2,1,0:T(8,128)(2,1)}), bf16[16,128,768]{2,1,0:T(8,128)(2,1)S(1)}, u32[]{:S(2)}, u32[]{:S(2)}) async-start(bf16[16,128,768]{2,1,0:T(8,128)(2,1)} %bitcast.94), calls=%async_computation | async-start | bytes 6291456 | tf_op jit(solution)/shard_map/all_to_all | solution.py:727
  97.3 47.7 %all-to-all-start.1 = ((bf16[16,64,768]{2,1,0:T(8,128)(2,1)}), bf16[16,64,768]{2,1,0:T(8,128)(2,1)}, u32[]{:S(2)}, u32[]{:S(2)}) async-start(bf16[16,64,768]{2,1,0:T(8,128)(2,1)} %bitcast.105), calls=%async_computation.1 | async-start | bytes 3145728 | tf_op jit(solution)/shard_map/all_to_all | solution.py:727
  145.0 41.1 %all-to-all-start.3 = ((bf16[16,64,768]{2,1,0:T(8,128)(2,1)}), bf16[16,64,768]{2,1,0:T(8,128)(2,1)S(1)}, u32[]{:S(2)}, u32[]{:S(2)}) async-start(bf16[16,64,768]{2,1,0:T(8,128)(2,1)} %bitcast.104), calls=%async_computation.3 | async-start | bytes 3145728 | tf_op jit(solution)/shard_map/all_to_all | solution.py:727
  186.0 41.2 %all-to-all-start.2 = ((bf16[16,64,768]{2,1,0:T(8,128)(2,1)}), bf16[16,64,768]{2,1,0:T(8,128)(2,1)}, u32[]{:S(2)}, u32[]{:S(2)}) async-start(bf16[16,64,768]{2,1,0:T(8,128)(2,1)} %bitcast.124), calls=%async_computation.2 | async-start | bytes 3145728 | tf_op jit(solution)/shard_map/all_to_all | solution.py:727
  227.2 44.8 %all-to-all-start.4 = ((bf16[16,64,768]{2,1,0:T(8,128)(2,1)}), bf16[16,64,768]{2,1,0:T(8,128)(2,1)S(1)}, u32[]{:S(2)}, u32[]{:S(2)}) async-start(bf16[16,64,768]{2,1,0:T(8,128)(2,1)} %bitcast.125), calls=%async_computation.4 | async-start | bytes 3145728 | tf_op jit(solution)/shard_map/all_to_all | solution.py:727
  245.6 65.7 %collective-permute-start.1 = (bf16[1536,768]{1,0:T(8,128)(2,1)}, bf16[1536,768]{1,0:T(8,128)(2,1)}, u32[]{:S(2)}, u32[]{:S(2)}) collective-permute-start(bf16[1536,768]{1,0:T(8,128)(2,1)} %add_convert_fusion.1), channel_id=1, source_target_pairs={{0,16},{16,0},{1,17},{17,1},{2,18},{18,2},{3,19},{19,3},{4,20},{20... | collective-permute-start | bytes 7077896 | tf_op jit(solution)/shard_map/ppermute | solution.py:825
  254.3 97.4 %collective-permute-start.2 = (bf16[768,1536]{1,0:T(8,128)(2,1)}, bf16[768,1536]{1,0:T(8,128)(2,1)}, u32[]{:S(2)}, u32[]{:S(2)}) collective-permute-start(bf16[768,1536]{1,0:T(8,128)(2,1)} %add_convert_fusion), channel_id=1, source_target_pairs={{0,16},{16,0},{1,17},{17,1},{2,18},{18,2},{3,19},{19,3},{4,20},{20... | collective-permute-start | bytes 7077896 | tf_op jit(solution)/shard_map/ppermute | solution.py:825
  286.8 97.0 %all-to-all-start.5 = ((bf16[16,128,768]{2,1,0:T(8,128)(2,1)}), bf16[16,128,768]{2,1,0:T(8,128)(2,1)S(1)}, u32[]{:S(2)}, u32[]{:S(2)}) async-start(bf16[16,128,768]{2,1,0:T(8,128)(2,1)} %bitcast.37), calls=%async_computation.5 | async-start | bytes 6291456 | tf_op jit(solution)/shard_map/all_to_all | solution.py:727
  311.3 72.5 %collective-permute-start.3 = (bf16[1,1024,768]{2,1,0:T(8,128)(2,1)}, bf16[1,1024,768]{2,1,0:T(8,128)(2,1)}, u32[]{:S(2)}, u32[]{:S(2)}) collective-permute-start(bf16[1,1024,768]{2,1,0:T(8,128)(2,1)} %bitcast.143), channel_id=1, source_target_pairs={{16,0},{17,1},{18,2},{19,3},{20,4},{21,5},{22,6},{23,7},{24,8},{25... | collective-permute-start | bytes 4718600 | tf_op jit(solution)/shard_map/ppermute | solution.py:709
  402.6 15.8 %collective-permute-start.8 = (bf16[384,1536]{1,0:T(8,128)(2,1)}, bf16[384,1536]{1,0:T(8,128)(2,1)S(1)}, u32[]{:S(2)}, u32[]{:S(2)}) collective-permute-start(bf16[384,1536]{1,0:T(8,128)(2,1)} %constant_dynamic-slice_fusion.1), channel_id=1, source_target_pairs={{0,1},{1,0},{2,3},{3,2},{4,5},{5,4},{6,7},{7,6},{8,9},{9,8},{10,11... | collective-permute-start | bytes 3538952 | tf_op jit(solution)/shard_map/ppermute | solution.py:638
  420.2 24.7 %collective-permute-start.10 = (bf16[96,1664]{1,0:T(8,128)(2,1)S(1)}, bf16[96,1664]{1,0:T(8,128)(2,1)S(1)}, u32[]{:S(2)}, u32[]{:S(2)}) collective-permute-start(bf16[96,1664]{1,0:T(8,128)(2,1)S(1)} %get-tuple-element.210), channel_id=1, source_target_pairs={{0,2},{1,3},{2,0},{3,1},{4,6},{5,7},{6,4},{7,5},{8,10},{9,11},{10,... | collective-permute-start | bytes 958472 | tf_op jit(solution)/shard_map/ppermute | solution.py:638
  422.0 23.0 %collective-permute-start.11 = (bf16[96,1664]{1,0:T(8,128)(2,1)S(1)}, bf16[96,1664]{1,0:T(8,128)(2,1)S(1)}, u32[]{:S(2)}, u32[]{:S(2)}) collective-permute-start(bf16[96,1664]{1,0:T(8,128)(2,1)S(1)} %get-tuple-element.211), channel_id=1, source_target_pairs={{0,16},{1,17},{2,18},{3,19},{4,20},{5,21},{6,22},{7,23},{8,24},{9,... | collective-permute-start | bytes 958472 | tf_op jit(solution)/shard_map/ppermute | solution.py:638
  425.7 12.7 %collective-permute-start.5 = (bf16[96,1536]{1,0:T(8,128)(2,1)S(1)}, bf16[96,1536]{1,0:T(8,128)(2,1)S(1)}, u32[]{:S(2)}, u32[]{:S(2)}) collective-permute-start(bf16[96,1536]{1,0:T(8,128)(2,1)S(1)} %get-tuple-element.213), channel_id=1, source_target_pairs={{0,2},{1,3},{2,0},{3,1},{4,6},{5,7},{6,4},{7,5},{8,10},{9,11},{10,... | collective-permute-start | bytes 884744 | tf_op jit(solution)/shard_map/ppermute | solution.py:638
  425.9 13.5 %collective-permute-start.6 = (bf16[96,1536]{1,0:T(8,128)(2,1)S(1)}, bf16[96,1536]{1,0:T(8,128)(2,1)S(1)}, u32[]{:S(2)}, u32[]{:S(2)}) collective-permute-start(bf16[96,1536]{1,0:T(8,128)(2,1)S(1)} %get-tuple-element.215), channel_id=1, source_target_pairs={{0,16},{1,17},{2,18},{3,19},{4,20},{5,21},{6,22},{7,23},{8,24},{9,... | collective-permute-start | bytes 884744 | tf_op jit(solution)/shard_map/ppermute | solution.py:638
  426.3 18.5 %collective-permute-start.7 = (bf16[96,1536]{1,0:T(8,128)(2,1)S(1)}, bf16[96,1536]{1,0:T(8,128)(2,1)S(1)}, u32[]{:S(2)}, u32[]{:S(2)}) collective-permute-start(bf16[96,1536]{1,0:T(8,128)(2,1)S(1)} %get-tuple-element.214), channel_id=1, source_target_pairs={{0,18},{1,19},{2,16},{3,17},{4,22},{5,23},{6,20},{7,21},{8,26},{9,... | collective-permute-start | bytes 884744 | tf_op jit(solution)/shard_map/ppermute | solution.py:638
  438.4 12.5 %collective-permute-start.12 = (bf16[96,1664]{1,0:T(8,128)(2,1)S(1)}, bf16[96,1664]{1,0:T(8,128)(2,1)S(1)}, u32[]{:S(2)}, u32[]{:S(2)}) collective-permute-start(bf16[96,1664]{1,0:T(8,128)(2,1)S(1)} %get-tuple-element.212), channel_id=1, source_target_pairs={{0,18},{1,19},{2,16},{3,17},{4,22},{5,23},{6,20},{7,21},{8,26},{9,... | collective-permute-start | bytes 958472 | tf_op jit(solution)/shard_map/ppermute | solution.py:638
  455.6 14.0 %collective-permute-start.19 = (bf16[24,1664]{1,0:T(8,128)(2,1)S(1)}, bf16[24,1664]{1,0:T(8,128)(2,1)S(1)}, u32[]{:S(2)}, u32[]{:S(2)}) collective-permute-start(bf16[24,1664]{1,0:T(8,128)(2,1)S(1)} %get-tuple-element.216), channel_id=1, source_target_pairs={{0,4},{1,5},{2,6},{3,7},{4,0},{5,1},{6,2},{7,3},{8,12},{9,13},{10,... | collective-permute-start | bytes 239624 | tf_op jit(solution)/shard_map/ppermute | solution.py:638
  456.3 14.7 %collective-permute-start.20 = (bf16[24,1664]{1,0:T(8,128)(2,1)S(1)}, bf16[24,1664]{1,0:T(8,128)(2,1)S(1)}, u32[]{:S(2)}, u32[]{:S(2)}) collective-permute-start(bf16[24,1664]{1,0:T(8,128)(2,1)S(1)} %get-tuple-element.218), channel_id=1, source_target_pairs={{0,8},{1,9},{2,10},{3,11},{4,12},{5,13},{6,14},{7,15},{8,0},{9,1},... | collective-permute-start | bytes 239624 | tf_op jit(solution)/shard_map/ppermute | solution.py:638
  481.6 30.2 %collective-permute-start.28 = (bf16[96,1664]{1,0:T(8,128)(2,1)S(1)}, bf16[96,1664]{1,0:T(8,128)(2,1)S(1)}, u32[]{:S(2)}, u32[]{:S(2)}) collective-permute-start(bf16[96,1664]{1,0:T(8,128)(2,1)S(1)} %constant_dynamic-update-slice_fusion.12), channel_id=1, source_target_pairs={{0,2},{1,3},{2,0},{3,1},{4,6},{5,7},{6,4},{7,5},{8,10},{9,11},{10,... | collective-permute-start | bytes 958472 | tf_op jit(solution)/shard_map/ppermute | solution.py:638
  483.1 28.8 %collective-permute-start.29 = (bf16[96,1664]{1,0:T(8,128)(2,1)S(1)}, bf16[96,1664]{1,0:T(8,128)(2,1)S(1)}, u32[]{:S(2)}, u32[]{:S(2)}) collective-permute-start(bf16[96,1664]{1,0:T(8,128)(2,1)S(1)} %constant_dynamic-update-slice_fusion.12), channel_id=1, source_target_pairs={{0,16},{1,17},{2,18},{3,19},{4,20},{5,21},{6,22},{7,23},{8,24},{9,... | collective-permute-start | bytes 958472 | tf_op jit(solution)/shard_map/ppermute | solution.py:638
  483.6 28.3 %collective-permute-start.30 = (bf16[96,1664]{1,0:T(8,128)(2,1)S(1)}, bf16[96,1664]{1,0:T(8,128)(2,1)S(1)}, u32[]{:S(2)}, u32[]{:S(2)}) collective-permute-start(bf16[96,1664]{1,0:T(8,128)(2,1)S(1)} %constant_dynamic-update-slice_fusion.12), channel_id=1, source_target_pairs={{0,18},{1,19},{2,16},{3,17},{4,22},{5,23},{6,20},{7,21},{8,26},{9,... | collective-permute-start | bytes 958472 | tf_op jit(solution)/shard_map/ppermute | solution.py:638
  485.2 18.3 %collective-permute-start.25 = (bf16[96,1536]{1,0:T(8,128)(2,1)S(1)}, bf16[96,1536]{1,0:T(8,128)(2,1)S(1)}, u32[]{:S(2)}, u32[]{:S(2)}) collective-permute-start(bf16[96,1536]{1,0:T(8,128)(2,1)S(1)} %constant_dynamic-update-slice_fusion.16), channel_id=1, source_target_pairs={{0,2},{1,3},{2,0},{3,1},{4,6},{5,7},{6,4},{7,5},{8,10},{9,11},{10,... | collective-permute-start | bytes 884744 | tf_op jit(solution)/shard_map/ppermute | solution.py:638
  486.6 19.2 %collective-permute-start.26 = (bf16[96,1536]{1,0:T(8,128)(2,1)S(1)}, bf16[96,1536]{1,0:T(8,128)(2,1)S(1)}, u32[]{:S(2)}, u32[]{:S(2)}) collective-permute-start(bf16[96,1536]{1,0:T(8,128)(2,1)S(1)} %constant_dynamic-update-slice_fusion.16), channel_id=1, source_target_pairs={{0,16},{1,17},{2,18},{3,19},{4,20},{5,21},{6,22},{7,23},{8,24},{9,... | collective-permute-start | bytes 884744 | tf_op jit(solution)/shard_map/ppermute | solution.py:638
  (45 other events, 432.3 us)

commit v3 on v2

--- a/solution.py
+++ b/solution.py
@@ -174,12 +174,30 @@
         attend(True)
 
 
+def probs_kernel(me_ref, low_ref, q_ref, k_ref, lse_ref, start_ref, out_ref, *, tile, block_len, own):
+    row, block = pl.program_id(0), pl.program_id(2)
+    me = me_ref[0]
+    low = low_ref[row, block]
+    queries = (q_ref[0].astype(f32) * HEAD_DIM**-0.5).astype(bf16)
+    starts = start_ref[0]
+    for at, size in pieces_of(k_ref.shape[1], min(512 if own else 1024, block_len)):
+
+        @pl.when(needed(at, size, block, low, me, block_len, tile, own))
+        def piece(at=at, size=size):
+            rows = slice(at, at + size)
+            mask = mask_of(at, size, block, me, block_len, tile, starts, own, True)
+            for head in range(GROUP):
+                query = head_of_pair(queries[:, pair_of(head)], head)
+                scores = dot_nt(k_ref[0, rows, pair_of(head)], query) - lse_ref[0, 0, head : head + 1, :]
+                out_ref[0, head, rows, :] = jnp.exp(jnp.where(mask, scores, NEG)).astype(bf16)
+
+
 def grad_kernel(me_ref, low_ref, *refs, tile, block_len, own):
-    q_ref, k_ref, v_ref, go_ref, ctx_ref, lse_ref, start_ref = refs[:7]
+    q_ref, k_ref, v_ref, go_ref, ctx_ref, probs_ref = refs[:6]
     if own:
-        dq_in, dq_out, dk_out, dv_out = refs[7:11]
+        dq_in, dq_out, dk_out, dv_out = refs[6:10]
     else:
-        dq_out, dk_out, dv_out = refs[7:10]
+        dq_out, dk_out, dv_out = refs[6:9]
     kt, dq, dk, dv = refs[-4:]
     row, block = pl.program_id(0), pl.program_id(2)
     me = me_ref[0]
@@ -200,7 +218,6 @@
 
     queries = (q_ref[0].astype(f32) * scale).astype(bf16)
     go = go_ref[0]
-    starts = start_ref[0]
     product = go.astype(f32) * ctx_ref[0].astype(f32)
     head_row = lax.broadcasted_iota(jnp.int32, (8, LANES), 0)
     head_lane = lax.broadcasted_iota(jnp.int32, (8, LANES), 1) // HEAD_DIM
@@ -213,23 +230,20 @@
         @pl.when(needed(at, size, block, low, me, block_len, tile, own))
         def piece(at=at, size=size):
             rows = slice(at, at + size)
-            mask = mask_of(at, size, block, me, block_len, tile, starts, own, True)
             for first in range(0, GROUP, 2):
                 pair = pair_of(first)
-                keys, values = k_ref[0, rows, pair], v_ref[0, rows, pair]
+                values = v_ref[0, rows, pair]
                 all_probs, all_grads, all_queries, all_go = [], [], [], []
                 for head in (first, first + 1):
-                    query = head_of_pair(queries[:, pair], head)
                     head_go = head_of_pair(go[:, pair], head)
-                    scores = dot_nt(keys, query) - lse_ref[0, 0, head : head + 1, :]
-                    probs = jnp.exp(jnp.where(mask, scores, NEG))
+                    probs = probs_ref[0, head, rows, :]
                     prob_grad = dot_nt(values, head_go)
-                    score_grad = (probs * (prob_grad - inner[head])).astype(bf16)
+                    score_grad = (probs.astype(f32) * (prob_grad - inner[head])).astype(bf16)
                     lanes = slice(head * HEAD_DIM, (head + 1) * HEAD_DIM)
                     dq[lanes] += dot(kt[lanes, rows], score_grad)
-                    all_probs.append(probs.astype(bf16))
+                    all_probs.append(probs)
                     all_grads.append(score_grad)
-                    all_queries.append(query)
+                    all_queries.append(head_of_pair(queries[:, pair], head))
                     all_go.append(head_go)
                 dv[rows, pair] += dot(jnp.concatenate(all_probs, 1), jnp.concatenate(all_go, 0))
                 dk[rows, pair] += dot(jnp.concatenate(all_grads, 1), jnp.concatenate(all_queries, 0))
@@ -310,13 +324,30 @@
         total = pltpu.VMEM((length, LANES), f32)
         return [pltpu.VMEM((LANES, length), bf16), pltpu.VMEM((LANES, self.tile), f32), total, total]
 
-    def backward_other(self, joint, other, grad, context, lse):
+    def probs_spec(self, length):
+        return pl.BlockSpec((1, GROUP, length, self.tile), lambda r, g, b, *_: (r, g, 0, b))
+
+    def probs(self, joint, keys, lse, own):
+        length = keys.shape[1]
+        shape = (self.rows, self.groups * GROUP, length, self.block_len)
+        (probs,) = self.call(
+            functools.partial(probs_kernel, own=own),
+            SHORT,
+            [self.queries(), self.keys(length, 1 if own else 0), self.stat(), self.row_starts()],
+            [self.probs_spec(length)],
+            [jax.ShapeDtypeStruct(shape, bf16)],
+            [],
+            (joint, keys, lse, self.start_row),
+        )
+        return probs
+
+    def backward_other(self, joint, other, grad, context, probs):
         size, length = self.block_len, other.shape[1]
         return self.call(
             functools.partial(grad_kernel, own=False),
             SHORT,
             [self.queries(), self.keys(length, 0), self.keys(length, 1)]
-            + [self.queries(), self.queries(), self.stat(), self.row_starts()],
+            + [self.queries(), self.queries(), self.probs_spec(length)],
             [self.turned(), self.keys(length, 0), self.keys(length, 0)],
             [
                 jax.ShapeDtypeStruct((self.rows, self.width, size), f32),
@@ -324,20 +355,20 @@
                 self.shape(length),
             ],
             self.grad_scratch(length),
-            (joint, other, other, grad, context, lse, self.start_row),
+            (joint, other, other, grad, context, probs),
         )
 
-    def backward_own(self, joint, grad, context, lse, dq_state):
+    def backward_own(self, joint, grad, context, probs, dq_state):
         size = self.block_len
         return self.call(
             functools.partial(grad_kernel, own=True),
             LONG,
             [self.queries(), self.keys(size, 1), self.keys(size, 2)]
-            + [self.queries(), self.queries(), self.stat(), self.row_starts(), self.turned()],
+            + [self.queries(), self.queries(), self.probs_spec(size), self.turned()],
             [self.queries(), self.keys(size, 0), self.keys(size, 0)],
             [self.shape(size)] * 3,
             self.grad_scratch(size),
-            (joint, joint, joint, grad, context, lse, self.start_row, dq_state),
+            (joint, joint, joint, grad, context, probs, dq_state),
         )
 
 
@@ -459,31 +490,27 @@
     )
 
 
-def weight_grads_kernel(*refs):
-    early_ref, late_ref = refs[-2:]
-    width = early_ref.shape[1] // 2
-    own, other, context = [turned(ref[...]) for ref in refs[:3]]
-    dq, dk, dv, dk_other, dv_other, attn_grad = [ref[...] for ref in refs[3:9]]
-    early_ref[:, :width] = (dot(own, dk) + dot(other, dk_other)).astype(bf16)
-    early_ref[:, width:] = (dot(own, dv) + dot(other, dv_other)).astype(bf16)
-    late_ref[:, :width] = dot(own, dq).astype(bf16)
-    late_ref[:, width:] = dot(context, attn_grad).astype(bf16)
-
-
-def weight_grads(own, other, context, dq, dk, dv, dk_other, dv_other, attn_grad):
-    width = own.shape[1]
+def weight_grads_kernel(*refs, count, blocks):
+    lefts = [turned(ref[...]) for ref in refs[:count]]
+    rights, out_ref = refs[count:-1], refs[-1]
+    width = out_ref.shape[1] // len(blocks)
+    for at, pairs in enumerate(blocks):
+        total = sum(dot(lefts[left], rights[right][...]) for left, right in pairs)
+        out_ref[:, at * width : (at + 1) * width] = total.astype(bf16)
+
+
+def weight_grads(lefts, rights, blocks):
+    width = lefts[0].shape[1]
     tile = tile_of(width, 256)
-    lefts, rights = [own, other, context], [dq, dk, dv, dk_other, dv_other, attn_grad]
     specs = [pl.BlockSpec((left.shape[0], tile), lambda i: (0, i)) for left in lefts]
     specs += [pl.BlockSpec(right.shape, lambda i: (0, 0), pipeline_mode=pl.Buffered(1)) for right in rights]
-    shape = jax.ShapeDtypeStruct((width, 2 * width), bf16)
-    spec = pl.BlockSpec((tile, 2 * width), lambda i: (i, 0))
+    columns = len(blocks) * rights[0].shape[1]
     return pl.pallas_call(
-        weight_grads_kernel,
+        functools.partial(weight_grads_kernel, count=len(lefts), blocks=blocks),
         grid=(width // tile,),
         in_specs=specs,
-        out_specs=[spec, spec],
-        out_shape=[shape, shape],
+        out_specs=pl.BlockSpec((tile, columns), lambda i: (i, 0)),
+        out_shape=jax.ShapeDtypeStruct((width, columns), bf16),
         compiler_params=params(),
         cost_estimate=SHORT,
     )(*lefts, *rights)
@@ -781,6 +808,9 @@
     )
     normed_two, grads_arrived = lax.optimization_barrier((normed_two, grads_arrived))
     placed = [place(target_halves_row - h * half_slots, normed_two, half_slots) for h in range(halves)]
+    placed[0], lse = lax.optimization_barrier((placed[0], lse))
+    probs_own, probs_other = attention.probs(joint, joint, lse, True), attention.probs(joint, other, lse, False)
+    placed[-1], probs_own, probs_other = lax.optimization_barrier((placed[-1], probs_own, probs_other))
     arrived = [exchange(part).reshape(peers, local_experts, rows * depth, width) for part in placed]
 
     own_experts = lax.axis_index("wide") * local_experts
@@ -856,7 +886,7 @@
     context_grad, output = lax.optimization_barrier((context_grad, output))
     produced = exchange(output).reshape(halves * half_slots, width)
     context_grad = context_grad.reshape(rows, block_len, width)
-    dq_state, dk_other, dv_other = attention.backward_other(joint, other, context_grad, context, lse)
+    dq_state, dk_other, dv_other = attention.backward_other(joint, other, context_grad, context, probs_other)
     dk_other, dv_other = dk_other.reshape(-1, width), dv_other.reshape(-1, width)
     other_len = other_flat.shape[0]
     other_grad, other_sums = by_tokens(
@@ -869,14 +899,16 @@
     other_grad = other_grad.reshape(rows, blocks - 1, block_len, width)
     context_grad, returned, down_got = lax.optimization_barrier((context_grad, other_grad, down_got))
     returned = [behind(returned[:, shift - 1], shift) for shift in shifts]
-    dq, dk, dv = attention.backward_own(joint, context_grad, context, lse, dq_state)
+    dq, dk, dv = attention.backward_own(joint, context_grad, context, probs_own, dq_state)
     dq, dk, dv = [part.reshape(flat, width) for part in (dq, dk, dv)]
-    tied = (dq, dk, dv, produced, down_got, up_got, returned)
-    dq, dk, dv, produced, down_got, up_got, returned = lax.optimization_barrier(tied)
-
-    early, late = weight_grads(
-        normed_one, normed_other, context_flat, dq, dk, dv, dk_other, dv_other, attn_grad
+    tied = (dq, dk, dv, produced, down_got, up_got)
+    dq, dk, dv, produced, down_got, up_got = lax.optimization_barrier(tied)
+
+    early = weight_grads(
+        [normed_one, normed_other], [dk, dv, dk_other, dv_other], (((0, 0), (1, 2)), ((0, 1), (1, 3)))
     )
+    late = weight_grads([normed_one, context_flat], [dq, attn_grad], (((0, 0),), ((1, 1),)))
+    dq, dk, dv, returned = lax.optimization_barrier((dq, dk, dv, returned))
     own_grad, own_sums = by_tokens(
         input_grad_kernel,
         flat,
@@ -888,22 +920,28 @@
 
     stages = stages_of(lax.axis_size("wide"), blocks)
     steps = list(zip(stages, places_of(stages)))
-    early, late, vectors = reduce_step([early, late, vectors], *steps[0])
+    early = [early]
+    for step in steps:
+        early = reduce_step(early, *step)
+    early = [x.astype(bf16) for x in early]
+    for step in reversed(steps):
+        early = gather_step(early, *step)
+
+    late = reduce_step([late, vectors], *steps[0])
+    late = [jnp.concatenate(late, 1)]
     rest = (down_own, up_own, down_got, up_got)
-    rest, early = lax.optimization_barrier((rest, early))
+    rest, late = lax.optimization_barrier((rest, late))
     down_own, up_own, down_got, up_got = rest
     down_share = summed_shares(down_own, down_got)
     up_share = summed_shares(up_own, up_got)
-    shares = [early, jnp.concatenate([late, vectors], 1)]
     for step in steps[1:-1]:
-        shares = reduce_step(shares, *step)
-    down_share, up_share, shares = lax.optimization_barrier((down_share, up_share, shares))
-    shares = reduce_step(shares, *steps[-1])
-    shares = [x.astype(bf16) for x in shares]
-
-    shares = gather_step(shares, *steps[-1])
+        late = reduce_step(late, *step)
+    down_share, up_share, late = lax.optimization_barrier((down_share, up_share, late))
+    late = reduce_step(late, *steps[-1])
+    late = [x.astype(bf16) for x in late]
+    late = gather_step(late, *steps[-1])
     rest = (middle, produced, own_grad, returned)
-    rest, shares = lax.optimization_barrier((rest, shares))
+    rest, late = lax.optimization_barrier((rest, late))
     middle, produced, own_grad, returned = rest
     total_grad = own_grad
     for part in returned:
@@ -918,9 +956,9 @@
         [low_shape],
     )
     for step in reversed(steps[1:-1]):
-        shares = gather_step(shares, *step)
-    stream_grad, result, shares = lax.optimization_barrier((stream_grad, result, shares))
-    in_sum, out_sum, vectors = finish(*gather_step(shares, *steps[0]))
+        late = gather_step(late, *step)
+    stream_grad, result, late = lax.optimization_barrier((stream_grad, result, late))
+    in_sum, out_sum, vectors = finish(*early, *gather_step(late, *steps[0]))
 
     out_shape = (rows, block_len, width)
     return (

time: 533 us -> 507 us (0.951)
  waiting for transfers between devices: 104 us -> 75.3 us
  Pallas kernels: 230 us -> 243 us
  starting transfers between devices: 103 us -> 96.9 us
    all_to_all x6, waiting for transfers between devices: 45.8 us -> 28.5 us  [exchange(): lax.all_to_all(array.reshape(experts, -1, width), 'wide', split_axis=0, c...]
    ppermute x1, waiting for transfers between devices: 32.2 us -> 19.5 us  [behind(): lax.ppermute(array, 'blk', [(i + shift, i) for i in range(blocks - shift)])]
    pallas_call x3 -> x5, Pallas kernels: 74.1 us -> 84.1 us  [call(): pl.pallas_call(functools.partial(kernel, tile=self.tile, block_len=self.b...]
    ppermute x2, waiting for transfers between devices: 0.01 us -> 8.14 us  [send_shares(): lax.ppermute(part, 'blk', [(i, (i + shift) % blocks) for i in range(block...]
    ppermute x29, waiting for transfers between devices: 25.6 us -> 19.2 us  [swap(): lax.ppermute(array, ('blk', 'wide'), [(i, i ^ mask) for i in range(total)])]
    ppermute x29, starting transfers between devices: 38.5 us -> 32.6 us  [swap(): lax.ppermute(array, ('blk', 'wide'), [(i, i ^ mask) for i in range(total)])]
    pallas_call x1 -> x2, Pallas kernels: 14.5 us -> 17.8 us  [weight_grads(): pl.pallas_call(functools.partial(weight_grads_kernel, count=len(lefts), b...]
  transfers between devices with their start and end apart: 39 -> 39, of which waited for: 13 -> 16; matrix products, arithmetic and copies ran while one was open for 15% -> 15% of each run, Pallas kernels for 39% -> 46%
where the time goes in v3:
time: 507 us; the launch traced here: 501 us
  Pallas kernels  243 us (48%)
  starting transfers between devices  96.9 us (19%)
  waiting for transfers between devices  75.3 us (15%)
  matrix products  35 us (7%)
  local copies, waits for them, and re-layouts  25.8 us (5%)
  other arithmetic  23 us (5%)
    pallas_call x5, Pallas kernels, call(): pl.pallas_call(functools.partial(kernel, tile=self.tile, block_len=self.b...  84.1 us
    pallas_call x7, Pallas kernels, by_tokens(): pl.pallas_call(kernel, grid=(flat // tile,), in_specs=specs, out_specs=[c...  61.2 us
    all_to_all x6, starting transfers between devices, exchange(): lax.all_to_all(array.reshape(experts, -1, width), 'wide', split_axis=0, c...  55.2 us
    pallas_call x2, Pallas kernels, run_expert(): pl.pallas_call(expert_kernel, grid=(rows // tile,), in_specs=in_specs, ou...  54.6 us
    ppermute x29, starting transfers between devices, swap(): lax.ppermute(array, ('blk', 'wide'), [(i, i ^ mask) for i in range(total)])  32.6 us
    all_to_all x6, waiting for transfers between devices, exchange(): lax.all_to_all(array.reshape(experts, -1, width), 'wide', split_axis=0, c...  28.5 us
    ppermute x1, waiting for transfers between devices, behind(): lax.ppermute(array, 'blk', [(i + shift, i) for i in range(blocks - shift)])  19.5 us
    ppermute x29, waiting for transfers between devices, swap(): lax.ppermute(array, ('blk', 'wide'), [(i, i ^ mask) for i in range(total)])  19.2 us
  transfers between devices with their start and end apart: 39, of which 16 were waited for; matrix products, arithmetic and copies ran while one was open for 15% of the time, Pallas kernels for 46%

profile of v3, /device:TPU:0, one launch (start us, length us, event | category | flops | bytes accessed | tf_op | source)
XLA Modules:
  0.0 500.8 jit_solution(18162975326680359526)
XLA Ops:
  18.8 7.3 %shard_map.208 = bf16[2048,768]{1,0:T(8,128)(2,1)} custom-call(s32[1,1024]{1,0:T(1,128)} %get-tuple-element.120.target_ref, bf16[1024,768]{1,0:T(8,128)(2,1)} %bitcast.106), custom_call_target="tpu_custom_call" | custom-call | flops 1 | bytes 1 | tf_op jit(solution)/shard_map/pallas_call | solution.py:385
  32.1 8.5 %shard_map.204 = (bf16[1024,768]{1,0:T(8,128)(2,1)}, bf16[1024,2304]{1,0:T(8,128)(2,1)}) custom-call(bf16[1024,768]{1,0:T(8,128)(2,1)} %bitcast.75, f32[1,768]{1,0:T(1,128)} %reshape.387.gain_ref, f32[1,768]{1,0:T(1,128)} %reshape.388.shift_ref, bf16[768,2304]{1,0:T(8,128)(2,1)} %refs_5_.1, bf16[768,2304]{1,0:T(8,128)(2,1)} %refs_5_.1, bf16[768,2304]{1,0:T(8,128)(2,1)} %refs_5_.1), custom_call_target="tpu_custom_call" | custom-call | flops 1 | bytes 1 | tf_op jit(solution)/shard_map/pallas_call | solution.py:580
  40.6 7.1 %shard_map.205 = (bf16[1024,768]{1,0:T(8,128)(2,1)}, bf16[1024,1536]{1,0:T(8,128)(2,1)}) custom-call(bf16[1024,768]{1,0:T(8,128)(2,1)} %bitcast.13.tokens_ref, f32[1,768]{1,0:T(1,128)} %reshape.387.gain_ref, f32[1,768]{1,0:T(1,128)} %reshape.388.shift_ref, bf16[768,2304]{1,0:T(8,128)(2,1)} %refs_5_.1, bf16[768,2304]{1,0:T(8,128)(2,1)} %refs_5_.1), custom_call_target="tpu_custom_call" | custom-call | flops 1 | bytes 1 | tf_op jit(solution)/shard_map/pallas_call | solution.py:580
  47.7 20.0 %shard_map.206 = (bf16[1,1024,768]{2,1,0:T(8,128)(2,1)}, f32[1,3,4,1024]{3,2,1,0:T(4,128)}) custom-call(s32[1]{0:T(128)} %bitcast.10.me_ref, s32[1,2]{1,0:T(1,128)} %slice.15.low_ref, bf16[1,1024,2304]{2,1,0:T(8,128)(2,1)} %bitcast.78, bf16[1,1024,2304]{2,1,0:T(8,128)(2,1)} %bitcast.79, bf16[1,1024,2304]{2,1,0:T(8,128)(2,1)} %bitcast.80, ...), custom_call_target="tpu_custom_call" | custom-call | flops 99999997952 | bytes 1 | tf_op jit(solution)/shard_map/pallas_call | solution.py:291
  67.8 7.5 %shard_map.207 = (f32[1024,768]{1,0:T(8,128)}, bf16[1024,768]{1,0:T(8,128)(2,1)}, f32[1024,1]{1,0:T(8,128)}) custom-call(bf16[1024,768]{1,0:T(8,128)(2,1)} %bitcast.99, bf16[1024,768]{1,0:T(8,128)(2,1)} %bitcast.76, s32[1,1024]{1,0:T(1,128)} %bitcast.136, bf16[768,768]{1,0:T(8,128)(2,1)} %weight_ref.3, f32[1,768]{1,0:T(1,128)} %reshape.389.gain_ref, ...), custom_call_target="tpu_custom_call" | custom-call | flops 1 | bytes 1 | tf_op jit(solution)/shard_map/pallas_call | solution.py:580
  75.3 16.2 %all-to-all-done = bf16[16,128,768]{2,1,0:T(8,128)(2,1)S(1)} async-done(((bf16[16,128,768]{2,1,0:T(8,128)(2,1)}), bf16[16,128,768]{2,1,0:T(8,128)(2,1)S(1)}, u32[]{:S(2)}, u32[]{:S(2)}) %all-to-all-start) | async-done | bytes 3145760 | tf_op jit(solution)/shard_map/all_to_all | solution.py:754
  97.3 15.5 %all-to-all-start.1 = ((bf16[16,64,768]{2,1,0:T(8,128)(2,1)}), bf16[16,64,768]{2,1,0:T(8,128)(2,1)}, u32[]{:S(2)}, u32[]{:S(2)}) async-start(bf16[16,64,768]{2,1,0:T(8,128)(2,1)} %bitcast.110), calls=%async_computation.1 | async-start | bytes 3145728 | tf_op jit(solution)/shard_map/all_to_all | solution.py:754
  113.4 10.5 %shard_map.213.refs_5_ = bf16[1,12,1024,1024]{3,2,1,0:T(8,128)(2,1)} custom-call(s32[1]{0:T(128)} %bitcast.10.me_ref, s32[1,2]{1,0:T(1,128)} %slice.15.low_ref, bf16[1,1024,2304]{2,1,0:T(8,128)(2,1)} %bitcast.81, bf16[1,1024,1536]{2,1,0:T(8,128)(2,1)} %bitcast.92, f32[1,3,4,1024]{3,2,1,0:T(4,128)} %get-tuple-element.129.lse_ref, s32[1,1,1024]{2,1,0:T(1,128)} %bitcast.139), custom_call_target="tpu_custom_call" | custom-call | flops 1 | bytes 1 | tf_op jit(solution)/shard_map/pallas_call | solution.py:291
  123.9 12.9 %shard_map.212.refs_5_ = bf16[1,12,1024,1024]{3,2,1,0:T(8,128)(2,1)} custom-call(s32[1]{0:T(128)} %bitcast.10.me_ref, s32[1,2]{1,0:T(1,128)} %slice.15.low_ref, bf16[1,1024,2304]{2,1,0:T(8,128)(2,1)} %bitcast.82, bf16[1,1024,2304]{2,1,0:T(8,128)(2,1)} %bitcast.83, f32[1,3,4,1024]{3,2,1,0:T(4,128)} %get-tuple-element.129.lse_ref, s32[1,1,1024]{2,1,0:T(1,128)} %bitcast.140), custom_call_target="tpu_custom_call" | custom-call | flops 1 | bytes 1 | tf_op jit(solution)/shard_map/pallas_call | solution.py:291
  144.8 9.1 %all-to-all-start.3 = ((bf16[16,64,768]{2,1,0:T(8,128)(2,1)}), bf16[16,64,768]{2,1,0:T(8,128)(2,1)S(1)}, u32[]{:S(2)}, u32[]{:S(2)}) async-start(bf16[16,64,768]{2,1,0:T(8,128)(2,1)} %bitcast.109), calls=%async_computation.3 | async-start | bytes 3145728 | tf_op jit(solution)/shard_map/all_to_all | solution.py:754
  155.2 27.3 %shard_map.210 = (bf16[16,2,64,768]{3,2,1,0:T(8,128)(2,1)}, bf16[1024,768]{1,0:T(8,128)(2,1)}, bf16[1024,3072]{1,0:T(8,128)(2,1)}, bf16[1024,3072]{1,0:T(8,128)(2,1)}, bf16[1024,768]{1,0:T(8,128)(2,1)}) custom-call(bf16[1024,768]{1,0:T(8,128)(2,1)} %bitcast.19.refs_0_, bf16[16,2,64,768]{3,2,1,0:T(8,128)(2,1)} %bitcast.88, bf16[768,3072]{1,0:T(8,128)(2,1)} %bitcast.95, ...), custom_call_target="tpu_custom_call" | custom-call | flops 1 | bytes 1 | tf_op jit(solution)/shard_map/pallas_call | solution.py:635
  185.9 9.3 %all-to-all-start.2 = ((bf16[16,64,768]{2,1,0:T(8,128)(2,1)}), bf16[16,64,768]{2,1,0:T(8,128)(2,1)}, u32[]{:S(2)}, u32[]{:S(2)}) async-start(bf16[16,64,768]{2,1,0:T(8,128)(2,1)} %bitcast.128), calls=%async_computation.2 | async-start | bytes 3145728 | tf_op jit(solution)/shard_map/all_to_all | solution.py:754
  196.3 27.3 %shard_map.214 = (bf16[16,2,64,768]{3,2,1,0:T(8,128)(2,1)}, bf16[1024,768]{1,0:T(8,128)(2,1)}, bf16[1024,3072]{1,0:T(8,128)(2,1)}, bf16[1024,3072]{1,0:T(8,128)(2,1)}, bf16[1024,768]{1,0:T(8,128)(2,1)}) custom-call(bf16[1024,768]{1,0:T(8,128)(2,1)} %bitcast.101, bf16[16,2,64,768]{3,2,1,0:T(8,128)(2,1)} %bitcast.89, ...), custom_call_target="tpu_custom_call", output_to_operand_aliasing={{0}: (5, {})} | custom-call | flops 1 | bytes 1 | tf_op jit(solution)/shard_map/pallas_call | solution.py:635
  227.3 9.1 %all-to-all-start.4 = ((bf16[16,64,768]{2,1,0:T(8,128)(2,1)}), bf16[16,64,768]{2,1,0:T(8,128)(2,1)S(1)}, u32[]{:S(2)}, u32[]{:S(2)}) async-start(bf16[16,64,768]{2,1,0:T(8,128)(2,1)} %bitcast.129), calls=%async_computation.4 | async-start | bytes 3145728 | tf_op jit(solution)/shard_map/all_to_all | solution.py:754
  273.2 13.6 %shard_map.215 = (f32[1024,768]{1,0:T(8,128)}, bf16[1024,768]{1,0:T(8,128)(2,1)}, bf16[1024,768]{1,0:T(8,128)(2,1)}, f32[2,768]{1,0:T(2,128)}) custom-call(s32[1,1024]{1,0:T(1,128)} %add_add_fusion.target_ref, f32[1024,768]{1,0:T(8,128)} %get-tuple-element.191.middle_ref, bf16[1024,768]{1,0:T(8,128)(2,1)} %bitcast.107, f32[1,768]{1,0:T(1,128)} %reshape.389.gain_ref, ...), custom_call_target="tpu_custom_call" | custom-call | flops 1 | bytes 1 | tf_op jit(solution)/shard_map/pallas_call | solution.py:580
  293.1 15.6 %shard_map.216 = (f32[1,768,1024]{2,1,0:T(8,128)}, bf16[1,1024,768]{2,1,0:T(8,128)(2,1)}, bf16[1,1024,768]{2,1,0:T(8,128)(2,1)}) custom-call(s32[1]{0:T(128)} %bitcast.10.me_ref, s32[1,2]{1,0:T(1,128)} %slice.15.low_ref, bf16[1,1024,2304]{2,1,0:T(8,128)(2,1)} %bitcast.84, bf16[1,1024,1536]{2,1,0:T(8,128)(2,1)} %bitcast.93, bf16[1,1024,1536]{2,1,0:T(8,128)(2,1)} %bitcast.94, ...), custom_call_target="tpu_custom_call" | custom-call | flops 1 | bytes 1 | tf_op jit(solution)/shard_map/pallas_call | solution.py:291
  308.7 7.4 %shard_map.217 = (bf16[1024,768]{1,0:T(8,128)(2,1)}, f32[2,768]{1,0:T(2,128)}) custom-call(bf16[1024,768]{1,0:T(8,128)(2,1)} %bitcast.13.tokens_ref, bf16[1024,768]{1,0:T(8,128)(2,1)} %bitcast.117, bf16[1024,768]{1,0:T(8,128)(2,1)} %bitcast.119, bf16[768,2304]{1,0:T(8,128)(2,1)} %refs_5_.1, bf16[768,2304]{1,0:T(8,128)(2,1)} %refs_5_.1), custom_call_target="tpu_custom_call" | custom-call | flops 1 | bytes 1 | tf_op jit(solution)/shard_map/pallas_call | solution.py:580
  317.3 24.9 %shard_map.218 = (bf16[1,1024,768]{2,1,0:T(8,128)(2,1)}, bf16[1,1024,768]{2,1,0:T(8,128)(2,1)}, bf16[1,1024,768]{2,1,0:T(8,128)(2,1)}) custom-call(s32[1]{0:T(128)} %bitcast.10.me_ref, s32[1,2]{1,0:T(1,128)} %slice.15.low_ref, bf16[1,1024,2304]{2,1,0:T(8,128)(2,1)} %bitcast.85, bf16[1,1024,2304]{2,1,0:T(8,128)(2,1)} %bitcast.86, ...), custom_call_target="tpu_custom_call" | custom-call | flops 99999997952 | bytes 1 | tf_op jit(solution)/shard_map/pallas_call | solution.py:291
  342.3 8.1 %collective-permute-done.2 = bf16[768,1536]{1,0:T(8,128)(2,1)} collective-permute-done((bf16[768,1536]{1,0:T(8,128)(2,1)}, bf16[768,1536]{1,0:T(8,128)(2,1)}, u32[]{:S(2)}, u32[]{:S(2)}) %collective-permute-start.2) | collective-permute-done | bytes 2359328 | tf_op jit(solution)/shard_map/ppermute | solution.py:855
  354.0 7.2 %shard_map.220 = bf16[768,1536]{1,0:T(8,128)(2,1)} custom-call(bf16[1024,768]{1,0:T(8,128)(2,1)} %get-tuple-element.178.refs_0_, bf16[1024,768]{1,0:T(8,128)(2,1)} %bitcast.100, bf16[1024,768]{1,0:T(8,128)(2,1)} %bitcast.115, bf16[1024,768]{1,0:T(8,128)(2,1)} %get-tuple-element.179.refs_3_), custom_call_target="tpu_custom_call" | custom-call | flops 1 | bytes 1 | tf_op jit(solution)/shard_map/pallas_call | solution.py:508
  364.2 19.5 %collective-permute-done.3 = bf16[1,1024,768]{2,1,0:T(8,128)(2,1)} collective-permute-done((bf16[1,1024,768]{2,1,0:T(8,128)(2,1)}, bf16[1,1024,768]{2,1,0:T(8,128)(2,1)}, u32[]{:S(2)}, u32[]{:S(2)}) %collective-permute-start.3) | collective-permute-done | bytes 1572896 | tf_op jit(solution)/shard_map/ppermute | solution.py:736
  383.6 8.9 %shard_map.219 = (f32[1024,768]{1,0:T(8,128)}, f32[2,768]{1,0:T(2,128)}) custom-call(bf16[1024,768]{1,0:T(8,128)(2,1)} %bitcast.77, bf16[1024,768]{1,0:T(8,128)(2,1)} %bitcast.116, bf16[1024,768]{1,0:T(8,128)(2,1)} %bitcast.111, bf16[1024,768]{1,0:T(8,128)(2,1)} %bitcast.113, bf16[768,2304]{1,0:T(8,128)(2,1)} %refs_5_.1, bf16[768,2304]{1,0:T(8,128)(2,1)} %refs_5_.1, ...), custom_call_target="tpu_custom_call" | custom-call | flops 1 | bytes 1 | tf_op jit(solution)/shard_map/pallas_call | solution.py:580
  395.0 10.7 %shard_map.223 = bf16[768,1536]{1,0:T(8,128)(2,1)} custom-call(bf16[1024,768]{1,0:T(8,128)(2,1)} %get-tuple-element.178.refs_0_, bf16[1024,768]{1,0:T(8,128)(2,1)} %get-tuple-element.197.refs_1_, bf16[1024,768]{1,0:T(8,128)(2,1)} %bitcast.112, bf16[1024,768]{1,0:T(8,128)(2,1)} %bitcast.114, bf16[1024,768]{1,0:T(8,128)(2,1)} %bitcast.118, ...), custom_call_target="tpu_custom_call" | custom-call | flops 1 | bytes 1 | tf_op jit(solution)/shard_map/pallas_call | solution.py:508
  470.0 8.2 %shard_map.222 = bf16[1024,768]{1,0:T(8,128)(2,1)} custom-call(s32[1,1024]{1,0:T(1,128)} %get-tuple-element.120.target_ref, f32[1024,768]{1,0:T(8,128)} %get-tuple-element.191.middle_ref, f32[1024,1]{1,0:T(8,128)} %get-tuple-element.192.gate_ref, bf16[2048,768]{1,0:T(8,128)(2,1)} %bitcast.104), custom_call_target="tpu_custom_call" | custom-call | flops 1 | bytes 1 | tf_op jit(solution)/shard_map/pallas_call | solution.py:580
  (214 shorter events, 187.3 us)
Async XLA Ops:
  0.6 39.9 %collective-permute-start = (bf16[1,1024,768]{2,1,0:T(8,128)(2,1)}, bf16[1,1024,768]{2,1,0:T(8,128)(2,1)}, u32[]{:S(2)}, u32[]{:S(2)}) collective-permute-start(bf16[1,1024,768]{2,1,0:T(8,128)(2,1)} %param.13), channel_id=1, source_target_pairs={{0,16},{1,17},{2,18},{3,19},{4,20},{5,21},{6,22},{7,23},{8,24},{9,... | collective-permute-start | bytes 4718600 | tf_op jit(solution)/shard_map/ppermute | solution.py:733
  26.1 65.3 %all-to-all-start = ((bf16[16,128,768]{2,1,0:T(8,128)(2,1)}), bf16[16,128,768]{2,1,0:T(8,128)(2,1)S(1)}, u32[]{:S(2)}, u32[]{:S(2)}) async-start(bf16[16,128,768]{2,1,0:T(8,128)(2,1)} %bitcast.105), calls=%async_computation | async-start | bytes 6291456 | tf_op jit(solution)/shard_map/all_to_all | solution.py:754
  97.3 47.5 %all-to-all-start.1 = ((bf16[16,64,768]{2,1,0:T(8,128)(2,1)}), bf16[16,64,768]{2,1,0:T(8,128)(2,1)}, u32[]{:S(2)}, u32[]{:S(2)}) async-start(bf16[16,64,768]{2,1,0:T(8,128)(2,1)} %bitcast.110), calls=%async_computation.1 | async-start | bytes 3145728 | tf_op jit(solution)/shard_map/all_to_all | solution.py:754
  144.8 41.1 %all-to-all-start.3 = ((bf16[16,64,768]{2,1,0:T(8,128)(2,1)}), bf16[16,64,768]{2,1,0:T(8,128)(2,1)S(1)}, u32[]{:S(2)}, u32[]{:S(2)}) async-start(bf16[16,64,768]{2,1,0:T(8,128)(2,1)} %bitcast.109), calls=%async_computation.3 | async-start | bytes 3145728 | tf_op jit(solution)/shard_map/all_to_all | solution.py:754
  185.9 41.4 %all-to-all-start.2 = ((bf16[16,64,768]{2,1,0:T(8,128)(2,1)}), bf16[16,64,768]{2,1,0:T(8,128)(2,1)}, u32[]{:S(2)}, u32[]{:S(2)}) async-start(bf16[16,64,768]{2,1,0:T(8,128)(2,1)} %bitcast.128), calls=%async_computation.2 | async-start | bytes 3145728 | tf_op jit(solution)/shard_map/all_to_all | solution.py:754
  227.3 44.8 %all-to-all-start.4 = ((bf16[16,64,768]{2,1,0:T(8,128)(2,1)}), bf16[16,64,768]{2,1,0:T(8,128)(2,1)S(1)}, u32[]{:S(2)}, u32[]{:S(2)}) async-start(bf16[16,64,768]{2,1,0:T(8,128)(2,1)} %bitcast.129), calls=%async_computation.4 | async-start | bytes 3145728 | tf_op jit(solution)/shard_map/all_to_all | solution.py:754
  245.5 70.6 %collective-permute-start.1 = (bf16[1536,768]{1,0:T(8,128)(2,1)}, bf16[1536,768]{1,0:T(8,128)(2,1)}, u32[]{:S(2)}, u32[]{:S(2)}) collective-permute-start(bf16[1536,768]{1,0:T(8,128)(2,1)} %add_convert_fusion.1), channel_id=1, source_target_pairs={{0,16},{16,0},{1,17},{17,1},{2,18},{18,2},{3,19},{19,3},{4,20},{20... | collective-permute-start | bytes 7077896 | tf_op jit(solution)/shard_map/ppermute | solution.py:855
  254.4 96.0 %collective-permute-start.2 = (bf16[768,1536]{1,0:T(8,128)(2,1)}, bf16[768,1536]{1,0:T(8,128)(2,1)}, u32[]{:S(2)}, u32[]{:S(2)}) collective-permute-start(bf16[768,1536]{1,0:T(8,128)(2,1)} %add_convert_fusion), channel_id=1, source_target_pairs={{0,16},{16,0},{1,17},{17,1},{2,18},{18,2},{3,19},{19,3},{4,20},{20... | collective-permute-start | bytes 7077896 | tf_op jit(solution)/shard_map/ppermute | solution.py:855
  286.9 65.5 %all-to-all-start.5 = ((bf16[16,128,768]{2,1,0:T(8,128)(2,1)}), bf16[16,128,768]{2,1,0:T(8,128)(2,1)S(1)}, u32[]{:S(2)}, u32[]{:S(2)}) async-start(bf16[16,128,768]{2,1,0:T(8,128)(2,1)} %bitcast.37), calls=%async_computation.5 | async-start | bytes 6291456 | tf_op jit(solution)/shard_map/all_to_all | solution.py:754
  316.0 67.6 %collective-permute-start.3 = (bf16[1,1024,768]{2,1,0:T(8,128)(2,1)}, bf16[1,1024,768]{2,1,0:T(8,128)(2,1)}, u32[]{:S(2)}, u32[]{:S(2)}) collective-permute-start(bf16[1,1024,768]{2,1,0:T(8,128)(2,1)} %bitcast.147), channel_id=1, source_target_pairs={{16,0},{17,1},{18,2},{19,3},{20,4},{21,5},{22,6},{23,7},{24,8},{25... | collective-permute-start | bytes 4718600 | tf_op jit(solution)/shard_map/ppermute | solution.py:736
  362.7 45.0 %collective-permute-start.4 = (bf16[384,1536]{1,0:T(8,128)(2,1)S(1)}, bf16[384,1536]{1,0:T(8,128)(2,1)S(1)}, u32[]{:S(2)}, u32[]{:S(2)}) collective-permute-start(bf16[384,1536]{1,0:T(8,128)(2,1)S(1)} %constant_dynamic-slice_fusion.2), channel_id=1, source_target_pairs={{0,1},{1,0},{2,3},{3,2},{4,5},{5,4},{6,7},{7,6},{8,9},{9,8},{10,11... | collective-permute-start | bytes 3538952 | tf_op jit(solution)/shard_map/ppermute | solution.py:665
  395.0 12.7 %collective-permute-start.5 = (bf16[384,128]{1,0:T(8,128)(2,1)S(1)}, bf16[384,128]{1,0:T(8,128)(2,1)S(1)}, u32[]{:S(2)}, u32[]{:S(2)}) collective-permute-start(bf16[384,128]{1,0:T(8,128)(2,1)S(1)} %constant_dynamic-slice_fusion.1), channel_id=1, source_target_pairs={{0,1},{1,0},{2,3},{3,2},{4,5},{5,4},{6,7},{7,6},{8,9},{9,8},{10,11... | collective-permute-start | bytes 294920 | tf_op jit(solution)/shard_map/ppermute | solution.py:665
  408.4 28.8 %collective-permute-start.6 = (bf16[96,1664]{1,0:T(8,128)(2,1)S(1)}, bf16[96,1664]{1,0:T(8,128)(2,1)S(1)}, u32[]{:S(2)}, u32[]{:S(2)}) collective-permute-start(bf16[96,1664]{1,0:T(8,128)(2,1)S(1)} %get-tuple-element.216), channel_id=1, source_target_pairs={{0,2},{1,3},{2,0},{3,1},{4,6},{5,7},{6,4},{7,5},{8,10},{9,11},{10,... | collective-permute-start | bytes 958472 | tf_op jit(solution)/shard_map/ppermute | solution.py:665
  410.2 27.5 %collective-permute-start.7 = (bf16[96,1664]{1,0:T(8,128)(2,1)S(1)}, bf16[96,1664]{1,0:T(8,128)(2,1)S(1)}, u32[]{:S(2)}, u32[]{:S(2)}) collective-permute-start(bf16[96,1664]{1,0:T(8,128)(2,1)S(1)} %get-tuple-element.218), channel_id=1, source_target_pairs={{0,16},{1,17},{2,18},{3,19},{4,20},{5,21},{6,22},{7,23},{8,24},{9,... | collective-permute-start | bytes 958472 | tf_op jit(solution)/shard_map/ppermute | solution.py:665
  410.7 14.0 %collective-permute-start.19 = (bf16[96,1536]{1,0:T(8,128)(2,1)S(1)}, bf16[96,1536]{1,0:T(8,128)(2,1)S(1)}, u32[]{:S(2)}, u32[]{:S(2)}) collective-permute-start(bf16[96,1536]{1,0:T(8,128)(2,1)S(1)} %get-tuple-element.219), channel_id=1, source_target_pairs={{0,2},{1,3},{2,0},{3,1},{4,6},{5,7},{6,4},{7,5},{8,10},{9,11},{10,... | collective-permute-start | bytes 884744 | tf_op jit(solution)/shard_map/ppermute | solution.py:665
  412.4 14.5 %collective-permute-start.20 = (bf16[96,1536]{1,0:T(8,128)(2,1)S(1)}, bf16[96,1536]{1,0:T(8,128)(2,1)S(1)}, u32[]{:S(2)}, u32[]{:S(2)}) collective-permute-start(bf16[96,1536]{1,0:T(8,128)(2,1)S(1)} %get-tuple-element.221), channel_id=1, source_target_pairs={{0,16},{1,17},{2,18},{3,19},{4,20},{5,21},{6,22},{7,23},{8,24},{9,... | collective-permute-start | bytes 884744 | tf_op jit(solution)/shard_map/ppermute | solution.py:665
  413.1 19.9 %collective-permute-start.21 = (bf16[96,1536]{1,0:T(8,128)(2,1)S(1)}, bf16[96,1536]{1,0:T(8,128)(2,1)S(1)}, u32[]{:S(2)}, u32[]{:S(2)}) collective-permute-start(bf16[96,1536]{1,0:T(8,128)(2,1)S(1)} %get-tuple-element.220), channel_id=1, source_target_pairs={{0,18},{1,19},{2,16},{3,17},{4,22},{5,23},{6,20},{7,21},{8,26},{9,... | collective-permute-start | bytes 884744 | tf_op jit(solution)/shard_map/ppermute | solution.py:665
  424.6 14.3 %collective-permute-start.8 = (bf16[96,1664]{1,0:T(8,128)(2,1)S(1)}, bf16[96,1664]{1,0:T(8,128)(2,1)S(1)}, u32[]{:S(2)}, u32[]{:S(2)}) collective-permute-start(bf16[96,1664]{1,0:T(8,128)(2,1)S(1)} %get-tuple-element.217), channel_id=1, source_target_pairs={{0,18},{1,19},{2,16},{3,17},{4,22},{5,23},{6,20},{7,21},{8,26},{9,... | collective-permute-start | bytes 958472 | tf_op jit(solution)/shard_map/ppermute | solution.py:665
  433.2 10.1 %collective-permute-start.22 = (bf16[24,1536]{1,0:T(8,128)(2,1)S(1)}, bf16[24,1536]{1,0:T(8,128)(2,1)S(1)}, u32[]{:S(2)}, u32[]{:S(2)}) collective-permute-start(bf16[24,1536]{1,0:T(8,128)(2,1)S(1)} %get-tuple-element.225), channel_id=1, source_target_pairs={{0,4},{1,5},{2,6},{3,7},{4,0},{5,1},{6,2},{7,3},{8,12},{9,13},{10,... | collective-permute-start | bytes 221192 | tf_op jit(solution)/shard_map/ppermute | solution.py:665
  455.7 22.5 %collective-permute-start.28 = (bf16[96,1536]{1,0:T(8,128)(2,1)S(1)}, bf16[96,1536]{1,0:T(8,128)(2,1)S(1)}, u32[]{:S(2)}, u32[]{:S(2)}) collective-permute-start(bf16[96,1536]{1,0:T(8,128)(2,1)S(1)} %constant_dynamic-update-slice_fusion.8), channel_id=1, source_target_pairs={{0,2},{1,3},{2,0},{3,1},{4,6},{5,7},{6,4},{7,5},{8,10},{9,11},{10,... | collective-permute-start | bytes 884744 | tf_op jit(solution)/shard_map/ppermute | solution.py:665
  457.1 23.9 %collective-permute-start.29 = (bf16[96,1536]{1,0:T(8,128)(2,1)S(1)}, bf16[96,1536]{1,0:T(8,128)(2,1)S(1)}, u32[]{:S(2)}, u32[]{:S(2)}) collective-permute-start(bf16[96,1536]{1,0:T(8,128)(2,1)S(1)} %constant_dynamic-update-slice_fusion.8), channel_id=1, source_target_pairs={{0,16},{1,17},{2,18},{3,19},{4,20},{5,21},{6,22},{7,23},{8,24},{9,... | collective-permute-start | bytes 884744 | tf_op jit(solution)/shard_map/ppermute | solution.py:665
  459.6 22.2 %collective-permute-start.30 = (bf16[96,1536]{1,0:T(8,128)(2,1)S(1)}, bf16[96,1536]{1,0:T(8,128)(2,1)S(1)}, u32[]{:S(2)}, u32[]{:S(2)}) collective-permute-start(bf16[96,1536]{1,0:T(8,128)(2,1)S(1)} %constant_dynamic-update-slice_fusion.8), channel_id=1, source_target_pairs={{0,18},{1,19},{2,16},{3,17},{4,22},{5,23},{6,20},{7,21},{8,26},{9,... | collective-permute-start | bytes 884744 | tf_op jit(solution)/shard_map/ppermute | solution.py:665
  462.1 20.4 %collective-permute-start.15 = (bf16[96,1664]{1,0:T(8,128)(2,1)S(1)}, bf16[96,1664]{1,0:T(8,128)(2,1)S(1)}, u32[]{:S(2)}, u32[]{:S(2)}) collective-permute-start(bf16[96,1664]{1,0:T(8,128)(2,1)S(1)} %constant_dynamic-update-slice_fusion.16), channel_id=1, source_target_pairs={{0,2},{1,3},{2,0},{3,1},{4,6},{5,7},{6,4},{7,5},{8,10},{9,11},{10,... | collective-permute-start | bytes 958472 | tf_op jit(solution)/shard_map/ppermute | solution.py:665
  463.5 19.0 %collective-permute-start.16 = (bf16[96,1664]{1,0:T(8,128)(2,1)S(1)}, bf16[96,1664]{1,0:T(8,128)(2,1)S(1)}, u32[]{:S(2)}, u32[]{:S(2)}) collective-permute-start(bf16[96,1664]{1,0:T(8,128)(2,1)S(1)} %constant_dynamic-update-slice_fusion.16), channel_id=1, source_target_pairs={{0,16},{1,17},{2,18},{3,19},{4,20},{5,21},{6,22},{7,23},{8,24},{9,... | collective-permute-start | bytes 958472 | tf_op jit(solution)/shard_map/ppermute | solution.py:665
  (47 other events, 402.9 us)

commit v4 on v3

--- a/solution.py
+++ b/solution.py
@@ -691,6 +691,10 @@
     gathered = []
     for x in parts:
         rows = x.shape[0]
+        if len(bits) == 1:
+            part = swap(x, bits[0])
+            gathered.append(jnp.where(code == 0, jnp.concatenate([x, part]), jnp.concatenate([part, x])))
+            continue
         whole = jnp.zeros((rows << len(bits), x.shape[1]), bf16)
         whole = lax.dynamic_update_slice_in_dim(whole, x, code * rows, 0)
         for other in range(1, 1 << len(bits)):

time: 507 us -> 509 us (level)
  other arithmetic: 23 us -> 30 us
  local copies, waits for them, and re-layouts: 25.8 us -> 19.8 us
    select_n x0 -> x2, other arithmetic: none -> 7.04 us  [gather_step(): jnp.where(code == 0, jnp.concatenate([x, part]), jnp.concatenate([part, x]))]
where the time goes in v4:
time: 509 us; the launch traced here: 503 us
  Pallas kernels  243 us (48%)
  starting transfers between devices  97 us (19%)
  waiting for transfers between devices  76 us (15%)
  matrix products  35 us (7%)
  other arithmetic  30 us (6%)
  local copies, waits for them, and re-layouts  19.8 us (4%)
    pallas_call x5, Pallas kernels, call(): pl.pallas_call(functools.partial(kernel, tile=self.tile, block_len=self.b...  84.2 us
    pallas_call x7, Pallas kernels, by_tokens(): pl.pallas_call(kernel, grid=(flat // tile,), in_specs=specs, out_specs=[c...  61.2 us
    all_to_all x6, starting transfers between devices, exchange(): lax.all_to_all(array.reshape(experts, -1, width), 'wide', split_axis=0, c...  55.1 us
    pallas_call x2, Pallas kernels, run_expert(): pl.pallas_call(expert_kernel, grid=(rows // tile,), in_specs=in_specs, ou...  54.6 us
    ppermute x29, starting transfers between devices, swap(): lax.ppermute(array, ('blk', 'wide'), [(i, i ^ mask) for i in range(total)])  32.7 us
    all_to_all x6, waiting for transfers between devices, exchange(): lax.all_to_all(array.reshape(experts, -1, width), 'wide', split_axis=0, c...  28.5 us
    ppermute x29, waiting for transfers between devices, swap(): lax.ppermute(array, ('blk', 'wide'), [(i, i ^ mask) for i in range(total)])  20 us
    ppermute x1, waiting for transfers between devices, behind(): lax.ppermute(array, 'blk', [(i + shift, i) for i in range(blocks - shift)])  19.5 us
  transfers between devices with their start and end apart: 39, of which 16 were waited for; matrix products, arithmetic and copies ran while one was open for 15% of the time, Pallas kernels for 46%

profile of v4, /device:TPU:0, one launch (start us, length us, event | category | flops | bytes accessed | tf_op | source)
XLA Modules:
  0.0 502.7 jit_solution(14960295813071219500)
XLA Ops:
  18.8 7.3 %shard_map.208 = bf16[2048,768]{1,0:T(8,128)(2,1)} custom-call(s32[1,1024]{1,0:T(1,128)} %get-tuple-element.120.target_ref, bf16[1024,768]{1,0:T(8,128)(2,1)} %bitcast.106), custom_call_target="tpu_custom_call" | custom-call | flops 1 | bytes 1 | tf_op jit(solution)/shard_map/pallas_call | solution.py:385
  32.1 8.5 %shard_map.204 = (bf16[1024,768]{1,0:T(8,128)(2,1)}, bf16[1024,2304]{1,0:T(8,128)(2,1)}) custom-call(bf16[1024,768]{1,0:T(8,128)(2,1)} %bitcast.75, f32[1,768]{1,0:T(1,128)} %reshape.387.gain_ref, f32[1,768]{1,0:T(1,128)} %reshape.388.shift_ref, bf16[768,2304]{1,0:T(8,128)(2,1)} %refs_5_.1, bf16[768,2304]{1,0:T(8,128)(2,1)} %refs_5_.1, bf16[768,2304]{1,0:T(8,128)(2,1)} %refs_5_.1), custom_call_target="tpu_custom_call" | custom-call | flops 1 | bytes 1 | tf_op jit(solution)/shard_map/pallas_call | solution.py:580
  40.6 7.1 %shard_map.205 = (bf16[1024,768]{1,0:T(8,128)(2,1)}, bf16[1024,1536]{1,0:T(8,128)(2,1)}) custom-call(bf16[1024,768]{1,0:T(8,128)(2,1)} %bitcast.13.tokens_ref, f32[1,768]{1,0:T(1,128)} %reshape.387.gain_ref, f32[1,768]{1,0:T(1,128)} %reshape.388.shift_ref, bf16[768,2304]{1,0:T(8,128)(2,1)} %refs_5_.1, bf16[768,2304]{1,0:T(8,128)(2,1)} %refs_5_.1), custom_call_target="tpu_custom_call" | custom-call | flops 1 | bytes 1 | tf_op jit(solution)/shard_map/pallas_call | solution.py:580
  47.7 20.0 %shard_map.206 = (bf16[1,1024,768]{2,1,0:T(8,128)(2,1)}, f32[1,3,4,1024]{3,2,1,0:T(4,128)}) custom-call(s32[1]{0:T(128)} %bitcast.10.me_ref, s32[1,2]{1,0:T(1,128)} %slice.15.low_ref, bf16[1,1024,2304]{2,1,0:T(8,128)(2,1)} %bitcast.78, bf16[1,1024,2304]{2,1,0:T(8,128)(2,1)} %bitcast.79, bf16[1,1024,2304]{2,1,0:T(8,128)(2,1)} %bitcast.80, ...), custom_call_target="tpu_custom_call" | custom-call | flops 99999997952 | bytes 1 | tf_op jit(solution)/shard_map/pallas_call | solution.py:291
  67.7 7.5 %shard_map.207 = (f32[1024,768]{1,0:T(8,128)}, bf16[1024,768]{1,0:T(8,128)(2,1)}, f32[1024,1]{1,0:T(8,128)}) custom-call(bf16[1024,768]{1,0:T(8,128)(2,1)} %bitcast.99, bf16[1024,768]{1,0:T(8,128)(2,1)} %bitcast.76, s32[1,1024]{1,0:T(1,128)} %bitcast.136, bf16[768,768]{1,0:T(8,128)(2,1)} %weight_ref.3, f32[1,768]{1,0:T(1,128)} %reshape.389.gain_ref, ...), custom_call_target="tpu_custom_call" | custom-call | flops 1 | bytes 1 | tf_op jit(solution)/shard_map/pallas_call | solution.py:580
  75.3 16.2 %all-to-all-done = bf16[16,128,768]{2,1,0:T(8,128)(2,1)S(1)} async-done(((bf16[16,128,768]{2,1,0:T(8,128)(2,1)}), bf16[16,128,768]{2,1,0:T(8,128)(2,1)S(1)}, u32[]{:S(2)}, u32[]{:S(2)}) %all-to-all-start) | async-done | bytes 3145760 | tf_op jit(solution)/shard_map/all_to_all | solution.py:758
  97.3 15.5 %all-to-all-start.1 = ((bf16[16,64,768]{2,1,0:T(8,128)(2,1)}), bf16[16,64,768]{2,1,0:T(8,128)(2,1)}, u32[]{:S(2)}, u32[]{:S(2)}) async-start(bf16[16,64,768]{2,1,0:T(8,128)(2,1)} %bitcast.110), calls=%async_computation.1 | async-start | bytes 3145728 | tf_op jit(solution)/shard_map/all_to_all | solution.py:758
  113.3 10.5 %shard_map.213.refs_5_ = bf16[1,12,1024,1024]{3,2,1,0:T(8,128)(2,1)} custom-call(s32[1]{0:T(128)} %bitcast.10.me_ref, s32[1,2]{1,0:T(1,128)} %slice.15.low_ref, bf16[1,1024,2304]{2,1,0:T(8,128)(2,1)} %bitcast.81, bf16[1,1024,1536]{2,1,0:T(8,128)(2,1)} %bitcast.92, f32[1,3,4,1024]{3,2,1,0:T(4,128)} %get-tuple-element.129.lse_ref, s32[1,1,1024]{2,1,0:T(1,128)} %bitcast.139), custom_call_target="tpu_custom_call" | custom-call | flops 1 | bytes 1 | tf_op jit(solution)/shard_map/pallas_call | solution.py:291
  123.9 12.9 %shard_map.212.refs_5_ = bf16[1,12,1024,1024]{3,2,1,0:T(8,128)(2,1)} custom-call(s32[1]{0:T(128)} %bitcast.10.me_ref, s32[1,2]{1,0:T(1,128)} %slice.15.low_ref, bf16[1,1024,2304]{2,1,0:T(8,128)(2,1)} %bitcast.82, bf16[1,1024,2304]{2,1,0:T(8,128)(2,1)} %bitcast.83, f32[1,3,4,1024]{3,2,1,0:T(4,128)} %get-tuple-element.129.lse_ref, s32[1,1,1024]{2,1,0:T(1,128)} %bitcast.140), custom_call_target="tpu_custom_call" | custom-call | flops 1 | bytes 1 | tf_op jit(solution)/shard_map/pallas_call | solution.py:291
  144.8 9.1 %all-to-all-start.3 = ((bf16[16,64,768]{2,1,0:T(8,128)(2,1)}), bf16[16,64,768]{2,1,0:T(8,128)(2,1)S(1)}, u32[]{:S(2)}, u32[]{:S(2)}) async-start(bf16[16,64,768]{2,1,0:T(8,128)(2,1)} %bitcast.109), calls=%async_computation.3 | async-start | bytes 3145728 | tf_op jit(solution)/shard_map/all_to_all | solution.py:758
  155.2 27.3 %shard_map.210 = (bf16[16,2,64,768]{3,2,1,0:T(8,128)(2,1)}, bf16[1024,768]{1,0:T(8,128)(2,1)}, bf16[1024,3072]{1,0:T(8,128)(2,1)}, bf16[1024,3072]{1,0:T(8,128)(2,1)}, bf16[1024,768]{1,0:T(8,128)(2,1)}) custom-call(bf16[1024,768]{1,0:T(8,128)(2,1)} %bitcast.19.refs_0_, bf16[16,2,64,768]{3,2,1,0:T(8,128)(2,1)} %bitcast.88, bf16[768,3072]{1,0:T(8,128)(2,1)} %bitcast.95, ...), custom_call_target="tpu_custom_call" | custom-call | flops 1 | bytes 1 | tf_op jit(solution)/shard_map/pallas_call | solution.py:635
  185.9 9.3 %all-to-all-start.2 = ((bf16[16,64,768]{2,1,0:T(8,128)(2,1)}), bf16[16,64,768]{2,1,0:T(8,128)(2,1)}, u32[]{:S(2)}, u32[]{:S(2)}) async-start(bf16[16,64,768]{2,1,0:T(8,128)(2,1)} %bitcast.128), calls=%async_computation.2 | async-start | bytes 3145728 | tf_op jit(solution)/shard_map/all_to_all | solution.py:758
  196.3 27.3 %shard_map.214 = (bf16[16,2,64,768]{3,2,1,0:T(8,128)(2,1)}, bf16[1024,768]{1,0:T(8,128)(2,1)}, bf16[1024,3072]{1,0:T(8,128)(2,1)}, bf16[1024,3072]{1,0:T(8,128)(2,1)}, bf16[1024,768]{1,0:T(8,128)(2,1)}) custom-call(bf16[1024,768]{1,0:T(8,128)(2,1)} %bitcast.101, bf16[16,2,64,768]{3,2,1,0:T(8,128)(2,1)} %bitcast.89, ...), custom_call_target="tpu_custom_call", output_to_operand_aliasing={{0}: (5, {})} | custom-call | flops 1 | bytes 1 | tf_op jit(solution)/shard_map/pallas_call | solution.py:635
  227.2 9.1 %all-to-all-start.4 = ((bf16[16,64,768]{2,1,0:T(8,128)(2,1)}), bf16[16,64,768]{2,1,0:T(8,128)(2,1)S(1)}, u32[]{:S(2)}, u32[]{:S(2)}) async-start(bf16[16,64,768]{2,1,0:T(8,128)(2,1)} %bitcast.129), calls=%async_computation.4 | async-start | bytes 3145728 | tf_op jit(solution)/shard_map/all_to_all | solution.py:758
  273.2 13.6 %shard_map.215 = (f32[1024,768]{1,0:T(8,128)}, bf16[1024,768]{1,0:T(8,128)(2,1)}, bf16[1024,768]{1,0:T(8,128)(2,1)}, f32[2,768]{1,0:T(2,128)}) custom-call(s32[1,1024]{1,0:T(1,128)} %add_add_fusion.target_ref, f32[1024,768]{1,0:T(8,128)} %get-tuple-element.191.middle_ref, bf16[1024,768]{1,0:T(8,128)(2,1)} %bitcast.107, f32[1,768]{1,0:T(1,128)} %reshape.389.gain_ref, ...), custom_call_target="tpu_custom_call" | custom-call | flops 1 | bytes 1 | tf_op jit(solution)/shard_map/pallas_call | solution.py:580
  293.0 15.6 %shard_map.216 = (f32[1,768,1024]{2,1,0:T(8,128)}, bf16[1,1024,768]{2,1,0:T(8,128)(2,1)}, bf16[1,1024,768]{2,1,0:T(8,128)(2,1)}) custom-call(s32[1]{0:T(128)} %bitcast.10.me_ref, s32[1,2]{1,0:T(1,128)} %slice.15.low_ref, bf16[1,1024,2304]{2,1,0:T(8,128)(2,1)} %bitcast.84, bf16[1,1024,1536]{2,1,0:T(8,128)(2,1)} %bitcast.93, bf16[1,1024,1536]{2,1,0:T(8,128)(2,1)} %bitcast.94, ...), custom_call_target="tpu_custom_call" | custom-call | flops 1 | bytes 1 | tf_op jit(solution)/shard_map/pallas_call | solution.py:291
  308.6 7.4 %shard_map.217 = (bf16[1024,768]{1,0:T(8,128)(2,1)}, f32[2,768]{1,0:T(2,128)}) custom-call(bf16[1024,768]{1,0:T(8,128)(2,1)} %bitcast.13.tokens_ref, bf16[1024,768]{1,0:T(8,128)(2,1)} %bitcast.117, bf16[1024,768]{1,0:T(8,128)(2,1)} %bitcast.119, bf16[768,2304]{1,0:T(8,128)(2,1)} %refs_5_.1, bf16[768,2304]{1,0:T(8,128)(2,1)} %refs_5_.1), custom_call_target="tpu_custom_call" | custom-call | flops 1 | bytes 1 | tf_op jit(solution)/shard_map/pallas_call | solution.py:580
  317.3 25.0 %shard_map.218 = (bf16[1,1024,768]{2,1,0:T(8,128)(2,1)}, bf16[1,1024,768]{2,1,0:T(8,128)(2,1)}, bf16[1,1024,768]{2,1,0:T(8,128)(2,1)}) custom-call(s32[1]{0:T(128)} %bitcast.10.me_ref, s32[1,2]{1,0:T(1,128)} %slice.15.low_ref, bf16[1,1024,2304]{2,1,0:T(8,128)(2,1)} %bitcast.85, bf16[1,1024,2304]{2,1,0:T(8,128)(2,1)} %bitcast.86, ...), custom_call_target="tpu_custom_call" | custom-call | flops 99999997952 | bytes 1 | tf_op jit(solution)/shard_map/pallas_call | solution.py:291
  342.3 8.1 %collective-permute-done.2 = bf16[768,1536]{1,0:T(8,128)(2,1)} collective-permute-done((bf16[768,1536]{1,0:T(8,128)(2,1)}, bf16[768,1536]{1,0:T(8,128)(2,1)}, u32[]{:S(2)}, u32[]{:S(2)}) %collective-permute-start.2) | collective-permute-done | bytes 2359328 | tf_op jit(solution)/shard_map/ppermute | solution.py:859
  354.0 7.2 %shard_map.220 = bf16[768,1536]{1,0:T(8,128)(2,1)} custom-call(bf16[1024,768]{1,0:T(8,128)(2,1)} %get-tuple-element.178.refs_0_, bf16[1024,768]{1,0:T(8,128)(2,1)} %bitcast.100, bf16[1024,768]{1,0:T(8,128)(2,1)} %bitcast.115, bf16[1024,768]{1,0:T(8,128)(2,1)} %get-tuple-element.179.refs_3_), custom_call_target="tpu_custom_call" | custom-call | flops 1 | bytes 1 | tf_op jit(solution)/shard_map/pallas_call | solution.py:508
  364.1 19.5 %collective-permute-done.3 = bf16[1,1024,768]{2,1,0:T(8,128)(2,1)} collective-permute-done((bf16[1,1024,768]{2,1,0:T(8,128)(2,1)}, bf16[1,1024,768]{2,1,0:T(8,128)(2,1)}, u32[]{:S(2)}, u32[]{:S(2)}) %collective-permute-start.3) | collective-permute-done | bytes 1572896 | tf_op jit(solution)/shard_map/ppermute | solution.py:740
  383.6 8.9 %shard_map.219 = (f32[1024,768]{1,0:T(8,128)}, f32[2,768]{1,0:T(2,128)}) custom-call(bf16[1024,768]{1,0:T(8,128)(2,1)} %bitcast.77, bf16[1024,768]{1,0:T(8,128)(2,1)} %bitcast.116, bf16[1024,768]{1,0:T(8,128)(2,1)} %bitcast.111, bf16[1024,768]{1,0:T(8,128)(2,1)} %bitcast.113, bf16[768,2304]{1,0:T(8,128)(2,1)} %refs_5_.1, bf16[768,2304]{1,0:T(8,128)(2,1)} %refs_5_.1, ...), custom_call_target="tpu_custom_call" | custom-call | flops 1 | bytes 1 | tf_op jit(solution)/shard_map/pallas_call | solution.py:580
  395.0 10.7 %shard_map.223 = bf16[768,1536]{1,0:T(8,128)(2,1)} custom-call(bf16[1024,768]{1,0:T(8,128)(2,1)} %get-tuple-element.178.refs_0_, bf16[1024,768]{1,0:T(8,128)(2,1)} %get-tuple-element.197.refs_1_, bf16[1024,768]{1,0:T(8,128)(2,1)} %bitcast.112, bf16[1024,768]{1,0:T(8,128)(2,1)} %bitcast.114, bf16[1024,768]{1,0:T(8,128)(2,1)} %bitcast.118, ...), custom_call_target="tpu_custom_call" | custom-call | flops 1 | bytes 1 | tf_op jit(solution)/shard_map/pallas_call | solution.py:508
  470.0 8.2 %shard_map.222 = bf16[1024,768]{1,0:T(8,128)(2,1)} custom-call(s32[1,1024]{1,0:T(1,128)} %get-tuple-element.120.target_ref, f32[1024,768]{1,0:T(8,128)} %get-tuple-element.191.middle_ref, f32[1024,1]{1,0:T(8,128)} %get-tuple-element.192.gate_ref, bf16[2048,768]{1,0:T(8,128)(2,1)} %bitcast.104), custom_call_target="tpu_custom_call" | custom-call | flops 1 | bytes 1 | tf_op jit(solution)/shard_map/pallas_call | solution.py:580
  (206 shorter events, 189.2 us)
Async XLA Ops:
  0.6 39.9 %collective-permute-start = (bf16[1,1024,768]{2,1,0:T(8,128)(2,1)}, bf16[1,1024,768]{2,1,0:T(8,128)(2,1)}, u32[]{:S(2)}, u32[]{:S(2)}) collective-permute-start(bf16[1,1024,768]{2,1,0:T(8,128)(2,1)} %param.13), channel_id=1, source_target_pairs={{0,16},{1,17},{2,18},{3,19},{4,20},{5,21},{6,22},{7,23},{8,24},{9,... | collective-permute-start | bytes 4718600 | tf_op jit(solution)/shard_map/ppermute | solution.py:737
  26.1 65.3 %all-to-all-start = ((bf16[16,128,768]{2,1,0:T(8,128)(2,1)}), bf16[16,128,768]{2,1,0:T(8,128)(2,1)S(1)}, u32[]{:S(2)}, u32[]{:S(2)}) async-start(bf16[16,128,768]{2,1,0:T(8,128)(2,1)} %bitcast.105), calls=%async_computation | async-start | bytes 6291456 | tf_op jit(solution)/shard_map/all_to_all | solution.py:758
  97.3 47.5 %all-to-all-start.1 = ((bf16[16,64,768]{2,1,0:T(8,128)(2,1)}), bf16[16,64,768]{2,1,0:T(8,128)(2,1)}, u32[]{:S(2)}, u32[]{:S(2)}) async-start(bf16[16,64,768]{2,1,0:T(8,128)(2,1)} %bitcast.110), calls=%async_computation.1 | async-start | bytes 3145728 | tf_op jit(solution)/shard_map/all_to_all | solution.py:758
  144.8 41.1 %all-to-all-start.3 = ((bf16[16,64,768]{2,1,0:T(8,128)(2,1)}), bf16[16,64,768]{2,1,0:T(8,128)(2,1)S(1)}, u32[]{:S(2)}, u32[]{:S(2)}) async-start(bf16[16,64,768]{2,1,0:T(8,128)(2,1)} %bitcast.109), calls=%async_computation.3 | async-start | bytes 3145728 | tf_op jit(solution)/shard_map/all_to_all | solution.py:758
  185.9 41.4 %all-to-all-start.2 = ((bf16[16,64,768]{2,1,0:T(8,128)(2,1)}), bf16[16,64,768]{2,1,0:T(8,128)(2,1)}, u32[]{:S(2)}, u32[]{:S(2)}) async-start(bf16[16,64,768]{2,1,0:T(8,128)(2,1)} %bitcast.128), calls=%async_computation.2 | async-start | bytes 3145728 | tf_op jit(solution)/shard_map/all_to_all | solution.py:758
  227.2 44.8 %all-to-all-start.4 = ((bf16[16,64,768]{2,1,0:T(8,128)(2,1)}), bf16[16,64,768]{2,1,0:T(8,128)(2,1)S(1)}, u32[]{:S(2)}, u32[]{:S(2)}) async-start(bf16[16,64,768]{2,1,0:T(8,128)(2,1)} %bitcast.129), calls=%async_computation.4 | async-start | bytes 3145728 | tf_op jit(solution)/shard_map/all_to_all | solution.py:758
  245.4 70.5 %collective-permute-start.1 = (bf16[1536,768]{1,0:T(8,128)(2,1)}, bf16[1536,768]{1,0:T(8,128)(2,1)}, u32[]{:S(2)}, u32[]{:S(2)}) collective-permute-start(bf16[1536,768]{1,0:T(8,128)(2,1)} %add_convert_fusion.1), channel_id=1, source_target_pairs={{0,16},{16,0},{1,17},{17,1},{2,18},{18,2},{3,19},{19,3},{4,20},{20... | collective-permute-start | bytes 7077896 | tf_op jit(solution)/shard_map/ppermute | solution.py:859
  254.4 96.0 %collective-permute-start.2 = (bf16[768,1536]{1,0:T(8,128)(2,1)}, bf16[768,1536]{1,0:T(8,128)(2,1)}, u32[]{:S(2)}, u32[]{:S(2)}) collective-permute-start(bf16[768,1536]{1,0:T(8,128)(2,1)} %add_convert_fusion), channel_id=1, source_target_pairs={{0,16},{16,0},{1,17},{17,1},{2,18},{18,2},{3,19},{19,3},{4,20},{20... | collective-permute-start | bytes 7077896 | tf_op jit(solution)/shard_map/ppermute | solution.py:859
  286.8 65.5 %all-to-all-start.5 = ((bf16[16,128,768]{2,1,0:T(8,128)(2,1)}), bf16[16,128,768]{2,1,0:T(8,128)(2,1)S(1)}, u32[]{:S(2)}, u32[]{:S(2)}) async-start(bf16[16,128,768]{2,1,0:T(8,128)(2,1)} %bitcast.37), calls=%async_computation.5 | async-start | bytes 6291456 | tf_op jit(solution)/shard_map/all_to_all | solution.py:758
  316.0 67.6 %collective-permute-start.3 = (bf16[1,1024,768]{2,1,0:T(8,128)(2,1)}, bf16[1,1024,768]{2,1,0:T(8,128)(2,1)}, u32[]{:S(2)}, u32[]{:S(2)}) collective-permute-start(bf16[1,1024,768]{2,1,0:T(8,128)(2,1)} %bitcast.147), channel_id=1, source_target_pairs={{16,0},{17,1},{18,2},{19,3},{20,4},{21,5},{22,6},{23,7},{24,8},{25... | collective-permute-start | bytes 4718600 | tf_op jit(solution)/shard_map/ppermute | solution.py:740
  362.7 45.0 %collective-permute-start.4 = (bf16[384,1536]{1,0:T(8,128)(2,1)S(1)}, bf16[384,1536]{1,0:T(8,128)(2,1)S(1)}, u32[]{:S(2)}, u32[]{:S(2)}) collective-permute-start(bf16[384,1536]{1,0:T(8,128)(2,1)S(1)} %constant_dynamic-slice_fusion.2), channel_id=1, source_target_pairs={{0,1},{1,0},{2,3},{3,2},{4,5},{5,4},{6,7},{7,6},{8,9},{9,8},{10,11... | collective-permute-start | bytes 3538952 | tf_op jit(solution)/shard_map/ppermute | solution.py:665
  394.9 12.7 %collective-permute-start.5 = (bf16[384,128]{1,0:T(8,128)(2,1)S(1)}, bf16[384,128]{1,0:T(8,128)(2,1)S(1)}, u32[]{:S(2)}, u32[]{:S(2)}) collective-permute-start(bf16[384,128]{1,0:T(8,128)(2,1)S(1)} %constant_dynamic-slice_fusion.1), channel_id=1, source_target_pairs={{0,1},{1,0},{2,3},{3,2},{4,5},{5,4},{6,7},{7,6},{8,9},{9,8},{10,11... | collective-permute-start | bytes 294920 | tf_op jit(solution)/shard_map/ppermute | solution.py:665
  408.4 28.8 %collective-permute-start.6 = (bf16[96,1664]{1,0:T(8,128)(2,1)S(1)}, bf16[96,1664]{1,0:T(8,128)(2,1)S(1)}, u32[]{:S(2)}, u32[]{:S(2)}) collective-permute-start(bf16[96,1664]{1,0:T(8,128)(2,1)S(1)} %get-tuple-element.216), channel_id=1, source_target_pairs={{0,2},{1,3},{2,0},{3,1},{4,6},{5,7},{6,4},{7,5},{8,10},{9,11},{10,... | collective-permute-start | bytes 958472 | tf_op jit(solution)/shard_map/ppermute | solution.py:665
  410.1 27.5 %collective-permute-start.7 = (bf16[96,1664]{1,0:T(8,128)(2,1)S(1)}, bf16[96,1664]{1,0:T(8,128)(2,1)S(1)}, u32[]{:S(2)}, u32[]{:S(2)}) collective-permute-start(bf16[96,1664]{1,0:T(8,128)(2,1)S(1)} %get-tuple-element.218), channel_id=1, source_target_pairs={{0,16},{1,17},{2,18},{3,19},{4,20},{5,21},{6,22},{7,23},{8,24},{9,... | collective-permute-start | bytes 958472 | tf_op jit(solution)/shard_map/ppermute | solution.py:665
  410.6 14.0 %collective-permute-start.19 = (bf16[96,1536]{1,0:T(8,128)(2,1)S(1)}, bf16[96,1536]{1,0:T(8,128)(2,1)S(1)}, u32[]{:S(2)}, u32[]{:S(2)}) collective-permute-start(bf16[96,1536]{1,0:T(8,128)(2,1)S(1)} %get-tuple-element.219), channel_id=1, source_target_pairs={{0,2},{1,3},{2,0},{3,1},{4,6},{5,7},{6,4},{7,5},{8,10},{9,11},{10,... | collective-permute-start | bytes 884744 | tf_op jit(solution)/shard_map/ppermute | solution.py:665
  412.3 14.5 %collective-permute-start.20 = (bf16[96,1536]{1,0:T(8,128)(2,1)S(1)}, bf16[96,1536]{1,0:T(8,128)(2,1)S(1)}, u32[]{:S(2)}, u32[]{:S(2)}) collective-permute-start(bf16[96,1536]{1,0:T(8,128)(2,1)S(1)} %get-tuple-element.221), channel_id=1, source_target_pairs={{0,16},{1,17},{2,18},{3,19},{4,20},{5,21},{6,22},{7,23},{8,24},{9,... | collective-permute-start | bytes 884744 | tf_op jit(solution)/shard_map/ppermute | solution.py:665
  413.1 19.9 %collective-permute-start.21 = (bf16[96,1536]{1,0:T(8,128)(2,1)S(1)}, bf16[96,1536]{1,0:T(8,128)(2,1)S(1)}, u32[]{:S(2)}, u32[]{:S(2)}) collective-permute-start(bf16[96,1536]{1,0:T(8,128)(2,1)S(1)} %get-tuple-element.220), channel_id=1, source_target_pairs={{0,18},{1,19},{2,16},{3,17},{4,22},{5,23},{6,20},{7,21},{8,26},{9,... | collective-permute-start | bytes 884744 | tf_op jit(solution)/shard_map/ppermute | solution.py:665
  424.6 14.3 %collective-permute-start.8 = (bf16[96,1664]{1,0:T(8,128)(2,1)S(1)}, bf16[96,1664]{1,0:T(8,128)(2,1)S(1)}, u32[]{:S(2)}, u32[]{:S(2)}) collective-permute-start(bf16[96,1664]{1,0:T(8,128)(2,1)S(1)} %get-tuple-element.217), channel_id=1, source_target_pairs={{0,18},{1,19},{2,16},{3,17},{4,22},{5,23},{6,20},{7,21},{8,26},{9,... | collective-permute-start | bytes 958472 | tf_op jit(solution)/shard_map/ppermute | solution.py:665
  433.2 10.1 %collective-permute-start.22 = (bf16[24,1536]{1,0:T(8,128)(2,1)S(1)}, bf16[24,1536]{1,0:T(8,128)(2,1)S(1)}, u32[]{:S(2)}, u32[]{:S(2)}) collective-permute-start(bf16[24,1536]{1,0:T(8,128)(2,1)S(1)} %get-tuple-element.225), channel_id=1, source_target_pairs={{0,4},{1,5},{2,6},{3,7},{4,0},{5,1},{6,2},{7,3},{8,12},{9,13},{10,... | collective-permute-start | bytes 221192 | tf_op jit(solution)/shard_map/ppermute | solution.py:665
  455.7 22.4 %collective-permute-start.28 = (bf16[96,1536]{1,0:T(8,128)(2,1)S(1)}, bf16[96,1536]{1,0:T(8,128)(2,1)}, u32[]{:S(2)}, u32[]{:S(2)}) collective-permute-start(bf16[96,1536]{1,0:T(8,128)(2,1)S(1)} %constant_dynamic-update-slice_fusion.4), channel_id=1, source_target_pairs={{0,2},{1,3},{2,0},{3,1},{4,6},{5,7},{6,4},{7,5},{8,10},{9,11},{10,... | collective-permute-start | bytes 884744 | tf_op jit(solution)/shard_map/ppermute | solution.py:665
  457.1 24.2 %collective-permute-start.29 = (bf16[96,1536]{1,0:T(8,128)(2,1)S(1)}, bf16[96,1536]{1,0:T(8,128)(2,1)}, u32[]{:S(2)}, u32[]{:S(2)}) collective-permute-start(bf16[96,1536]{1,0:T(8,128)(2,1)S(1)} %constant_dynamic-update-slice_fusion.4), channel_id=1, source_target_pairs={{0,16},{1,17},{2,18},{3,19},{4,20},{5,21},{6,22},{7,23},{8,24},{9,... | collective-permute-start | bytes 884744 | tf_op jit(solution)/shard_map/ppermute | solution.py:665
  457.8 24.4 %collective-permute-start.30 = (bf16[96,1536]{1,0:T(8,128)(2,1)S(1)}, bf16[96,1536]{1,0:T(8,128)(2,1)}, u32[]{:S(2)}, u32[]{:S(2)}) collective-permute-start(bf16[96,1536]{1,0:T(8,128)(2,1)S(1)} %constant_dynamic-update-slice_fusion.4), channel_id=1, source_target_pairs={{0,18},{1,19},{2,16},{3,17},{4,22},{5,23},{6,20},{7,21},{8,26},{9,... | collective-permute-start | bytes 884744 | tf_op jit(solution)/shard_map/ppermute | solution.py:665
  462.1 21.2 %collective-permute-start.15 = (bf16[96,1664]{1,0:T(8,128)(2,1)S(1)}, bf16[96,1664]{1,0:T(8,128)(2,1)S(1)}, u32[]{:S(2)}, u32[]{:S(2)}) collective-permute-start(bf16[96,1664]{1,0:T(8,128)(2,1)S(1)} %constant_dynamic-update-slice_fusion.12), channel_id=1, source_target_pairs={{0,2},{1,3},{2,0},{3,1},{4,6},{5,7},{6,4},{7,5},{8,10},{9,11},{10,... | collective-permute-start | bytes 958472 | tf_op jit(solution)/shard_map/ppermute | solution.py:665
  463.5 19.9 %collective-permute-start.16 = (bf16[96,1664]{1,0:T(8,128)(2,1)S(1)}, bf16[96,1664]{1,0:T(8,128)(2,1)S(1)}, u32[]{:S(2)}, u32[]{:S(2)}) collective-permute-start(bf16[96,1664]{1,0:T(8,128)(2,1)S(1)} %constant_dynamic-update-slice_fusion.12), channel_id=1, source_target_pairs={{0,16},{1,17},{2,18},{3,19},{4,20},{5,21},{6,22},{7,23},{8,24},{9,... | collective-permute-start | bytes 958472 | tf_op jit(solution)/shard_map/ppermute | solution.py:665
  (45 other events, 395.2 us)
